TPU v7x, 256 devices: a whole 4x4x8 slice. The times are simulated.
256 devices in a mesh: seq: 32 (over y, z), res: 8 (over x, core).
Axes of the slice: x: 4, y: 4, z: 8, core: 2. Of those that a mesh axis runs over, the one named last changes fastest.
Arguments:
- homolog_features: float32 [4096, 16384], P('seq', 'res')
- homolog_loss_slope: float32 [4096, 16384], P('seq', 'res'), may hold values from -6 to 6
- pair_update_gradient: float32 [256, 256, 128], P('res'), may hold values from -384 to 384
- alignment_mask: int32 [4096, 256], P('seq', 'res'), may hold values from 0 to 1, as said below
- asking_matrix: float32 [64, 64], replicated, may hold values from -0.75 to 0.75
- key_weight: float32 [64, 8], replicated
- content_matrix: float32 [64, 8], replicated, may hold values from -0.75 to 0.75
- sigmoid_filter_matrix: float32 [64, 64], replicated, may hold values from -0.75 to 0.75
- final_mixing_matrix: float32 [64, 64], replicated, may hold values from -0.75 to 0.75
- first_factor_matrix: float32 [64, 32], replicated, may hold values from -0.75 to 0.75
- second_factor_matrix: float32 [64, 32], replicated, may hold values from -0.75 to 0.75
- pair_weight: float32 [1024, 128], replicated, may hold values from -0.1875 to 0.1875
Outputs:
- input_grad_out: float32 [4096, 16384], P('seq', 'res')
Inputs may be any that keep to these rules, and one draw needn't show every extreme that they name: `alignment_mask`: 1 marks a sequence present at a residue; sequence 0 is present at every residue.
All inputs are finite; a program needn't handle non-finite values.
Results may differ from a plain program's by a relative error of at most 0.0003.
Values sent between devices are 32-bit elements; how exact they have to be, the bound alone decides.
No kernel may reach another device: no remote copies, remote signals or barrier semaphores. Data moves between devices by JAX's collectives and lax.ppermute only.
A program may use at most 128 MiB of HBM per device.

v0:
```python
import math

import jax
import jax.numpy as jnp
from jax import lax
from jax.sharding import PartitionSpec as P

FEATURE_DEPTH = 64
HEAD_COUNT = 8
HEAD_SIZE = 8
FACTOR_WIDTH = 32


EPSILON = 1e-05
MASK_FILL = -1000000000.0
PRECISE = lax.Precision.HIGHEST


def layer_normalize(values):
    center = values - jnp.mean(values, axis=-1, keepdims=True)
    inverse_norm = lax.rsqrt(jnp.mean(center * center, axis=-1, keepdims=True) + EPSILON)
    return (center * inverse_norm, inverse_norm)


def norm_back(normed_input, inverse_norm, incoming_loss_slope):
    return inverse_norm * (
        incoming_loss_slope
        - jnp.mean(incoming_loss_slope, axis=-1, keepdims=True)
        - normed_input * jnp.mean(incoming_loss_slope * normed_input, axis=-1, keepdims=True)
    )


def linear_project(values, weight):
    return jnp.einsum("...c,cd->...d", values, weight, precision=PRECISE)


def weigh(weights, vectors):
    return jnp.einsum("srh,srd->rhd", weights, vectors, precision=PRECISE)


def body(
    homolog_features,
    homolog_loss_slope,
    pair_update_gradient,
    alignment_mask,
    asking_matrix,
    key_weight,
    content_matrix,
    sigmoid_filter_matrix,
    final_mixing_matrix,
    first_factor_matrix,
    second_factor_matrix,
    pair_weight,
):
    homolog_entries, amino_positions = alignment_mask.shape
    homolog_offset = homolog_features.reshape(homolog_entries, amino_positions, FEATURE_DEPTH)
    incoming_loss_slope = homolog_loss_slope.reshape(
        homolog_entries, amino_positions, FEATURE_DEPTH
    )
    present_mask = alignment_mask.astype(jnp.float32)
    normed_input, inverse_norm = layer_normalize(homolog_offset)
    query_sum, col_count = lax.psum(
        (jnp.sum(present_mask[:, :, None] * normed_input, axis=0), jnp.sum(present_mask, axis=0)),
        "seq",
    )
    queries = (
        linear_project(query_sum / col_count[:, None], asking_matrix) * HEAD_SIZE ** (-0.5)
    ).reshape(amino_positions, HEAD_COUNT, HEAD_SIZE)
    key_vecs = linear_project(normed_input, key_weight)
    values = linear_project(normed_input, content_matrix)
    scores = jnp.einsum("rhd,srd->srh", queries, key_vecs, precision=PRECISE)
    scores = jnp.where(present_mask[:, :, None] > 0, scores, MASK_FILL)
    local_top = jnp.max(scores, axis=0)
    score_top = lax.pmax(local_top, "seq")
    raw_weights = jnp.exp(scores - score_top[None])
    totals, weighted = lax.psum((jnp.sum(raw_weights, axis=0), weigh(raw_weights, values)), "seq")
    attn_probs = raw_weights / totals[None]
    attended_heads = weighted / totals[..., None]
    attended_output = attended_heads.reshape(amino_positions, HEAD_COUNT * HEAD_SIZE)
    gate_activation = jax.nn.sigmoid(linear_project(normed_input, sigmoid_filter_matrix))
    middle_output = homolog_offset + linear_project(
        gate_activation * attended_output[None], final_mixing_matrix
    )
    normed_mid, inverse_mid = layer_normalize(middle_output)
    left_act = present_mask[:, :, None] * linear_project(normed_mid, first_factor_matrix)
    right_act = present_mask[:, :, None] * linear_project(normed_mid, second_factor_matrix)
    right_all, mask_all = (
        lax.all_gather(right_act, "res", axis=1, tiled=True),
        lax.all_gather(alignment_mask, "res", axis=1, tiled=True),
    )
    pair_count = lax.psum(
        jnp.dot(present_mask.T, mask_all.astype(jnp.float32), precision=PRECISE), "seq"
    )
    full_cols = right_all.shape[1]
    block_rows = math.gcd(amino_positions, 8)
    blocks = amino_positions // block_rows

    def opm_step(running, block_index):
        row_begin = block_index * block_rows
        grad_rows = lax.dynamic_slice_in_dim(pair_update_gradient, row_begin, block_rows, 0)
        count_rows = lax.dynamic_slice_in_dim(pair_count, row_begin, block_rows, 0)
        left_rows = lax.dynamic_slice_in_dim(left_act, row_begin, block_rows, 1)
        outer_grad = (
            jnp.einsum("ijk,mk->ijm", grad_rows, pair_weight, precision=PRECISE)
            / count_rows[:, :, None]
        )
        outer_grad = outer_grad.reshape(block_rows, full_cols, FACTOR_WIDTH, FACTOR_WIDTH)
        left_part = jnp.einsum("ijcf,sjf->sic", outer_grad, right_all, precision=PRECISE)
        running = running + jnp.einsum("ijcf,sic->sjf", outer_grad, left_rows, precision=PRECISE)
        return (running, left_part)

    right_terms, left_parts = lax.scan(
        opm_step,
        jnp.zeros((homolog_entries, full_cols, FACTOR_WIDTH), jnp.float32),
        jnp.arange(blocks, dtype=jnp.int32),
    )
    left_grad = jnp.transpose(left_parts, (1, 0, 2, 3)).reshape(
        homolog_entries, amino_positions, FACTOR_WIDTH
    )
    right_grad = lax.psum_scatter(right_terms, "res", scatter_dimension=1, tiled=True)
    mid_in = linear_project(
        present_mask[:, :, None] * left_grad, first_factor_matrix.T
    ) + linear_project(present_mask[:, :, None] * right_grad, second_factor_matrix.T)
    mid_grad = incoming_loss_slope + norm_back(normed_mid, inverse_mid, mid_in)
    out_grad = linear_project(mid_grad, final_mixing_matrix.T)
    gate_pre = out_grad * attended_output[None] * gate_activation * (1.0 - gate_activation)
    att_grad = lax.psum(jnp.sum(out_grad * gate_activation, axis=0), "seq").reshape(
        amino_positions, HEAD_COUNT, HEAD_SIZE
    )
    along = jnp.sum(att_grad * attended_heads, axis=-1)
    score_grad = attn_probs * (
        jnp.einsum("rhd,srd->srh", att_grad, values, precision=PRECISE) - along[None]
    )
    query_grad = lax.psum(
        jnp.einsum("srh,srd->rhd", score_grad, key_vecs, precision=PRECISE), "seq"
    )
    key_grad = jnp.einsum("srh,rhd->srd", score_grad, queries, precision=PRECISE)
    value_grad = jnp.einsum("srh,rhd->srd", attn_probs, att_grad, precision=PRECISE)
    mean_grad = linear_project(
        query_grad.reshape(amino_positions, HEAD_COUNT * HEAD_SIZE) * HEAD_SIZE ** (-0.5),
        asking_matrix.T,
    )
    x_grad = (
        linear_project(gate_pre, sigmoid_filter_matrix.T)
        + linear_project(key_grad, key_weight.T)
        + linear_project(value_grad, content_matrix.T)
    )
    x_grad = x_grad + present_mask[:, :, None] * mean_grad[None] / col_count[None, :, None]
    returned_tuple = mid_grad + norm_back(normed_input, inverse_norm, x_grad)
    return returned_tuple.reshape(homolog_entries, amino_positions * FEATURE_DEPTH)


def solution(mesh):
    in_specs = (
        P("seq", "res"),
        P("seq", "res"),
        P("res", None, None),
        P("seq", "res"),
        P(),
        P(),
        P(),
        P(),
        P(),
        P(),
        P(),
        P(),
    )
    out_specs = P("seq", "res")
    return jax.shard_map(body, mesh=mesh, in_specs=in_specs, out_specs=out_specs, check_vma=False)
```

profile of v0, /device:TPU:32, one launch (start us, length us, event | category | flops | bytes accessed | tf_op | source)
XLA Modules:
  0.0 1052.7 jit_solution(8251784860857441679)
XLA Ops:
  6.5 0.7 convert_element_type.6
  7.3 0.8 convert_reduce_fusion
  8.1 0.7 broadcast_compare_fusion
  8.8 14.4 %all_gather.6 = s32[128,256]{0,1:T(8,128)} all-gather(s32[128,32]{0,1:T(8,128)} %param.17), channel_id=1, replica_groups=mesh['seq'=32,'res'=8] {'res'}, dimensions={1}, use_global_device_ids=true | all-gather | bytes 147456 | tf_op jit(solution)/shard_map/all_gather | solution.py:89
  23.2 1.5 copy.70
  25.1 1.3 copy.73
  26.5 1.4 copy.72
  28.0 1.3 copy.74
  29.3 2.1 multiply_reduce_fusion.4
  31.5 140.5 %all-reduce.1 = (f32[32,64]{1,0:T(8,128)S(1)}, f32[32]{0:T(128)S(1)}) all-reduce(f32[32,64]{1,0:T(8,128)S(1)} %reduce_sum.122, f32[32]{0:T(128)S(1)} %convert_reduce_fusion), channel_id=1, replica_groups=mesh['seq'=32,'res'=8] {'seq'}, use_global_device_ids=true, to_apply=%region_3.0 | all-reduce | flops 2080 | bytes 16640 | tf_op jit(solution)/shard_map/psum | solution.py:62
  172.5 0.7 fusion.39
  173.8 140.0 %pmax.7 = f32[32,8]{1,0:T(8,128)S(1)} all-reduce(f32[32,8]{1,0:T(8,128)S(1)} %get-tuple-element.148), channel_id=1, replica_groups=mesh['seq'=32,'res'=8] {'seq'}, use_global_device_ids=true, to_apply=%region_7.8 | all-reduce | flops 256 | bytes 2048 | tf_op jit(solution)/shard_map/pmax | solution.py:74
  313.7 0.7 fusion.37
  315.4 139.8 %all-reduce = (f32[32,8,8]{2,1,0:T(8,128)S(1)}, f32[32,8]{1,0:T(8,128)S(1)}, f32[32,256]{1,0:T(8,128)}) all-reduce(f32[32,8,8]{2,1,0:T(8,128)S(1)} %fusion.61, f32[32,8]{1,0:T(8,128)S(1)} %fusion.60, f32[32,256]{1,0:T(8,128)S(1)} %fusion.57), channel_id=1, replica_groups=mesh['seq'=32,'res'=8] {'seq'}, use_global_device_ids=true, to_apply=%region_8.9 | all-reduce | flops 10496 | bytes 83968 | tf_op jit(solution)/shard_map/psum | solution.py:76
  455.4 1.3 fusion.26
  456.8 1.3 fusion.90
  458.3 1.6 convolution_multiply_fusion
  460.0 2.3 convolution_multiply_fusion.1
  462.3 29.8 %all-gather.2.cloned.1.call-done = f32[128,256,32]{0,2,1:T(8,128)} async-done(((f32[128,32,32]{0,2,1:T(8,128)}), f32[128,256,32]{0,2,1:T(8,128)}) %all-gather.2.cloned.1.call-update) | async-done | bytes 4194320 | tf_op jit(solution)/shard_map/all_gather | solution.py:88
  492.1 5.3 copy.80
  497.9 198.0 %while.13 = (s32[]{:T(128)}, f32[128,256,32]{1,0,2:T(8,128)}, f32[4,128,8,32]{1,3,2,0:T(8,128)}, s32[4]{0:T(128)}, f32[128,32,32]{0,2,1:T(8,128)}, /*index=5*/f3...) while((s32[]{:T(128)}, f32[128,256,32]{1,0,2:T(8,128)}, ...), condition=%wide.region_15.16_spmd.clone, body=%wide.region_14.15_spmd.clone.sunk | while | flops 9667870720 | bytes 98329368 | solution.py:112
  498.3 1.3 dynamic_slice.31
  500.3 0.7 constant_dynamic-slice_fusion.2
  501.0 10.0 broadcast_divide_fusion.3
  511.1 9.1 copy.110
  520.2 15.1 %bitcast_add_fusion.2 = f32[128,256,32]{1,0,2:T(8,128)} fusion(f32[128,256,32]{1,0,2:T(8,128)} %get-tuple-element.227, f32[8,256,32,32]{1,3,2,0:T(8,128)} %bitcast.138, pred[]{:T(512)S(6)} %compare.3, f32[128,32,32]{0,2,1:T(8,128)} %get-tuple-element.243, s32[]{:T(128)S(6)} %select_n.13), kind=kOutput, calls=%fused_computation.5.clone.1 | convolution fusion | flops 3223322624 | bytes 16908292 | tf_op jit(solution)/shard_map/while/body/eval_jaxpr/ijcf,sic->sjf/dot_general | solution.py:109
  535.3 11.5 %fusion.121 = f32[4,128,8,32]{1,3,2,0:T(8,128)} fusion(f32[4,128,8,32]{1,3,2,0:T(8,128)} %get-tuple-element.228, s32[]{:T(128)} %get-tuple-element.226, f32[128,256,32]{1,0,2:T(8,128)S(1)} %copy-done.1, f32[8,256,32,32]{1,3,2,0:T(8,128)S(1)} %bitcast.141), kind=kOutput, calls=%fused_computation.8.clone.1 | convolution fusion | flops 3221225472 | bytes 12714496 | tf_op jit(solution)/shard_map/while/body/eval_jaxpr/ijcf,sjf->sic/dot_general | solution.py:108
  546.8 1.3 dynamic_slice.31
  548.8 0.7 constant_dynamic-slice_fusion.2
  549.5 10.0 broadcast_divide_fusion.3
  559.6 9.1 copy.110
  568.7 16.2 %bitcast_add_fusion.2 = f32[128,256,32]{1,0,2:T(8,128)} fusion(f32[128,256,32]{1,0,2:T(8,128)} %get-tuple-element.227, f32[8,256,32,32]{1,3,2,0:T(8,128)} %bitcast.138, pred[]{:T(512)S(6)} %compare.3, f32[128,32,32]{0,2,1:T(8,128)} %get-tuple-element.243, s32[]{:T(128)S(6)} %select_n.13), kind=kOutput, calls=%fused_computation.5.clone.1 | convolution fusion | flops 3223322624 | bytes 16908292 | tf_op jit(solution)/shard_map/while/body/eval_jaxpr/ijcf,sic->sjf/dot_general | solution.py:109
  584.9 11.5 %fusion.121 = f32[4,128,8,32]{1,3,2,0:T(8,128)} fusion(f32[4,128,8,32]{1,3,2,0:T(8,128)} %get-tuple-element.228, s32[]{:T(128)} %get-tuple-element.226, f32[128,256,32]{1,0,2:T(8,128)S(1)} %copy-done.1, f32[8,256,32,32]{1,3,2,0:T(8,128)S(1)} %bitcast.141), kind=kOutput, calls=%fused_computation.8.clone.1 | convolution fusion | flops 3221225472 | bytes 12714496 | tf_op jit(solution)/shard_map/while/body/eval_jaxpr/ijcf,sjf->sic/dot_general | solution.py:108
  596.5 1.3 dynamic_slice.31
  599.2 10.0 broadcast_divide_fusion.3
  609.2 9.1 copy.110
  618.4 16.2 %bitcast_add_fusion.2 = f32[128,256,32]{1,0,2:T(8,128)} fusion(f32[128,256,32]{1,0,2:T(8,128)} %get-tuple-element.227, f32[8,256,32,32]{1,3,2,0:T(8,128)} %bitcast.138, pred[]{:T(512)S(6)} %compare.3, f32[128,32,32]{0,2,1:T(8,128)} %get-tuple-element.243, s32[]{:T(128)S(6)} %select_n.13), kind=kOutput, calls=%fused_computation.5.clone.1 | convolution fusion | flops 3223322624 | bytes 16908292 | tf_op jit(solution)/shard_map/while/body/eval_jaxpr/ijcf,sic->sjf/dot_general | solution.py:109
  634.6 11.5 %fusion.121 = f32[4,128,8,32]{1,3,2,0:T(8,128)} fusion(f32[4,128,8,32]{1,3,2,0:T(8,128)} %get-tuple-element.228, s32[]{:T(128)} %get-tuple-element.226, f32[128,256,32]{1,0,2:T(8,128)S(1)} %copy-done.1, f32[8,256,32,32]{1,3,2,0:T(8,128)S(1)} %bitcast.141), kind=kOutput, calls=%fused_computation.8.clone.1 | convolution fusion | flops 3221225472 | bytes 12714496 | tf_op jit(solution)/shard_map/while/body/eval_jaxpr/ijcf,sjf->sic/dot_general | solution.py:108
  646.1 1.3 dynamic_slice.31
  648.2 0.7 constant_dynamic-slice_fusion.2
  648.9 10.0 broadcast_divide_fusion.3
  658.9 9.1 copy.110
  668.0 16.2 %bitcast_add_fusion.2 = f32[128,256,32]{1,0,2:T(8,128)} fusion(f32[128,256,32]{1,0,2:T(8,128)} %get-tuple-element.227, f32[8,256,32,32]{1,3,2,0:T(8,128)} %bitcast.138, pred[]{:T(512)S(6)} %compare.3, f32[128,32,32]{0,2,1:T(8,128)} %get-tuple-element.243, s32[]{:T(128)S(6)} %select_n.13), kind=kOutput, calls=%fused_computation.5.clone.1 | convolution fusion | flops 3223322624 | bytes 16908292 | tf_op jit(solution)/shard_map/while/body/eval_jaxpr/ijcf,sic->sjf/dot_general | solution.py:109
  684.3 11.5 %fusion.121 = f32[4,128,8,32]{1,3,2,0:T(8,128)} fusion(f32[4,128,8,32]{1,3,2,0:T(8,128)} %get-tuple-element.228, s32[]{:T(128)} %get-tuple-element.226, f32[128,256,32]{1,0,2:T(8,128)S(1)} %copy-done.1, f32[8,256,32,32]{1,3,2,0:T(8,128)S(1)} %bitcast.141), kind=kOutput, calls=%fused_computation.8.clone.1 | convolution fusion | flops 3221225472 | bytes 12714496 | tf_op jit(solution)/shard_map/while/body/eval_jaxpr/ijcf,sjf->sic/dot_general | solution.py:108
  696.0 5.5 copy.81
  701.5 2.5 copy.69
  704.0 1.1 bitcast_multiply_fusion
  705.1 2.7 fusion.74
  707.8 34.2 %reduce-scatter.2.cloned.1.call-done = f32[128,32,32]{0,2,1:T(8,128)} async-done(((f32[128,256,32]{0,2,1:T(8,128)}), f32[128,32,32]{0,2,1:T(8,128)}) %reduce-scatter.2.cloned.1.call-update) | async-done | bytes 524304 | tf_op jit(solution)/shard_map/reduce_scatter | solution.py:120
  742.1 2.7 fusion.88
  745.3 1.0 copy-done.2
  746.3 1.3 multiply_reduce_fusion.1
  748.3 1.5 copy.83
  749.8 139.2 %psum.54 = f32[32,8,8]{2,1,0:T(8,128)} all-reduce(f32[32,8,8]{2,1,0:T(8,128)} %copy.83), channel_id=1, replica_groups=mesh['seq'=32,'res'=8] {'seq'}, use_global_device_ids=true, to_apply=%region_20.21 | all-reduce | flops 2048 | bytes 16384 | tf_op jit(solution)/shard_map/psum | solution.py:127
  889.0 2.1 convolution_bitcast_fusion
  891.1 1.2 multiply_reduce_fusion.6
  892.3 1.4 fusion.29
  893.7 1.0 convolution_bitcast_fusion.1
  895.1 3.0 fusion.30
  898.2 140.1 %psum.55 = f32[32,8,8]{0,2,1:T(8,128)S(1)} all-reduce(f32[32,8,8]{0,2,1:T(8,128)S(1)} %copy.86), channel_id=1, replica_groups=mesh['seq'=32,'res'=8] {'seq'}, use_global_device_ids=true, to_apply=%region_22.23 | all-reduce | flops 2048 | bytes 16384 | tf_op jit(solution)/shard_map/psum | solution.py:134
  1038.3 1.0 fusion.63
  1039.2 2.3 convolution_add_fusion.1
  1041.6 2.3 fusion.87
  1044.4 1.3 copy.87
  (102 shorter events, 6.5 us)
Async XLA Ops:
  6.5 450.2 %copy-start = (f32[64,64]{1,0:T(8,128)S(1)}, f32[64,64]{1,0:T(8,128)}, u32[]{:S(2)}) copy-start(f32[64,64]{1,0:T(8,128)} %param.22) | copy-start | bytes 49156
  6.5 485.6 %all-gather.2.cloned.1.call-start = ((), (), s32[]{:S(2)}) async-start(), calls=%async_computation.1 | async-start | bytes 4718592 | tf_op jit(solution)/shard_map/all_gather | solution.py:88
  25.1 4.2 copy-start.4
  27.9 144.1 %copy-start.15 = (f32[64,64]{1,0:T(8,128)S(1)}, f32[64,64]{1,0:T(8,128)}, u32[]{:S(2)}) copy-start(f32[64,64]{1,0:T(8,128)} %param.18) | copy-start | bytes 49156
  27.9 144.6 %copy-start.16 = (f32[64,8]{0,1:T(8,128)S(1)}, f32[64,8]{0,1:T(8,128)}, u32[]{:S(2)}) copy-start(f32[64,8]{0,1:T(8,128)} %param.19) | copy-start | bytes 6148
  28.0 285.8 %copy-start.18 = (f32[64,8]{0,1:T(8,128)S(1)}, f32[64,8]{0,1:T(8,128)}, u32[]{:S(2)}) copy-start(f32[64,8]{0,1:T(8,128)} %param.20) | copy-start | bytes 6148
  29.3 285.8 %copy-start.9 = (s32[128,256]{0,1:T(8,128)S(1)}, s32[128,256]{0,1:T(8,128)}, u32[]{:S(2)}) copy-start(s32[128,256]{0,1:T(8,128)} %all_gather.6) | copy-start | bytes 393220
  29.3 285.8 %copy-start.10 = (s32[128,32]{0,1:T(8,128)S(1)}, s32[128,32]{0,1:T(8,128)}, u32[]{:S(2)}) copy-start(s32[128,32]{0,1:T(8,128)} %param.17) | copy-start | bytes 49156
  29.3 426.1 %copy-start.14 = (f32[64,64]{1,0:T(8,128)S(1)}, f32[64,64]{1,0:T(8,128)}, u32[]{:S(2)}) copy-start(f32[64,64]{1,0:T(8,128)} %param.21) | copy-start | bytes 49156
  172.0 0.5 copy-start.19
  173.8 283.0 %copy-start.6 = (f32[128,32,8]{0,2,1:T(8,128)}, f32[128,32,8]{0,2,1:T(8,128)S(1)}, u32[]{:S(2)}) copy-start(f32[128,32,8]{0,2,1:T(8,128)S(1)} %get-tuple-element.149) | copy-start | bytes 393220
  314.5 142.3 %copy-start.7 = (f32[128,32,8]{0,2,1:T(8,128)}, f32[128,32,8]{0,2,1:T(8,128)S(1)}, u32[]{:S(2)}) copy-start(f32[128,32,8]{0,2,1:T(8,128)S(1)} %fusion.37) | copy-start | bytes 393220
  455.1 1.6 copy-start.8
  455.1 3.0 copy-start.12
  455.4 2.9 copy-start.11
  459.9 282.1 %reduce-scatter.2.cloned.1.call-start = ((), (), s32[]{:S(2)}) async-start(), calls=%async_computation.2 | async-start | bytes 4718592 | tf_op jit(solution)/shard_map/reduce_scatter | solution.py:120
  520.2 15.1 %slice-start = ((s8[8388608]{0:T(1024)(128)(4,1)}), s8[4194304]{0:T(1024)(128)(4,1)S(1)}, s32[]{:S(2)}) async-start(s8[8388608]{0:T(1024)(128)(4,1)} %bitcast.139), calls=%async_computation.3 | async-start | bytes 8388608 | tf_op jit(solution)/shard_map/while
  520.2 15.1 %slice-start.1 = ((s8[8388608]{0:T(1024)(128)(4,1)}), s8[4194304]{0:T(1024)(128)(4,1)S(1)}, s32[]{:S(2)}) async-start(s8[8388608]{0:T(1024)(128)(4,1)} %bitcast.139), calls=%async_computation.4 | async-start | bytes 8388608 | tf_op jit(solution)/shard_map/while
  520.2 15.1 %copy-start.1 = (f32[128,256,32]{1,0,2:T(8,128)S(1)}, f32[128,256,32]{1,0,2:T(8,128)}, u32[]{:S(2)}) copy-start(f32[128,256,32]{1,0,2:T(8,128)} %get-tuple-element.247) | copy-start | bytes 12582916 | tf_op jit(solution)/shard_map/while
  568.7 16.3 %slice-start = ((s8[8388608]{0:T(1024)(128)(4,1)}), s8[4194304]{0:T(1024)(128)(4,1)S(1)}, s32[]{:S(2)}) async-start(s8[8388608]{0:T(1024)(128)(4,1)} %bitcast.139), calls=%async_computation.3 | async-start | bytes 8388608 | tf_op jit(solution)/shard_map/while
  568.7 16.3 %slice-start.1 = ((s8[8388608]{0:T(1024)(128)(4,1)}), s8[4194304]{0:T(1024)(128)(4,1)S(1)}, s32[]{:S(2)}) async-start(s8[8388608]{0:T(1024)(128)(4,1)} %bitcast.139), calls=%async_computation.4 | async-start | bytes 8388608 | tf_op jit(solution)/shard_map/while
  568.7 16.3 %copy-start.1 = (f32[128,256,32]{1,0,2:T(8,128)S(1)}, f32[128,256,32]{1,0,2:T(8,128)}, u32[]{:S(2)}) copy-start(f32[128,256,32]{1,0,2:T(8,128)} %get-tuple-element.247) | copy-start | bytes 12582916 | tf_op jit(solution)/shard_map/while
  618.4 16.3 %slice-start = ((s8[8388608]{0:T(1024)(128)(4,1)}), s8[4194304]{0:T(1024)(128)(4,1)S(1)}, s32[]{:S(2)}) async-start(s8[8388608]{0:T(1024)(128)(4,1)} %bitcast.139), calls=%async_computation.3 | async-start | bytes 8388608 | tf_op jit(solution)/shard_map/while
  618.4 16.3 %slice-start.1 = ((s8[8388608]{0:T(1024)(128)(4,1)}), s8[4194304]{0:T(1024)(128)(4,1)S(1)}, s32[]{:S(2)}) async-start(s8[8388608]{0:T(1024)(128)(4,1)} %bitcast.139), calls=%async_computation.4 | async-start | bytes 8388608 | tf_op jit(solution)/shard_map/while
  618.4 16.3 %copy-start.1 = (f32[128,256,32]{1,0,2:T(8,128)S(1)}, f32[128,256,32]{1,0,2:T(8,128)}, u32[]{:S(2)}) copy-start(f32[128,256,32]{1,0,2:T(8,128)} %get-tuple-element.247) | copy-start | bytes 12582916 | tf_op jit(solution)/shard_map/while
  668.0 16.3 %slice-start = ((s8[8388608]{0:T(1024)(128)(4,1)}), s8[4194304]{0:T(1024)(128)(4,1)S(1)}, s32[]{:S(2)}) async-start(s8[8388608]{0:T(1024)(128)(4,1)} %bitcast.139), calls=%async_computation.3 | async-start | bytes 8388608 | tf_op jit(solution)/shard_map/while
  668.0 16.3 %slice-start.1 = ((s8[8388608]{0:T(1024)(128)(4,1)}), s8[4194304]{0:T(1024)(128)(4,1)S(1)}, s32[]{:S(2)}) async-start(s8[8388608]{0:T(1024)(128)(4,1)} %bitcast.139), calls=%async_computation.4 | async-start | bytes 8388608 | tf_op jit(solution)/shard_map/while
  668.0 16.3 %copy-start.1 = (f32[128,256,32]{1,0,2:T(8,128)S(1)}, f32[128,256,32]{1,0,2:T(8,128)}, u32[]{:S(2)}) copy-start(f32[128,256,32]{1,0,2:T(8,128)} %get-tuple-element.247) | copy-start | bytes 12582916 | tf_op jit(solution)/shard_map/while
  742.1 2.7 copy-start.5
  745.3 1.0 copy-start.2
  746.3 144.8 %copy-start.13 = (f32[32,8]{1,0:T(8,128)S(1)}, f32[32,8]{1,0:T(8,128)}, u32[]{:S(2)}) copy-start(f32[32,8]{1,0:T(8,128)} %copy-done.12) | copy-start | bytes 3076
  748.3 291.0 %copy-start.17 = (f32[64,8]{0,1:T(8,128)S(1)}, f32[64,8]{0,1:T(8,128)}, u32[]{:S(2)}) copy-start(f32[64,8]{0,1:T(8,128)} %param.19) | copy-start | bytes 6148
  898.1 145.8 %copy-start.3 = (f32[128,32,64]{0,2,1:T(8,128)S(1)}, f32[128,32,64]{0,2,1:T(8,128)}, u32[]{:S(2)}) copy-start(f32[128,32,64]{0,2,1:T(8,128)} %copy-done.2) | copy-start | bytes 3145732
Sparse Core Ops, SparseCore 0:
  460.1 32.0 all-gather.1
  701.6 40.3 reduce-scatter.1
where the time goes:
time: 1060 us; the launch traced here: 1050 us
  blocking collectives  714 us (67%)
  matrix products  180 us (17%)
  local copies, waits for them, and re-layouts  69.5 us (7%)
  waiting for transfers between devices  64.1 us (6%)
  between operations  14 us (1%)
    psum x1, blocking collectives, body(): lax.psum((jnp.sum(present_mask[:, :, None] * normed_input, axis=0), jnp.s...  141 us
    psum x1, blocking collectives, body(): lax.psum(jnp.einsum('srh,srd->rhd', score_grad, key_vecs, precision=PRECI...  140 us
    pmax x1, blocking collectives, body(): score_top = lax.pmax(local_top, 'seq')  140 us
    psum x1, blocking collectives, body(): lax.psum((jnp.sum(raw_weights, axis=0), weigh(raw_weights, values)), 'seq')  140 us
    psum x1, blocking collectives, body(): lax.psum(jnp.sum(out_grad * gate_activation, axis=0), 'seq')  139 us
    dot_general x4, matrix products, opm_step(): jnp.einsum('ijcf,sic->sjf', outer_grad, left_rows, precision=PRECISE)  63.8 us
    dot_general x4, matrix products, opm_step(): jnp.einsum('ijcf,sjf->sic', outer_grad, right_all, precision=PRECISE)  46.1 us
    dot_general x4, matrix products, opm_step(): jnp.einsum('ijk,mk->ijm', grad_rows, pair_weight, precision=PRECISE)  40.2 us
  transfers between devices with their start and end apart: 2, of which 2 were waited for; matrix products, arithmetic and copies ran while one was open for 1% of the time, Pallas kernels for 0%

commit v1 on v0

v1 whole, which is shorter than its diff:
```python
import jax
import jax.numpy as jnp
from jax import lax
from jax.experimental import pallas as pl
from jax.experimental.pallas import tpu as pltpu
from jax.sharding import Mesh
from jax.sharding import PartitionSpec as P

FEATURE_DEPTH = 64
HEAD_COUNT = 8
HEAD_SIZE = 8
FACTOR_WIDTH = 32
RES = 32
SEQ = 128

EPSILON = 1e-05
MASK_FILL = -1000000000.0
PRECISE = lax.Precision.HIGHEST
F32 = jnp.float32


def split(values):
    high = values.astype(jnp.bfloat16)
    low = (values - high.astype(jnp.float32)).astype(jnp.bfloat16)
    return high, low


def dot_nn(a, b):
    return lax.dot_general(a, b, (((1,), (0,)), ((), ())), preferred_element_type=jnp.float32)


def dot_nt(a, b):
    return lax.dot_general(a, b, (((1,), (1,)), ((), ())), preferred_element_type=jnp.float32)


def exact_nn(a, b):
    return lax.dot_general(a, b, (((1,), (0,)), ((), ())), preferred_element_type=F32, precision=PRECISE)


def exact_nt(a, b):
    return lax.dot_general(a, b, (((1,), (1,)), ((), ())), preferred_element_type=F32, precision=PRECISE)


def lhs_parts(weight):
    high, low = split(weight)
    return jnp.concatenate([high, high, low], axis=1)


def project(parts, values):
    high, low = split(values)
    return dot_nn(parts, jnp.concatenate([high, low, high], axis=0))


def row_lane(shape):
    return lax.broadcasted_iota(jnp.int32, shape, 0), lax.broadcasted_iota(jnp.int32, shape, 1)


def sum_lanes_01(ones, values):
    high, rest = values.astype(jnp.bfloat16), values
    rest = rest - high.astype(F32)
    mid = rest.astype(jnp.bfloat16)
    low = (rest - mid.astype(F32)).astype(jnp.bfloat16)
    return dot_nt(ones, high) + dot_nt(ones, mid) + dot_nt(ones, low)


def own_blocks(values):
    rows, _ = row_lane((RES, 128))
    total = jnp.zeros((RES, 128), F32)
    for pair in range(RES // 2):
        total = jnp.where(rows // 2 == pair, values[:, 128 * pair : 128 * pair + 128], total)
    return jnp.where(rows[:, :64] % 2 == 0, total[:, :64], total[:, 64:])


def pack(values):
    return jnp.concatenate([values[:16], values[16:]], axis=1)


def unpack(values):
    return jnp.concatenate([values[:, :64], values[:, 64:]], axis=0)


def over_heads(values):
    return jnp.broadcast_to(values[:, None, :], (RES, 8, values.shape[1])).reshape(RES * 8, values.shape[1])


def head_column(values):
    rows, lanes = row_lane((RES * 8, values.shape[1]))
    return jnp.sum(jnp.where(rows % 8 == lanes, over_heads(values), 0.0), axis=1, keepdims=True)


def head_blocks(values):
    rows, lanes = row_lane((RES * 8, 64))
    picked = jnp.where(rows % 8 == lanes // 8, over_heads(values), 0.0)
    r, c = row_lane((64, RES * 8))
    spread = exact_nn(picked, (r % 8 == c % 8).astype(F32))
    rows, lanes = row_lane((RES * 8, RES * 8))
    return jnp.where(rows // 8 == lanes // 8, spread, 0.0)


def fold_blocks(values):
    rows, lanes = row_lane((RES * 8, RES * 8))
    r, c = row_lane((RES * 8, 128))
    fold = jnp.where((r % 8 == c % 8) & (c < 64), 1.0, 0.0)
    return exact_nn(jnp.where(rows // 8 == lanes // 8, values, 0.0), fold)


def sum_heads(values):
    return jnp.sum(values.reshape(RES, 8, values.shape[1]), axis=1)


def send_all(send, rows, values):
    send[:, rows, :] = jnp.broadcast_to(values[None], (send.shape[0],) + values.shape)


def norm_kernel(m0, mask, m0t, x0t, inverse, present, send):
    shown = mask[...].astype(F32).T
    present[...] = shown
    for pair in range(RES // 2):
        block = m0[:, 128 * pair : 128 * pair + 128].T
        m0t[128 * pair : 128 * pair + 128] = block
        for k in range(2):
            part = block[64 * k : 64 * k + 64]
            center = part - jnp.mean(part, axis=0, keepdims=True)
            scale = lax.rsqrt(jnp.mean(center * center, axis=0, keepdims=True) + EPSILON)
            row = 2 * pair + k
            inverse[row : row + 1] = scale
            x0t[64 * row : 64 * row + 64] = center * scale
    ones = shown.astype(jnp.bfloat16)
    sums = own_blocks(sum_lanes_01(ones, x0t[...]))
    counts = dot_nt(jnp.ones((16, SEQ), jnp.bfloat16), ones)
    send[...] = jnp.zeros_like(send)
    send_all(send, slice(0, 16), pack(sums))
    send_all(send, slice(16, 17), jnp.concatenate([counts[0:1], jnp.zeros((1, 96), F32)], axis=1))


def pair_kernel(sent, mask, mask_core, mask_1, mask_2, mask_3, send):
    send[...] = sent[...]
    own = mask[...].astype(F32).T.astype(jnp.bfloat16)
    rows = jnp.concatenate([own, mask_core[...].astype(F32).T.astype(jnp.bfloat16)], axis=0)
    columns = jnp.concatenate(
        [own] + [part[...].astype(F32).T.astype(jnp.bfloat16) for part in (mask_1, mask_2, mask_3)], axis=0
    )
    count = dot_nt(rows, columns)
    share = 64 // send.shape[0]
    for peer in range(send.shape[0]):
        send[peer, 17 : 17 + share, :] = count[share * peer : share * peer + share]


def project_kernel(x0t, slope, key, value_gate, keys, values, gate, slope_t):
    parts = lhs_parts(value_gate[...])
    for pair in range(RES // 2):
        slope_t[128 * pair : 128 * pair + 128] = slope[:, 128 * pair : 128 * pair + 128].T
        row = 128 * pair
        both = jnp.concatenate([x0t[row : row + 64], x0t[row + 64 : row + 128]], axis=1)
        found = project(parts, both)
        key_rows = exact_nn(key[...], both)
        gates = jax.nn.sigmoid(found[8:72])
        for k in range(2):
            lanes = slice(SEQ * k, SEQ * k + SEQ)
            head = 8 * (2 * pair + k)
            keys[head : head + 8] = key_rows[:, lanes]
            values[head : head + 8] = found[0:8, lanes]
            gate[row + 64 * k : row + 64 * k + 64] = gates[:, lanes]


def score_kernel(got, keys, values, present, asking, weights, local, counts, query_blocks, send):
    sums = jnp.sum(got[...], axis=0)
    r, c = row_lane((RES, RES))
    count = jnp.sum(jnp.where(r == c, jnp.broadcast_to(sums[16:17, :RES], (RES, RES)), 0.0), axis=1, keepdims=True)
    counts[...] = jnp.broadcast_to(count, (RES, 128))
    queries = exact_nn(unpack(sums[:16]) / count, asking[...]) * HEAD_SIZE ** (-0.5)
    blocks = head_blocks(queries)
    query_blocks[...] = blocks
    scores = exact_nn(blocks, keys[...])
    scores = jnp.where(over_heads(present[...]) > 0, scores, MASK_FILL)
    top = jnp.max(scores, axis=1, keepdims=True)
    raw = jnp.exp(scores - top)
    weights[...] = raw
    total = jnp.sum(raw, axis=1, keepdims=True)
    folded = fold_blocks(exact_nt(raw, values[...]))
    rows, lanes = row_lane((RES * 8, 128))
    head = rows % 8
    packed = jnp.where(lanes < 64, jnp.where(lanes // 8 == head, folded, 0.0), 0.0)
    packed = jnp.where(lanes == 64 + head, top, packed)
    packed = jnp.where(lanes == 72 + head, total, packed)
    packed = sum_heads(packed)
    local[...] = packed
    send_all(send, slice(0, 32), packed)
    share = 64 // send.shape[0]
    send[:, 32:, :] = jnp.zeros((send.shape[0], send.shape[1] - 32, 128), F32)
    send_all(send, slice(32, 32 + share), sums[17 : 17 + share])


def attend_kernel(
    got, local, raw, m0t, gate, present, mixing, factors,
    probs, attended, mixed, x1t, inverse_mid, left, right, inverse_count, scratch,
):
    peers = got.shape[0]
    share = 64 // peers
    for peer in range(peers):
        inverse_count[share * peer : share * peer + share] = 1.0 / got[peer, 32 : 32 + share, :]
    parts = got[:, 0:32, :]
    top = jnp.max(parts, axis=0)
    lane = lax.broadcasted_iota(jnp.int32, (peers, RES, 128), 2)
    factor = jnp.where((lane >= 64) & (lane < 72), jnp.exp(parts - top[None]), 0.0)
    r, c = row_lane((128, 128))
    expand = ((c < 64) & (r == 64 + c // 8)) | ((c >= 72) & (c < 80) & (r == c - 8))
    expand = jnp.where(expand, 1.0, 0.0).astype(jnp.bfloat16)
    high, low = split(factor.reshape(peers * RES, 128))
    factor = (dot_nn(high, expand) + dot_nn(low, expand)).reshape(peers, RES, 128)
    total = jnp.sum(factor * parts, axis=0)
    share = jnp.exp(local[:, 64:72] - top[:, 64:72]) / total[:, 72:80]
    probs[...] = raw[...] * head_column(share)
    spread = jnp.where((c < 64) & (r == 72 + c // 8), 1.0, 0.0)
    heads = total[:, :64] / exact_nn(total, spread)[:, :64]
    attended[...] = heads
    heads_t = heads.T
    mixing_parts = lhs_parts(mixing[...])
    factor_parts = lhs_parts(factors[...])
    for pair in range(RES // 2):
        shown, used, base = [], [], []
        for k in range(2):
            i = 2 * pair + k
            rows = slice(64 * i, 64 * i + 64)
            use = gate[rows] * heads_t[:, i : i + 1]
            mixed[rows] = use
            used.append(use)
            base.append(m0t[rows])
            shown.append(present[i : i + 1])
        middle = jnp.concatenate(base, axis=1) + project(mixing_parts, jnp.concatenate(used, axis=1))
        center = middle - jnp.mean(middle, axis=0, keepdims=True)
        scale = lax.rsqrt(jnp.mean(center * center, axis=0, keepdims=True) + EPSILON)
        normed = center * scale
        found = project(factor_parts, normed) * jnp.concatenate(shown, axis=1)
        for k in range(2):
            i = 2 * pair + k
            lanes = slice(SEQ * k, SEQ * k + SEQ)
            x1t[64 * i : 64 * i + 64] = normed[:, lanes]
            inverse_mid[i : i + 1] = scale[:, lanes]
            left[32 * i : 32 * i + 32] = found[:32, lanes]
            scratch[32 * i : 32 * i + 32] = found[32:, lanes]
    for f in range(FACTOR_WIDTH):
        right[f] = scratch[pl.ds(f, RES, stride=FACTOR_WIDTH), :]


def middle_kernel(
    left_own, left_far, right_own, right_1, right_2, right_3, x1t, inverse_mid, present, slope_t, gate,
    factors_back, mixing_back, mid, out_grad, send, scratch,
):
    for f in range(FACTOR_WIDTH):
        scratch[32 * f : 32 * f + 32] = (right_own[f] + right_1[f]) + (right_2[f] + right_3[f])
    parts = lhs_parts(factors_back[...])
    mixing_parts = lhs_parts(mixing_back[...])
    ones = jnp.ones((16, SEQ), jnp.bfloat16)
    sums = []
    for pair in range(RES // 2):
        grads = []
        for k in range(2):
            i = 2 * pair + k
            rows = slice(32 * i, 32 * i + 32)
            both = jnp.concatenate(
                [left_own[rows] + left_far[rows], scratch[pl.ds(i, FACTOR_WIDTH, stride=RES), :]], axis=0
            )
            grads.append(both * present[i : i + 1])
        mid_in = project(parts, jnp.concatenate(grads, axis=1))
        rows = slice(128 * pair, 128 * pair + 128)
        normed = jnp.concatenate([x1t[128 * pair : 128 * pair + 64], x1t[128 * pair + 64 : 128 * pair + 128]], axis=1)
        scale = jnp.concatenate([inverse_mid[2 * pair : 2 * pair + 1], inverse_mid[2 * pair + 1 : 2 * pair + 2]], axis=1)
        back = scale * (
            mid_in
            - jnp.mean(mid_in, axis=0, keepdims=True)
            - normed * jnp.mean(mid_in * normed, axis=0, keepdims=True)
        )
        back = back + jnp.concatenate(
            [slope_t[128 * pair : 128 * pair + 64], slope_t[128 * pair + 64 : 128 * pair + 128]], axis=1
        )
        grad = project(mixing_parts, back)
        gated = []
        for k in range(2):
            lanes = slice(SEQ * k, SEQ * k + SEQ)
            rows = slice(128 * pair + 64 * k, 128 * pair + 64 * k + 64)
            mid[rows] = back[:, lanes]
            out_grad[rows] = grad[:, lanes]
            gated.append(grad[:, lanes] * gate[rows])
        sums.append(sum_lanes_01(ones, jnp.concatenate(gated, axis=0)))
    sums = [jnp.concatenate([part, part], axis=0) for part in sums]
    send_all(send, slice(0, 16), pack(own_blocks(jnp.concatenate(sums, axis=1))))


def gate_back_kernel(out_grad, mixed, gate, filter_weight, x_grad):
    parts = lhs_parts(filter_weight[...])
    for pair in range(RES // 2):
        both = []
        for k in range(2):
            rows = slice(128 * pair + 64 * k, 128 * pair + 64 * k + 64)
            both.append(out_grad[rows] * mixed[rows] * (1.0 - gate[rows]))
        found = project(parts, jnp.concatenate(both, axis=1))
        for k in range(2):
            x_grad[128 * pair + 64 * k : 128 * pair + 64 * k + 64] = found[:, SEQ * k : SEQ * k + SEQ]


def score_back_kernel(got, attended, probs, keys, values, score_grad, grad_blocks, send):
    att_grad = unpack(jnp.sum(got[...], axis=0))
    blocks = head_blocks(att_grad)
    grad_blocks[...] = blocks
    rows, lanes = row_lane((RES * 8, 64))
    along = jnp.sum(
        jnp.where(rows % 8 == lanes // 8, over_heads(att_grad * attended[...]), 0.0), axis=1, keepdims=True
    )
    grad = probs[...] * (exact_nn(blocks, values[...]) - along)
    score_grad[...] = grad
    folded = fold_blocks(exact_nt(grad, keys[...]))[:, :64]
    send_all(send, slice(0, 16), pack(sum_heads(jnp.where(rows % 8 == lanes // 8, folded, 0.0))))


def key_back_kernel(score_grad, grad_blocks, query_blocks, probs, partial, key_value, x_grad):
    key_grad = exact_nn(query_blocks[...].T, score_grad[...])
    value_grad = exact_nn(grad_blocks[...].T, probs[...])
    parts = lhs_parts(key_value[...])
    for pair in range(RES // 2):
        both = []
        for k in range(2):
            rows = slice(16 * pair + 8 * k, 16 * pair + 8 * k + 8)
            both.append(jnp.concatenate([key_grad[rows], value_grad[rows]], axis=0))
        found = project(parts, jnp.concatenate(both, axis=1))
        for k in range(2):
            rows = slice(128 * pair + 64 * k, 128 * pair + 64 * k + 64)
            x_grad[rows] = partial[rows] + found[:, SEQ * k : SEQ * k + SEQ]


def final_kernel(got, counts, asking, present, x0t, inverse, x_grad, mid, out):
    query_grad = unpack(jnp.sum(got[...], axis=0)) * HEAD_SIZE ** (-0.5)
    mean_grad = (exact_nt(query_grad, asking[...]) / counts[:, :64]).T
    for pair in range(RES // 2):
        done = []
        for k in range(2):
            i = 2 * pair + k
            rows = slice(64 * i, 64 * i + 64)
            grad = x_grad[rows] + mean_grad[:, i : i + 1] * present[i : i + 1]
            normed = x0t[rows]
            back = inverse[i : i + 1] * (
                grad - jnp.mean(grad, axis=0, keepdims=True) - normed * jnp.mean(grad * normed, axis=0, keepdims=True)
            )
            done.append(mid[rows] + back)
        out[:, 128 * pair : 128 * pair + 128] = jnp.concatenate(done, axis=0).T


def call(kernel, shapes, *operands, scratch=(), flops=100_000_000, vmem=24):
    shapes = [jax.ShapeDtypeStruct(shape, F32) for shape in shapes]
    size = sum(4 * array.size for array in shapes) + sum(array.size * array.dtype.itemsize for array in operands)
    return pl.pallas_call(
        kernel,
        out_shape=shapes,
        scratch_shapes=list(scratch),
        compiler_params=pltpu.CompilerParams(vmem_limit_bytes=vmem * 2**20),
        cost_estimate=pl.CostEstimate(flops=flops, bytes_accessed=int(size), transcendentals=0),
        name=kernel.__name__,
    )(*operands)


ROWS = 8


def right_kernel(place, own_g, far_g, inverse_count, weight, left, high, low, out, weights, total):
    step = pl.program_id(0)
    x = place[0]

    @pl.when(step == 0)
    def _():
        w_high, w_low = split(weight[...])
        weights[:, 0:128] = w_high
        weights[:, 128:256] = w_low
        weights[:, 256:384] = w_high
        total[...] = jnp.zeros_like(total)

    near = step < pl.num_programs(0) // 2
    for pair in range(ROWS // 2):
        blocks = []
        for row in (2 * pair, 2 * pair + 1):
            for d in range(4):
                chip = lax.rem(x + d, 4)
                blocks.append(jnp.where(near, own_g[row, chip, 0], far_g[row, chip]))
        g_high, g_low = split(jnp.concatenate(blocks, axis=0))
        grads = dot_nt(weights[...], jnp.concatenate([g_high, g_high, g_low], axis=1))
        grads = grads * jnp.concatenate(
            [inverse_count[2 * pair : 2 * pair + 1], inverse_count[2 * pair + 1 : 2 * pair + 2]], axis=1
        )
        grads_high, grads_low = split(grads)
        for k in range(2):
            row = (2 * pair + k) * FACTOR_WIDTH
            rows, lanes = slice(row, row + FACTOR_WIDTH), slice(128 * k, 128 * k + 128)
            high[:, rows, :] = grads_high[:, lanes].reshape(FACTOR_WIDTH, FACTOR_WIDTH, 128)
            low[:, rows, :] = grads_low[:, lanes].reshape(FACTOR_WIDTH, FACTOR_WIDTH, 128)
    l_high, l_low = split(left[...].T)
    stacked = jnp.concatenate([l_high, l_low], axis=0)
    for f in range(0, FACTOR_WIDTH, 2):
        first = dot_nn(stacked, jnp.concatenate([high[f], high[f + 1]], axis=1))
        second = dot_nn(l_high, jnp.concatenate([low[f], low[f + 1]], axis=1))
        total[:, 128 * f : 128 * f + 256] += first[:128] + first[128:] + second

    @pl.when(step == pl.num_programs(0) - 1)
    def _():
        for f in range(FACTOR_WIDTH):
            block = total[:, 128 * f : 128 * f + 128].T
            for d in range(4):
                out[d, f] = block[32 * d : 32 * d + 32]


def right_products(place, pair_grad, far_grad, inverse_count, weight, left):
    block = ROWS * FACTOR_WIDTH
    steps = 64 // ROWS
    half = steps // 2
    grid_spec = pltpu.PrefetchScalarGridSpec(
        num_scalar_prefetch=1,
        grid=(steps,),
        in_specs=[
            pl.BlockSpec((ROWS, 4, 1, 32, 128), lambda t, s: (jnp.minimum(t, half - 1), 0, s[1], 0, 0)),
            pl.BlockSpec((ROWS, 4, 32, 128), lambda t, s: (jnp.maximum(t - half, 0), 0, 0, 0)),
            pl.BlockSpec((ROWS, 128), lambda t, s: (t, 0)),
            pl.BlockSpec((1024, 128), lambda t, s: (0, 0)),
            pl.BlockSpec((block, 128), lambda t, s: (t, 0)),
        ],
        out_specs=[
            pl.BlockSpec((FACTOR_WIDTH, block, 128), lambda t, s: (0, t, 0)),
            pl.BlockSpec((FACTOR_WIDTH, block, 128), lambda t, s: (0, t, 0)),
            pl.BlockSpec((4, FACTOR_WIDTH, 32, 128), lambda t, s: (0, 0, 0, 0)),
        ],
        scratch_shapes=[
            pltpu.VMEM((1024, 384), jnp.bfloat16),
            pltpu.VMEM((128, 4096), jnp.float32),
        ],
    )
    return pl.pallas_call(
        right_kernel,
        grid_spec=grid_spec,
        out_shape=[
            jax.ShapeDtypeStruct((FACTOR_WIDTH, 64 * FACTOR_WIDTH, 128), jnp.bfloat16),
            jax.ShapeDtypeStruct((FACTOR_WIDTH, 64 * FACTOR_WIDTH, 128), jnp.bfloat16),
            jax.ShapeDtypeStruct((4, FACTOR_WIDTH, 32, 128), jnp.float32),
        ],
        compiler_params=pltpu.CompilerParams(vmem_limit_bytes=48 * 2**20),
        cost_estimate=pl.CostEstimate(flops=16_000_000_000, bytes_accessed=42_000_000, transcendentals=0),
        name="right_products",
    )(place, pair_grad, far_grad, inverse_count, weight, left)


def left_kernel(high, low, right_0, right_1, right_2, right_3, out, weights):
    @pl.when(pl.program_id(0) == 0)
    def _():
        for f in range(FACTOR_WIDTH):
            for d, right in enumerate((right_0, right_1, right_2, right_3)):
                r_high, r_low = split(right[f])
                row = (f % 2) * 128 + d * 32
                weights[f // 2, row : row + 32, 0:128] = r_high
                weights[f // 2, row : row + 32, 128:256] = r_low

    first = jnp.zeros((ROWS * FACTOR_WIDTH, 256), jnp.float32)
    second = jnp.zeros((ROWS * FACTOR_WIDTH, 128), jnp.float32)
    for f in range(0, FACTOR_WIDTH, 2):
        first += dot_nn(jnp.concatenate([high[f], high[f + 1]], axis=1), weights[f // 2])
        second += dot_nn(jnp.concatenate([low[f], low[f + 1]], axis=1), weights[f // 2, :, 0:128])
    out[...] = first[:, :128] + first[:, 128:] + second


def left_products(high, low, rights):
    block = ROWS * FACTOR_WIDTH
    whole = pl.BlockSpec((FACTOR_WIDTH, 32, 128), lambda t: (0, 0, 0))
    return pl.pallas_call(
        left_kernel,
        grid=(64 // ROWS,),
        in_specs=[
            pl.BlockSpec((FACTOR_WIDTH, block, 128), lambda t: (0, t, 0)),
            pl.BlockSpec((FACTOR_WIDTH, block, 128), lambda t: (0, t, 0)),
            whole,
            whole,
            whole,
            whole,
        ],
        out_specs=pl.BlockSpec((block, 128), lambda t: (t, 0)),
        out_shape=jax.ShapeDtypeStruct((64 * FACTOR_WIDTH, 128), jnp.float32),
        scratch_shapes=[pltpu.VMEM((FACTOR_WIDTH // 2, 256, 256), jnp.bfloat16)],
        compiler_params=pltpu.CompilerParams(vmem_limit_bytes=40 * 2**20),
        cost_estimate=pl.CostEstimate(flops=9_000_000_000, bytes_accessed=37_000_000, transcendentals=0),
        name="left_products",
    )(high, low, *rights)


def swap_core(values):
    return lax.ppermute(values, "core", [(0, 1), (1, 0)])


def fetch_chip(values, distance):
    return lax.ppermute(values, "x", [((i + distance) % 4, i) for i in range(4)])


def send_chip(values, distance):
    return lax.ppermute(values, "x", [(i, (i + distance) % 4) for i in range(4)])


def exchange(send):
    return lax.all_to_all(send, "seq", 0, 0, tiled=True)


def body(
    homolog_features,
    homolog_loss_slope,
    pair_update_gradient,
    alignment_mask,
    asking_matrix,
    key_weight,
    content_matrix,
    sigmoid_filter_matrix,
    final_mixing_matrix,
    first_factor_matrix,
    second_factor_matrix,
    pair_weight,
):
    peers = lax.axis_size("seq")
    share = 64 // peers
    counted, shared = -(-(17 + share) // 8) * 8, -(-(32 + share) // 8) * 8
    x, core = lax.axis_index("x"), lax.axis_index("core")
    place = jnp.stack([x, core]).astype(jnp.int32)
    mask_core = swap_core(alignment_mask)
    mask_chips = [fetch_chip(alignment_mask, d) for d in (1, 2, 3)]
    pair_grad = pair_update_gradient.reshape(32, 4, 2, 32, 128)
    far_grad = swap_core(lax.dynamic_index_in_dim(pair_grad, 1 - core, 2, keepdims=False))
    weight = pair_weight.reshape(FACTOR_WIDTH, FACTOR_WIDTH, 128).swapaxes(0, 1).reshape(1024, 128)
    value_gate = jnp.concatenate([content_matrix, sigmoid_filter_matrix], axis=1).T
    key_value = jnp.concatenate([key_weight, content_matrix], axis=1)
    factors = jnp.concatenate([first_factor_matrix, second_factor_matrix], axis=1)

    flat, heads, stat = (RES * 64, SEQ), (RES * 8, SEQ), (RES, SEQ)
    m0t, x0t, inverse, present, send = call(
        norm_kernel, [flat, flat, stat, stat, (peers, counted, 128)], homolog_features, alignment_mask
    )
    (send,) = call(pair_kernel, [(peers, counted, 128)], send, alignment_mask, mask_core, *mask_chips)
    got = exchange(send)
    keys, values, gate, slope_t = call(
        project_kernel, [heads, heads, flat, flat], x0t, homolog_loss_slope, key_weight.T, value_gate
    )
    raw, local, counts, query_blocks, send = call(
        score_kernel, [heads, stat, stat, (RES * 8, RES * 8), (peers, shared, 128)], got, keys, values, present, asking_matrix
    )
    got = exchange(send)
    probs, attended, mixed, x1t, inverse_mid, left, right, inverse_count = call(
        attend_kernel,
        [heads, (RES, 64), flat, flat, stat, (RES * 32, SEQ), (FACTOR_WIDTH, RES, SEQ), (64, 128)],
        got, local, raw, m0t, gate, present, final_mixing_matrix.T, factors.T,
        scratch=[pltpu.VMEM((RES * 32, SEQ), F32)],
    )
    left_rows = jnp.concatenate([left, swap_core(left)], axis=0)
    rights = [right] + [fetch_chip(right, d) for d in (1, 2, 3)]
    high, low, right_parts = right_products(place, pair_grad, far_grad, inverse_count, weight, left_rows)
    right_sent = [send_chip(right_parts[d], d) for d in (1, 2, 3)]
    left_parts = left_products(high, low, rights)
    half = RES * FACTOR_WIDTH
    mid, out_grad, send = call(
        middle_kernel, [flat, flat, (peers, 16, 128)],
        left_parts[:half], swap_core(left_parts[half:]), right_parts[0], *right_sent,
        x1t, inverse_mid, present, slope_t, gate, factors, final_mixing_matrix,
        scratch=[pltpu.VMEM((RES * 32, SEQ), F32)],
    )
    got = exchange(send)
    (gate_grad,) = call(gate_back_kernel, [flat], out_grad, mixed, gate, sigmoid_filter_matrix)
    score_grad, grad_blocks, send = call(
        score_back_kernel, [heads, (RES * 8, RES * 8), (peers, 16, 128)], got, attended, probs, keys, values
    )
    got = exchange(send)
    (x_grad,) = call(key_back_kernel, [flat], score_grad, grad_blocks, query_blocks, probs, gate_grad, key_value)
    (out,) = call(final_kernel, [(SEQ, RES * 64)], got, counts, asking_matrix, present, x0t, inverse, x_grad, mid)
    return out


def solution(mesh):
    grid = Mesh(mesh.devices.reshape(mesh.devices.shape[0], 4, 2), ("seq", "x", "core"))
    res = ("x", "core")
    in_specs = (
        P("seq", res),
        P("seq", res),
        P(res, None, None),
        P("seq", res),
        P(),
        P(),
        P(),
        P(),
        P(),
        P(),
        P(),
        P(),
    )
    return jax.shard_map(body, mesh=grid, in_specs=in_specs, out_specs=P("seq", res), check_vma=False)
```

time: 1060 us -> 198 us (0.19)
  blocking collectives: 714 us -> 16.6 us
  matrix products: 180 us -> 0 us
  Pallas kernels: 0 us -> 57.2 us
  local copies, waits for them, and re-layouts: 69.5 us -> 33.4 us
  starting transfers between devices: 0.04 us -> 32.6 us
  between operations: 14 us -> 0.33 us
  waiting for transfers between devices: 64.1 us -> 52.9 us
    psum x4 -> x0, blocking collectives: 560 us -> none  [the longest x1 141 us: body(): lax.psum((jnp.sum(present_mask[:, :, None] * normed_input, axis=0), jnp.s...]
    dot_general x33 -> x0, matrix products: 180 us -> none  [the longest x4 63.8 us: opm_step(): jnp.einsum('ijcf,sic->sjf', outer_grad, left_rows, precision=PRECISE)]
    pmax x1 -> x0, blocking collectives: 140 us -> none  [body(): score_top = lax.pmax(local_top, 'seq')]
    pallas_call x0 -> x12, Pallas kernels: none -> 57.2 us  [the longest x1 22.3 us: right_products(): pl.pallas_call(right_kernel, grid_spec=grid_spec, out_shape=[jax.ShapeDty...]
    div x5 -> x0, local copies, waits for them, and re-layouts: 36.6 us -> none  [the longest x4 36.5 us: opm_step(): jnp.einsum('ijk,mk->ijm', grad_rows, pair_weight, precision=PRECISE)]
    reduce_scatter x1 -> x0, waiting for transfers between devices: 34.2 us -> none  [body(): lax.psum_scatter(right_terms, 'res', scatter_dimension=1, tiled=True)]
    all_gather x1 -> x0, waiting for transfers between devices: 29.8 us -> none  [body(): lax.all_gather(right_act, 'res', axis=1, tiled=True)]
    all_to_all x0 -> x3, waiting for transfers between devices: none -> 27.3 us  [exchange(): return lax.all_to_all(send, 'seq', 0, 0, tiled=True)]
  transfers between devices with their start and end apart: 2 -> 16, of which waited for: 2 -> 8; matrix products, arithmetic and copies ran while one was open for 1% -> 6% of each run, Pallas kernels for 0% -> 16%
where the time goes in v1:
time: 198 us; the launch traced here: 196 us
  Pallas kernels  57.2 us (29%)
  waiting for transfers between devices  52.9 us (27%)
  local copies, waits for them, and re-layouts  33.4 us (17%)
  starting transfers between devices  32.6 us (16%)
  blocking collectives  16.6 us (8%)
  other arithmetic  2.66 us (1%)
    all_to_all x3, waiting for transfers between devices, exchange(): return lax.all_to_all(send, 'seq', 0, 0, tiled=True)  27.3 us
    unnamed x95, local copies, waits for them, and re-layouts  27 us
    pallas_call x1, Pallas kernels, right_products(): pl.pallas_call(right_kernel, grid_spec=grid_spec, out_shape=[jax.ShapeDty...  22.3 us
    ppermute x3, waiting for transfers between devices, send_chip(): lax.ppermute(values, 'x', [(i, (i + distance) % 4) for i in range(4)])  22.3 us
    all_to_all x3, starting transfers between devices, exchange(): return lax.all_to_all(send, 'seq', 0, 0, tiled=True)  20.7 us
    pallas_call x10, Pallas kernels, call(): pl.pallas_call(kernel, out_shape=shapes, scratch_shapes=list(scratch), co...  18.8 us
    all_to_all x1, blocking collectives, exchange(): return lax.all_to_all(send, 'seq', 0, 0, tiled=True)  16.6 us
    pallas_call x1, Pallas kernels, left_products(): pl.pallas_call(left_kernel, grid=(64 // ROWS,), in_specs=[pl.BlockSpec((F...  16.1 us
  transfers between devices with their start and end apart: 16, of which 8 were waited for; matrix products, arithmetic and copies ran while one was open for 6% of the time, Pallas kernels for 16%

profile of v1, /device:TPU:32, one launch (start us, length us, event | category | flops | bytes accessed | tf_op | source)
XLA Modules:
  0.0 195.6 jit_solution(2055457481942514487)
XLA Ops:
  0.0 0.8 copy.27.mask
  0.9 2.8 %collective-permute-start.2 = (s32[128,32]{1,0:T(8,128)S(1)}, s32[128,32]{1,0:T(8,128)S(1)}, u32[]{:S(2)}, u32[]{:S(2)}) collective-permute-start(s32[128,32]{1,0:T(8,128)S(1)} %copy.27.mask), channel_id=1, source_target_pairs={{2,0},{4,2},{6,4},{0,6},{3,1},{5,3},{7,5},{1,7},{10,8},{12,10},{14... | collective-permute-start | bytes 49160 | tf_op jit(solution)/shard_map/ppermute | solution.py:493
  3.7 0.8 collective-permute-start.3
  4.5 0.9 collective-permute-start.4
  5.4 1.2 copy-done.6
  6.7 1.1 norm_kernel.1
  7.8 1.0 copy-done.4
  9.4 0.7 collective-permute-done.3.mask_2
  10.1 0.7 collective-permute-done.4.mask_3
  10.8 1.0 pair_kernel.1
  11.8 11.4 %all-to-all-start = ((f32[32,24,128]{2,1,0:T(8,128)}), f32[32,24,128]{2,1,0:T(8,128)S(1)}, u32[]{:S(2)}, u32[]{:S(2)}) async-start(f32[32,24,128]{2,1,0:T(8,128)} %pair_kernel.1), calls=%async_computation | async-start | bytes 786432 | tf_op jit(solution)/shard_map/all_to_all | solution.py:501
  23.2 3.3 %dynamic-slice_bitcast_fusion = f32[32,4,32,128]{3,2,1,0:T(8,128)} fusion(f32[32,4,2,32,128]{4,3,2,1,0:T(8,128)} %bitcast.26, s32[]{:T(128)S(6)} %select_n.4), kind=kLoop, calls=%fused_computation | loop fusion | bytes 4194308 | tf_op jit(solution)/shard_map/jit(dynamic_index_in_dim)/squeeze | solution.py:526
  26.6 0.7 copy-done.37
  27.3 0.8 project_kernel.1
  28.2 1.0 copy-done
  29.2 0.6 copy-done.12
  29.9 0.6 copy-done.15
  30.5 7.4 %all-to-all-done.got = f32[32,24,128]{2,1,0:T(8,128)S(1)} async-done(((f32[32,24,128]{2,1,0:T(8,128)}), f32[32,24,128]{2,1,0:T(8,128)S(1)}, u32[]{:S(2)}, u32[]{:S(2)}) %all-to-all-start) | async-done | bytes 393248 | tf_op jit(solution)/shard_map/all_to_all | solution.py:501
  37.9 0.9 copy-done.13
  38.9 0.9 copy-done.16
  39.8 0.8 copy-done.23
  40.5 3.1 %score_kernel.1 = (f32[256,128]{1,0:T(8,128)S(1)}, f32[32,128]{1,0:T(8,128)S(1)}, f32[32,128]{1,0:T(8,128)S(1)}, f32[256,256]{1,0:T(8,128)S(1)}, f32[32,40,128]{2,1,0:T(8,128)}) custom-call(f32[32,24,128]{2,1,0:T(8,128)S(1)} %all-to-all-done.got, f32[256,128]{1,0:T(8,128)S(1)} %copy-done.13, f32[256,128]{1,0:T(8,128)S(1)} %copy-done.16, ...), custom_call_target="tpu_custom_call" | custom-call | flops 100000000 | bytes 1769472 | tf_op jit(solution)/shard_map/score_kernel/pallas_call | solution.py:351
  43.6 0.7 copy-done.18
  44.3 0.6 copy-done.29
  45.6 4.8 %all-to-all-start.1 = ((f32[32,40,128]{2,1,0:T(8,128)}), f32[32,40,128]{2,1,0:T(8,128)S(1)}, u32[]{:S(2)}, u32[]{:S(2)}) async-start(f32[32,40,128]{2,1,0:T(8,128)} %get-tuple-element.41), calls=%async_computation.1 | async-start | bytes 1310720 | tf_op jit(solution)/shard_map/all_to_all | solution.py:501
  50.3 0.8 copy.35
  51.1 0.8 copy.36
  52.6 0.8 copy.34
  53.5 16.6 %all-to-all-done.1.got = f32[32,40,128]{2,1,0:T(8,128)S(1)} async-done(((f32[32,40,128]{2,1,0:T(8,128)}), f32[32,40,128]{2,1,0:T(8,128)S(1)}, u32[]{:S(2)}, u32[]{:S(2)}) %all-to-all-start.1) | async-done | bytes 655392 | tf_op jit(solution)/shard_map/all_to_all | solution.py:501
  70.1 1.2 copy-done.5
  71.3 0.9 copy-done.30
  72.2 3.1 %attend_kernel.1 = (f32[256,128]{1,0:T(8,128)S(1)}, f32[32,64]{1,0:T(8,128)S(1)}, f32[2048,128]{1,0:T(8,128)S(1)}, f32[2048,128]{1,0:T(8,128)S(1)}, f32[32,128]{...) custom-call(f32[32,40,128]{2,1,0:T(8,128)S(1)} %all-to-all-done.1.got, ...), custom_call_target="tpu_custom_call" | custom-call | flops 100000000 | bytes 6283264 | tf_op jit(solution)/shard_map/attend_kernel/pallas_call | solution.py:351
  75.3 1.0 copy-done.2
  76.3 1.0 copy-done.8
  77.3 0.6 copy-done.38
  77.9 1.4 copy.38
  79.3 0.6 collective-permute-start.6
  79.9 1.5 collective-permute-start.7
  81.5 1.1 pad_maximum_fusion.left
  82.6 22.3 %right_products.1 = (bf16[32,2048,128]{2,1,0:T(8,128)(2,1)}, bf16[32,2048,128]{2,1,0:T(8,128)(2,1)}, f32[4,32,32,128]{3,2,1,0:T(8,128)S(1)}) custom-call(s32[2]{0:T(128)S(1)} %pad_add_fusion.place, f32[32,4,2,32,128]{4,3,2,1,0:T(8,128)} %bitcast.27, f32[32,4,32,128]{3,2,1,0:T(8,128)} %collective-permute-done.far_g, f32[64,128]{1,0:T(8,128)S(1)} %copy-done.39, ...), custom_call_target="tpu_custom_call" | custom-call | flops 16000000000 | bytes 42000000 | tf_op jit(solution)/shard_map/right_products/pallas_call | solution.py:433
  104.9 1.8 collective-permute-done.8.right_3
  106.7 16.1 %left_products.1 = f32[2048,128]{1,0:T(8,128)S(1)} custom-call(bf16[32,2048,128]{2,1,0:T(8,128)(2,1)} %get-tuple-element.48.high, bf16[32,2048,128]{2,1,0:T(8,128)(2,1)} %get-tuple-element.49.low, f32[32,32,128]{2,1,0:T(8,128)S(1)} %get-tuple-element.50.right_0, f32[32,32,128]{2,1,0:T(8,128)S(1)} %collective-permute-done.6.right_1, ...), custom_call_target="tpu_custom_call" | custom-call | flops 8999999488 | bytes 37000000 | tf_op jit(solution)/shard_map/left_products/pallas_call | solution.py:468
  123.5 2.7 %collective-permute-start.11 = (f32[32,32,128]{2,1,0:T(8,128)S(1)}, f32[32,32,128]{2,1,0:T(8,128)S(1)}, u32[]{:S(2)}, u32[]{:S(2)}) collective-permute-start(f32[32,32,128]{2,1,0:T(8,128)S(1)} %get-tuple-element.68), channel_id=1, source_target_pairs={{0,4},{2,6},{4,0},{6,2},{1,5},{3,7},{5,1},{7,3},{8,12},{10,14},{12... | collective-permute-start | bytes 1572872 | tf_op jit(solution)/shard_map/ppermute | solution.py:497
  126.3 2.0 %collective-permute-start.12 = (f32[32,32,128]{2,1,0:T(8,128)S(1)}, f32[32,32,128]{2,1,0:T(8,128)S(1)}, u32[]{:S(2)}, u32[]{:S(2)}) collective-permute-start(f32[32,32,128]{2,1,0:T(8,128)S(1)} %get-tuple-element.67), channel_id=1, source_target_pairs={{0,6},{2,0},{4,2},{6,4},{1,7},{3,1},{5,3},{7,5},{8,14},{10,8},{12,... | collective-permute-start | bytes 1572872 | tf_op jit(solution)/shard_map/ppermute | solution.py:497
  128.4 21.7 %collective-permute-done.10.right_1 = f32[32,32,128]{2,1,0:T(8,128)S(1)} collective-permute-done((f32[32,32,128]{2,1,0:T(8,128)S(1)}, f32[32,32,128]{2,1,0:T(8,128)S(1)}, u32[]{:S(2)}, u32[]{:S(2)}) %collective-permute-start.10) | collective-permute-done | bytes 524320 | tf_op jit(solution)/shard_map/ppermute | solution.py:497
  150.1 0.6 collective-permute-done.12.right_3
  150.7 4.1 %middle_kernel.1 = (f32[2048,128]{1,0:T(8,128)S(1)}, f32[2048,128]{1,0:T(8,128)S(1)}, f32[32,16,128]{2,1,0:T(8,128)S(1)}) custom-call(f32[1024,128]{1,0:T(8,128)S(1)} %get-tuple-element.72.left_own, f32[1024,128]{1,0:T(8,128)S(1)} %collective-permute-done.9.left_far, f32[32,32,128]{2,1,0:T(8,128)S(1)} %get-tuple-element.70.right_own, ...), custom_call_target="tpu_custom_call" | custom-call | flops 100000000 | bytes 8716288 | tf_op jit(solution)/shard_map/middle_kernel/pallas_call | solution.py:351
  154.8 16.6 %all_to_all.20.got = f32[32,16,128]{2,1,0:T(8,128)S(1)} all-to-all(f32[32,16,128]{2,1,0:T(8,128)S(1)} %get-tuple-element.55), channel_id=1, replica_groups=mesh['seq'=32,'x'=4,'core'=2] {'seq'}, dimensions={0} | all-to-all | bytes 524288 | tf_op jit(solution)/shard_map/all_to_all | solution.py:501
  171.4 2.1 %score_back_kernel.1 = (f32[256,128]{1,0:T(8,128)S(1)}, f32[256,256]{1,0:T(8,128)S(1)}, f32[32,16,128]{2,1,0:T(8,128)S(1)}) custom-call(f32[32,16,128]{2,1,0:T(8,128)S(1)} %all_to_all.20.got, f32[32,64]{1,0:T(8,128)S(1)} %get-tuple-element.56.attended, f32[256,128]{1,0:T(8,128)S(1)} %get-tuple-element.57.probs, f32[256,128]{1,0:T(8,128)S(1)} %copy-done.14, ...), custom_call_target="tpu_custom_call" | custom-call | flops 100000000 | bytes 1318912 | tf_op jit(solution)/shard_map/score_back_kernel/pallas_call | solution.py:351
  173.5 0.7 copy-done.20
  174.2 0.7 copy-done.22
  174.9 0.7 copy-done.31
  175.6 4.6 %all-to-all-start.3 = ((f32[32,16,128]{2,1,0:T(8,128)}), f32[32,16,128]{2,1,0:T(8,128)S(1)}, u32[]{:S(2)}, u32[]{:S(2)}) async-start(f32[32,16,128]{2,1,0:T(8,128)} %copy-done.22), calls=%async_computation.3 | async-start | bytes 524288 | tf_op jit(solution)/shard_map/all_to_all | solution.py:501
  180.1 1.3 pad_maximum_fusion.2
  181.4 1.4 copy.39.key_value
  182.8 1.2 copy-done.9
  184.0 1.2 copy-done.11
  185.3 0.8 copy-done.28
  187.1 0.9 key_back_kernel.1.x_grad
  188.0 3.3 %all-to-all-done.3.got = f32[32,16,128]{2,1,0:T(8,128)S(1)} async-done(((f32[32,16,128]{2,1,0:T(8,128)}), f32[32,16,128]{2,1,0:T(8,128)S(1)}, u32[]{:S(2)}, u32[]{:S(2)}) %all-to-all-start.3) | async-done | bytes 262176 | tf_op jit(solution)/shard_map/all_to_all | solution.py:501
  191.3 0.8 copy-done.24
  192.1 0.7 copy-done.34
  192.8 0.7 copy-done.36
  193.5 2.1 %final_kernel.1 = f32[128,2048]{1,0:T(8,128)} custom-call(f32[32,16,128]{2,1,0:T(8,128)S(1)} %all-to-all-done.3.got, f32[32,128]{1,0:T(8,128)S(1)} %copy-done.36, f32[64,64]{1,0:T(8,128)S(1)} %copy-done.24, f32[32,128]{1,0:T(8,128)S(1)} %get-tuple-element.40.present, f32[2048,128]{1,0:T(8,128)S(1)} %get-tuple-element.37.x0t, f32[32,128]{1,0:T(8,128)S(1)} %copy-done.34, ...), custom_call_target="tpu_custom_call" | custom-call | flops 100000000 | bytes 4521984 | tf_op jit(solution)/shard_map/final_kernel/pallas_call | solution.py:351
  (88 shorter events, 4.0 us)
Async XLA Ops:
  0.8 8.6 %collective-permute-start.1 = (s32[128,32]{1,0:T(8,128)S(1)}, s32[128,32]{1,0:T(8,128)S(1)}, u32[]{:S(2)}, u32[]{:S(2)}) collective-permute-start(s32[128,32]{1,0:T(8,128)S(1)} %copy.27.mask), channel_id=1, source_target_pairs={{0,1},{1,0},{2,3},{3,2},{4,5},{5,4},{6,7},{7,6},{8,9},{9,8},{10,11... | collective-permute-start | bytes 49160 | tf_op jit(solution)/shard_map/ppermute | solution.py:489
  0.9 8.5 %collective-permute-start.2 = (s32[128,32]{1,0:T(8,128)S(1)}, s32[128,32]{1,0:T(8,128)S(1)}, u32[]{:S(2)}, u32[]{:S(2)}) collective-permute-start(s32[128,32]{1,0:T(8,128)S(1)} %copy.27.mask), channel_id=1, source_target_pairs={{2,0},{4,2},{6,4},{0,6},{3,1},{5,3},{7,5},{1,7},{10,8},{12,10},{14... | collective-permute-start | bytes 49160 | tf_op jit(solution)/shard_map/ppermute | solution.py:493
  3.7 6.4 %collective-permute-start.3 = (s32[128,32]{1,0:T(8,128)S(1)}, s32[128,32]{1,0:T(8,128)S(1)}, u32[]{:S(2)}, u32[]{:S(2)}) collective-permute-start(s32[128,32]{1,0:T(8,128)S(1)} %copy.27.mask), channel_id=1, source_target_pairs={{4,0},{6,2},{0,4},{2,6},{5,1},{7,3},{1,5},{3,7},{12,8},{14,10},{8,... | collective-permute-start | bytes 49160 | tf_op jit(solution)/shard_map/ppermute | solution.py:493
  4.5 6.3 %collective-permute-start.4 = (s32[128,32]{1,0:T(8,128)S(1)}, s32[128,32]{1,0:T(8,128)S(1)}, u32[]{:S(2)}, u32[]{:S(2)}) collective-permute-start(s32[128,32]{1,0:T(8,128)S(1)} %copy.27.mask), channel_id=1, source_target_pairs={{6,0},{0,2},{2,4},{4,6},{7,1},{1,3},{3,5},{5,7},{14,8},{8,10},{10,... | collective-permute-start | bytes 49160 | tf_op jit(solution)/shard_map/ppermute | solution.py:493
  5.4 1.2 copy-start.6
  7.8 1.0 copy-start.4
  8.8 0.6 copy-start.33
  11.8 26.2 %all-to-all-start = ((f32[32,24,128]{2,1,0:T(8,128)}), f32[32,24,128]{2,1,0:T(8,128)S(1)}, u32[]{:S(2)}, u32[]{:S(2)}) async-start(f32[32,24,128]{2,1,0:T(8,128)} %pair_kernel.1), calls=%async_computation | async-start | bytes 786432 | tf_op jit(solution)/shard_map/all_to_all | solution.py:501
  23.2 3.3 %copy-start.27 = (f32[64,64]{1,0:T(8,128)S(1)}, f32[64,64]{1,0:T(8,128)}, u32[]{:S(2)}) copy-start(f32[64,64]{1,0:T(8,128)} %filter_weight.1) | copy-start | bytes 49156
  23.2 3.4 %copy-start.44 = (f32[64,8]{0,1:T(8,128)S(1)}, f32[64,8]{0,1:T(8,128)}, u32[]{:S(2)}) copy-start(f32[64,8]{0,1:T(8,128)} %param.18) | copy-start | bytes 6148
  23.2 3.4 %copy-start.7 = (f32[128,2048]{1,0:T(8,128)S(1)}, f32[128,2048]{1,0:T(8,128)}, u32[]{:S(2)}) copy-start(f32[128,2048]{1,0:T(8,128)} %slope.1) | copy-start | bytes 3145732
  26.5 56.1 %collective-permute-start = (f32[32,4,32,128]{3,2,1,0:T(8,128)}, f32[32,4,32,128]{3,2,1,0:T(8,128)}, u32[]{:S(2)}, u32[]{:S(2)}) collective-permute-start(f32[32,4,32,128]{3,2,1,0:T(8,128)} %dynamic-slice_bitcast_fusion), channel_id=1, source_target_pairs={{0,1},{1,0},{2,3},{3,2},{4,5},{5,4},{6,7},{7,6},{8,9},{9,8},{10,11... | collective-permute-start | bytes 6291464 | tf_op jit(solution)/shard_map/ppermute | solution.py:489
  26.6 0.7 copy-start.37
  28.2 1.1 copy-start
  29.2 0.6 copy-start.12
  29.9 0.6 copy-start.15
  37.9 0.9 copy-start.13
  38.8 0.9 copy-start.16
  39.8 0.8 copy-start.23
  43.6 0.7 copy-start.18
  44.3 0.6 copy-start.29
  45.0 0.6 copy-start.35
  45.6 24.5 %all-to-all-start.1 = ((f32[32,40,128]{2,1,0:T(8,128)}), f32[32,40,128]{2,1,0:T(8,128)S(1)}, u32[]{:S(2)}, u32[]{:S(2)}) async-start(f32[32,40,128]{2,1,0:T(8,128)} %get-tuple-element.41), calls=%async_computation.1 | async-start | bytes 1310720 | tf_op jit(solution)/shard_map/all_to_all | solution.py:501
  51.1 0.8 copy-start.40
  52.0 0.6 copy-start.42
  70.1 1.2 copy-start.5
  71.3 0.9 copy-start.30
  75.3 1.0 copy-start.2
  76.3 1.0 copy-start.8
  77.3 0.6 copy-start.38
  77.9 4.7 %copy-start.39 = (f32[64,128]{1,0:T(8,128)S(1)}, f32[64,128]{1,0:T(8,128)}, u32[]{:S(2)}) copy-start(f32[64,128]{1,0:T(8,128)} %copy-done.38) | copy-start | bytes 98308
  77.9 3.6 %collective-permute-start.5 = (f32[1024,128]{1,0:T(8,128)}, f32[1024,128]{1,0:T(8,128)S(1)}, u32[]{:S(2)}, u32[]{:S(2)}) collective-permute-start(f32[1024,128]{1,0:T(8,128)} %get-tuple-element.47), channel_id=1, source_target_pairs={{0,1},{1,0},{2,3},{3,2},{4,5},{5,4},{6,7},{7,6},{8,9},{9,8},{10,11... | collective-permute-start | bytes 1572872 | tf_op jit(solution)/shard_map/ppermute | solution.py:489
  79.3 25.6 %collective-permute-start.6 = (f32[32,32,128]{2,1,0:T(8,128)S(1)}, f32[32,32,128]{2,1,0:T(8,128)S(1)}, u32[]{:S(2)}, u32[]{:S(2)}) collective-permute-start(f32[32,32,128]{2,1,0:T(8,128)S(1)} %get-tuple-element.50.right_0), channel_id=1, source_target_pairs={{2,0},{4,2},{6,4},{0,6},{3,1},{5,3},{7,5},{1,7},{10,8},{12,10},{14... | collective-permute-start | bytes 1572872 | tf_op jit(solution)/shard_map/ppermute | solution.py:493
  79.9 25.0 %collective-permute-start.7 = (f32[32,32,128]{2,1,0:T(8,128)S(1)}, f32[32,32,128]{2,1,0:T(8,128)S(1)}, u32[]{:S(2)}, u32[]{:S(2)}) collective-permute-start(f32[32,32,128]{2,1,0:T(8,128)S(1)} %get-tuple-element.50.right_0), channel_id=1, source_target_pairs={{4,0},{6,2},{0,4},{2,6},{5,1},{7,3},{1,5},{3,7},{12,8},{14,10},{8,... | collective-permute-start | bytes 1572872 | tf_op jit(solution)/shard_map/ppermute | solution.py:493
  81.5 25.3 %collective-permute-start.8 = (f32[32,32,128]{2,1,0:T(8,128)S(1)}, f32[32,32,128]{2,1,0:T(8,128)S(1)}, u32[]{:S(2)}, u32[]{:S(2)}) collective-permute-start(f32[32,32,128]{2,1,0:T(8,128)S(1)} %get-tuple-element.50.right_0), channel_id=1, source_target_pairs={{6,0},{0,2},{2,4},{4,6},{7,1},{1,3},{3,5},{5,7},{14,8},{8,10},{10,... | collective-permute-start | bytes 1572872 | tf_op jit(solution)/shard_map/ppermute | solution.py:493
  122.9 5.4 %collective-permute-start.9 = (f32[1024,128]{1,0:T(8,128)S(1)}, f32[1024,128]{1,0:T(8,128)S(1)}, u32[]{:S(2)}, u32[]{:S(2)}) collective-permute-start(f32[1024,128]{1,0:T(8,128)S(1)} %get-tuple-element.71), channel_id=1, source_target_pairs={{0,1},{1,0},{2,3},{3,2},{4,5},{5,4},{6,7},{7,6},{8,9},{9,8},{10,11... | collective-permute-start | bytes 1572872 | tf_op jit(solution)/shard_map/ppermute | solution.py:489
  123.0 5.3 %copy-start.41 = (f32[64,32]{1,0:T(8,128)S(1)}, f32[64,32]{1,0:T(8,128)}, u32[]{:S(2)}) copy-start(f32[64,32]{1,0:T(8,128)} %copy-done.40) | copy-start | bytes 24580
  123.0 5.3 %copy-start.43 = (f32[64,32]{1,0:T(8,128)S(1)}, f32[64,32]{1,0:T(8,128)}, u32[]{:S(2)}) copy-start(f32[64,32]{1,0:T(8,128)} %copy-done.42) | copy-start | bytes 24580
  123.0 27.7 %copy-start.1 = (f32[2048,128]{1,0:T(8,128)S(1)}, f32[2048,128]{1,0:T(8,128)}, u32[]{:S(2)}) copy-start(f32[2048,128]{1,0:T(8,128)} %copy-done) | copy-start | bytes 3145732
  123.0 27.6 %copy-start.3 = (f32[2048,128]{1,0:T(8,128)S(1)}, f32[2048,128]{1,0:T(8,128)}, u32[]{:S(2)}) copy-start(f32[2048,128]{1,0:T(8,128)} %copy-done.2) | copy-start | bytes 3145732
  123.0 27.6 %copy-start.26 = (f32[64,64]{1,0:T(8,128)S(1)}, f32[64,64]{1,0:T(8,128)}, u32[]{:S(2)}) copy-start(f32[64,64]{1,0:T(8,128)} %mixing_back.1) | copy-start | bytes 49156
  123.2 26.8 %collective-permute-start.10 = (f32[32,32,128]{2,1,0:T(8,128)S(1)}, f32[32,32,128]{2,1,0:T(8,128)S(1)}, u32[]{:S(2)}, u32[]{:S(2)}) collective-permute-start(f32[32,32,128]{2,1,0:T(8,128)S(1)} %get-tuple-element.69), channel_id=1, source_target_pairs={{0,2},{2,4},{4,6},{6,0},{1,3},{3,5},{5,7},{7,1},{8,10},{10,12},{12... | collective-permute-start | bytes 1572872 | tf_op jit(solution)/shard_map/ppermute | solution.py:497
  123.5 26.5 %collective-permute-start.11 = (f32[32,32,128]{2,1,0:T(8,128)S(1)}, f32[32,32,128]{2,1,0:T(8,128)S(1)}, u32[]{:S(2)}, u32[]{:S(2)}) collective-permute-start(f32[32,32,128]{2,1,0:T(8,128)S(1)} %get-tuple-element.68), channel_id=1, source_target_pairs={{0,4},{2,6},{4,0},{6,2},{1,5},{3,7},{5,1},{7,3},{8,12},{10,14},{12... | collective-permute-start | bytes 1572872 | tf_op jit(solution)/shard_map/ppermute | solution.py:497
  126.3 24.4 %collective-permute-start.12 = (f32[32,32,128]{2,1,0:T(8,128)S(1)}, f32[32,32,128]{2,1,0:T(8,128)S(1)}, u32[]{:S(2)}, u32[]{:S(2)}) collective-permute-start(f32[32,32,128]{2,1,0:T(8,128)S(1)} %get-tuple-element.67), channel_id=1, source_target_pairs={{0,6},{2,0},{4,2},{6,4},{1,7},{3,1},{5,3},{7,5},{8,14},{10,8},{12,... | collective-permute-start | bytes 1572872 | tf_op jit(solution)/shard_map/ppermute | solution.py:497
  150.7 20.7 %copy-start.14 = (f32[256,128]{1,0:T(8,128)S(1)}, f32[256,128]{1,0:T(8,128)}, u32[]{:S(2)}) copy-start(f32[256,128]{1,0:T(8,128)} %copy-done.12) | copy-start | bytes 393220
  150.7 20.7 %copy-start.17 = (f32[256,128]{1,0:T(8,128)S(1)}, f32[256,128]{1,0:T(8,128)}, u32[]{:S(2)}) copy-start(f32[256,128]{1,0:T(8,128)} %copy-done.15) | copy-start | bytes 393220
  154.8 18.7 %copy-start.10 = (f32[2048,128]{1,0:T(8,128)}, f32[2048,128]{1,0:T(8,128)S(1)}, u32[]{:S(2)}) copy-start(f32[2048,128]{1,0:T(8,128)S(1)} %get-tuple-element.64.out_grad) | copy-start | bytes 3145732
  173.5 0.7 copy-start.20
  174.2 0.7 copy-start.22
  174.9 0.7 copy-start.31
  175.6 15.8 %all-to-all-start.3 = ((f32[32,16,128]{2,1,0:T(8,128)}), f32[32,16,128]{2,1,0:T(8,128)S(1)}, u32[]{:S(2)}, u32[]{:S(2)}) async-start(f32[32,16,128]{2,1,0:T(8,128)} %copy-done.22), calls=%async_computation.3 | async-start | bytes 524288 | tf_op jit(solution)/shard_map/all_to_all | solution.py:501
  182.8 1.2 copy-start.9
  184.0 1.2 copy-start.11
  185.3 0.8 copy-start.28
  186.0 0.9 copy-start.19
  186.0 1.0 copy-start.21
  186.0 1.0 copy-start.25
  186.0 1.1 copy-start.32
  191.3 0.8 copy-start.24
  192.1 0.7 copy-start.34
  192.8 0.7 copy-start.36

commit v2 on v1

--- a/solution.py
+++ b/solution.py
@@ -1,3 +1,5 @@
+import functools
+
 import jax
 import jax.numpy as jnp
 from jax import lax
@@ -112,12 +114,11 @@
     send[:, rows, :] = jnp.broadcast_to(values[None], (send.shape[0],) + values.shape)
 
 
-def norm_kernel(m0, mask, m0t, x0t, inverse, present, send):
+def norm_kernel(m0, mask, x0t, inverse, present, send):
     shown = mask[...].astype(F32).T
     present[...] = shown
     for pair in range(RES // 2):
         block = m0[:, 128 * pair : 128 * pair + 128].T
-        m0t[128 * pair : 128 * pair + 128] = block
         for k in range(2):
             part = block[64 * k : 64 * k + 64]
             center = part - jnp.mean(part, axis=0, keepdims=True)
@@ -146,9 +147,10 @@
         send[peer, 17 : 17 + share, :] = count[share * peer : share * peer + share]
 
 
-def project_kernel(x0t, slope, key, value_gate, keys, values, gate, slope_t):
+def project_kernel(x0t, m0, slope, key, value_gate, keys, values, gate, m0t, slope_t):
     parts = lhs_parts(value_gate[...])
     for pair in range(RES // 2):
+        m0t[128 * pair : 128 * pair + 128] = m0[:, 128 * pair : 128 * pair + 128].T
         slope_t[128 * pair : 128 * pair + 128] = slope[:, 128 * pair : 128 * pair + 128].T
         row = 128 * pair
         both = jnp.concatenate([x0t[row : row + 64], x0t[row + 64 : row + 128]], axis=1)
@@ -177,46 +179,86 @@
     raw = jnp.exp(scores - top)
     weights[...] = raw
     total = jnp.sum(raw, axis=1, keepdims=True)
-    folded = fold_blocks(exact_nt(raw, values[...]))
-    rows, lanes = row_lane((RES * 8, 128))
-    head = rows % 8
-    packed = jnp.where(lanes < 64, jnp.where(lanes // 8 == head, folded, 0.0), 0.0)
-    packed = jnp.where(lanes == 64 + head, top, packed)
-    packed = jnp.where(lanes == 72 + head, total, packed)
-    packed = sum_heads(packed)
-    local[...] = packed
-    send_all(send, slice(0, 32), packed)
+    rows, lanes = row_lane((RES * 8, 64))
+    own_head = rows % 8 == lanes // 8
+    weighted = sum_heads(jnp.where(own_head, fold_blocks(exact_nt(raw, values[...]))[:, :64], 0.0))
+    send_all(send, slice(0, 16), pack(weighted))
+    rows, lanes = row_lane((RES * 8, 16))
+    stats = jnp.where(lanes == rows % 8, top, jnp.where(lanes == 8 + rows % 8, total, 0.0))
+    stats = sum_heads(stats)
+    local[...] = stats
     share = 64 // send.shape[0]
-    send[:, 32:, :] = jnp.zeros((send.shape[0], send.shape[1] - 32, 128), F32)
-    send_all(send, slice(32, 32 + share), sums[17 : 17 + share])
+    pairs = sums[17 : 17 + share]
+    stats = jnp.concatenate([stats[8 * k : 8 * k + 8] for k in range(4)], axis=1)
+    if share == 2:
+        right = jnp.concatenate([pairs[:, :64], pairs[:, 64:], jnp.zeros((4, 64), F32)], axis=0)
+    else:
+        right = jnp.zeros((8, 64), F32)
+        send_all(send, slice(send.shape[1] - share, send.shape[1]), pairs)
+    send_all(send, slice(16, 24), jnp.concatenate([stats, right], axis=1))
+    products = raw.reshape(RES, 8, 1, SEQ) * values[...].reshape(RES, 1, 8, SEQ)
+    products = products.reshape(RES * 64, SEQ)
+    half = RES // 2
+    rows, lanes = row_lane((half * 64, 128))
+    same = rows // 64 == lanes // 8
+    r, c = row_lane((128, 64))
+    fold = jnp.where(r % 8 == c % 8, 1.0, 0.0).astype(jnp.bfloat16)
+    moments = []
+    for k in range(2):
+        a_high, a_low = split(products[half * 64 * k : half * 64 * (k + 1)])
+        b_high, b_low = split(keys[128 * k : 128 * k + 128])
+        found = dot_nt(
+            jnp.concatenate([a_high, a_high, a_low], axis=1), jnp.concatenate([b_high, b_low, b_high], axis=1)
+        )
+        f_high, f_low = split(jnp.where(same, found, 0.0))
+        spread = dot_nn(f_high, fold) + dot_nn(f_low, fold)
+        spread = jnp.where(rows[:, :64] % 8 == lanes[:, :64] // 8, spread, 0.0)
+        moments.append(jnp.sum(spread.reshape(half * 8, 8, 64), axis=1))
+    moments = jnp.concatenate(moments, axis=0)
+    firsts = fold_blocks(exact_nt(raw, keys[...]))
+    rows, lanes = row_lane((RES * 8, 64))
+    rest = jnp.where(lanes < 8, firsts[:, :64], jnp.where(lanes == 8, top, jnp.where(lanes == 9, total, 0.0)))
+    block = jnp.concatenate([moments, rest], axis=1)
+    size = RES * 8 // send.shape[0]
+    send[:, 24 : 24 + size, :] = block.reshape(send.shape[0], size, 128)
 
 
 def attend_kernel(
     got, local, raw, m0t, gate, present, mixing, factors,
-    probs, attended, mixed, x1t, inverse_mid, left, right, inverse_count, scratch,
+    probs, attended, mixed, x1t, inverse_mid, left, right, inverse_count, moments, scratch, arrive,
 ):
     peers = got.shape[0]
     share = 64 // peers
     for peer in range(peers):
-        inverse_count[share * peer : share * peer + share] = 1.0 / got[peer, 32 : 32 + share, :]
-    parts = got[:, 0:32, :]
-    top = jnp.max(parts, axis=0)
-    lane = lax.broadcasted_iota(jnp.int32, (peers, RES, 128), 2)
-    factor = jnp.where((lane >= 64) & (lane < 72), jnp.exp(parts - top[None]), 0.0)
-    r, c = row_lane((128, 128))
-    expand = ((c < 64) & (r == 64 + c // 8)) | ((c >= 72) & (c < 80) & (r == c - 8))
-    expand = jnp.where(expand, 1.0, 0.0).astype(jnp.bfloat16)
-    high, low = split(factor.reshape(peers * RES, 128))
-    factor = (dot_nn(high, expand) + dot_nn(low, expand)).reshape(peers, RES, 128)
-    total = jnp.sum(factor * parts, axis=0)
-    share = jnp.exp(local[:, 64:72] - top[:, 64:72]) / total[:, 72:80]
-    probs[...] = raw[...] * head_column(share)
-    spread = jnp.where((c < 64) & (r == 72 + c // 8), 1.0, 0.0)
-    heads = total[:, :64] / exact_nn(total, spread)[:, :64]
+        if share == 2:
+            pairs = jnp.concatenate([got[peer, 16:18, 64:], got[peer, 18:20, 64:]], axis=1)
+        else:
+            pairs = got[peer, got.shape[1] - share :, :]
+        inverse_count[share * peer : share * peer + share] = 1.0 / pairs
+    weighted = jnp.concatenate([got[:, 0:16, 0:64], got[:, 0:16, 64:128]], axis=1)
+    stats = jnp.concatenate([got[:, 16:24, 16 * k : 16 * k + 16] for k in range(4)], axis=1)
+    tops = stats[:, :, 0:8]
+    top = jnp.max(tops, axis=0)
+    factor = jnp.exp(tops - top[None])
+    total = jnp.sum(factor * stats[:, :, 8:16], axis=0)
+    r, c = row_lane((8, 64))
+    expand = jnp.where(r == c // 8, 1.0, 0.0)
+    high, low = split(factor.reshape(peers * RES, 8))
+    wide = expand.astype(jnp.bfloat16)
+    factor = (dot_nn(high, wide) + dot_nn(low, wide)).reshape(peers, RES, 64)
+    heads = jnp.sum(factor * weighted, axis=0) / exact_nn(total, expand)
+    probs[...] = raw[...] * head_column(jnp.exp(local[:, 0:8] - top) / total)
     attended[...] = heads
+    size = RES * 8 // peers
+    block = got[:, 24 : 24 + size, :]
+    tops = block[:, :, 72:73]
+    block = jnp.sum(jnp.exp(tops - jnp.max(tops, axis=0)[None]) * block, axis=0)
+    lanes = lax.broadcasted_iota(jnp.int32, block.shape, 1)
+    moments[...] = jnp.where(lanes < 72, block / block[:, 73:74], 0.0)
     heads_t = heads.T
     mixing_parts = lhs_parts(mixing[...])
     factor_parts = lhs_parts(factors[...])
+    arrive()
     for pair in range(RES // 2):
         shown, used, base = [], [], []
         for k in range(2):
@@ -244,7 +286,7 @@
 
 
 def middle_kernel(
-    left_own, left_far, right_own, right_1, right_2, right_3, x1t, inverse_mid, present, slope_t, gate,
+    left_own, left_far_0, left_far_1, right_own, right_1, right_2, right_3, moments, x1t, inverse_mid, present, slope_t, gate,
     factors_back, mixing_back, mid, out_grad, send, scratch,
 ):
     for f in range(FACTOR_WIDTH):
@@ -258,8 +300,10 @@
         for k in range(2):
             i = 2 * pair + k
             rows = slice(32 * i, 32 * i + 32)
+            left_far = left_far_0 if i < RES // 2 else left_far_1
+            near = slice(32 * (i % 16), 32 * (i % 16) + 32)
             both = jnp.concatenate(
-                [left_own[rows] + left_far[rows], scratch[pl.ds(i, FACTOR_WIDTH, stride=RES), :]], axis=0
+                [left_own[rows] + left_far[near], scratch[pl.ds(i, FACTOR_WIDTH, stride=RES), :]], axis=0
             )
             grads.append(both * present[i : i + 1])
         mid_in = project(parts, jnp.concatenate(grads, axis=1))
@@ -285,6 +329,7 @@
         sums.append(sum_lanes_01(ones, jnp.concatenate(gated, axis=0)))
     sums = [jnp.concatenate([part, part], axis=0) for part in sums]
     send_all(send, slice(0, 16), pack(own_blocks(jnp.concatenate(sums, axis=1))))
+    send_all(send, slice(16, 16 + moments.shape[0]), moments[...])
 
 
 def gate_back_kernel(out_grad, mixed, gate, filter_weight, x_grad):
@@ -299,44 +344,39 @@
             x_grad[128 * pair + 64 * k : 128 * pair + 64 * k + 64] = found[:, SEQ * k : SEQ * k + SEQ]
 
 
-def score_back_kernel(got, attended, probs, keys, values, score_grad, grad_blocks, send):
-    att_grad = unpack(jnp.sum(got[...], axis=0))
+def finish_kernel(
+    got, attended, probs, keys, values, query_blocks, partial, key_value, counts, asking, present, x0t, inverse, mid, out, arrive
+):
+    att_grad = unpack(jnp.sum(got[:, 0:16, :], axis=0))
+    moments = got[:, 16:, :].reshape(RES * 8, 128)
+    rows, lanes = row_lane((RES * 8, 64))
+    own_head = rows % 8 == lanes // 8
+    along = jnp.sum(jnp.where(own_head, over_heads(att_grad * attended[...]), 0.0), axis=1, keepdims=True)
+    r, c = row_lane((64, 64))
+    spread = exact_nn(jnp.where(own_head, over_heads(att_grad), 0.0), (r % 8 == c // 8).astype(F32))
+    both = jnp.concatenate([spread * moments[:, :64], -along * moments[:, 64:]], axis=1)
+    r, c = row_lane((128, 64))
+    query_grad = exact_nn(both, jnp.where((r < 72) & (r % 8 == c % 8), 1.0, 0.0))
+    query_grad = sum_heads(jnp.where(own_head, query_grad, 0.0)) * HEAD_SIZE ** (-0.5)
+    mean_grad = (exact_nt(query_grad, asking[...]) / counts[:, :64]).T
+
     blocks = head_blocks(att_grad)
-    grad_blocks[...] = blocks
-    rows, lanes = row_lane((RES * 8, 64))
-    along = jnp.sum(
-        jnp.where(rows % 8 == lanes // 8, over_heads(att_grad * attended[...]), 0.0), axis=1, keepdims=True
-    )
-    grad = probs[...] * (exact_nn(blocks, values[...]) - along)
-    score_grad[...] = grad
-    folded = fold_blocks(exact_nt(grad, keys[...]))[:, :64]
-    send_all(send, slice(0, 16), pack(sum_heads(jnp.where(rows % 8 == lanes // 8, folded, 0.0))))
-
-
-def key_back_kernel(score_grad, grad_blocks, query_blocks, probs, partial, key_value, x_grad):
-    key_grad = exact_nn(query_blocks[...].T, score_grad[...])
-    value_grad = exact_nn(grad_blocks[...].T, probs[...])
+    score_grad = probs[...] * (exact_nn(blocks, values[...]) - along)
+    key_grad = exact_nn(query_blocks[...].T, score_grad)
+    value_grad = exact_nn(blocks.T, probs[...])
     parts = lhs_parts(key_value[...])
+    arrive()
     for pair in range(RES // 2):
         both = []
         for k in range(2):
             rows = slice(16 * pair + 8 * k, 16 * pair + 8 * k + 8)
             both.append(jnp.concatenate([key_grad[rows], value_grad[rows]], axis=0))
         found = project(parts, jnp.concatenate(both, axis=1))
-        for k in range(2):
-            rows = slice(128 * pair + 64 * k, 128 * pair + 64 * k + 64)
-            x_grad[rows] = partial[rows] + found[:, SEQ * k : SEQ * k + SEQ]
-
-
-def final_kernel(got, counts, asking, present, x0t, inverse, x_grad, mid, out):
-    query_grad = unpack(jnp.sum(got[...], axis=0)) * HEAD_SIZE ** (-0.5)
-    mean_grad = (exact_nt(query_grad, asking[...]) / counts[:, :64]).T
-    for pair in range(RES // 2):
         done = []
         for k in range(2):
             i = 2 * pair + k
             rows = slice(64 * i, 64 * i + 64)
-            grad = x_grad[rows] + mean_grad[:, i : i + 1] * present[i : i + 1]
+            grad = partial[rows] + found[:, SEQ * k : SEQ * k + SEQ] + mean_grad[:, i : i + 1] * present[i : i + 1]
             normed = x0t[rows]
             back = inverse[i : i + 1] * (
                 grad - jnp.mean(grad, axis=0, keepdims=True) - normed * jnp.mean(grad * normed, axis=0, keepdims=True)
@@ -345,23 +385,68 @@
         out[:, 128 * pair : 128 * pair + 128] = jnp.concatenate(done, axis=0).T
 
 
-def call(kernel, shapes, *operands, scratch=(), flops=100_000_000, vmem=24):
+def whole(shape):
+    return pl.BlockSpec(shape, lambda *_: (0,) * len(shape))
+
+
+def staged(kernel, count, late, *refs):
+    operands, rest = refs[: count[0]], refs[count[0] :]
+    results, rest = rest[: count[1]], rest[count[1] :]
+    total = count[0] + count[1]
+    held, sems, scratch = rest[:total], rest[total], rest[total + 1 :]
+    copies = [pltpu.make_async_copy(operands[k], held[k], sems.at[k]) for k in range(count[0])]
+    for copy in copies:
+        copy.start()
+
+    def arrive():
+        for k in late:
+            copies[k].wait()
+
+    for k in range(count[0]):
+        if k not in late:
+            copies[k].wait()
+    kernel(*held, *scratch, *([arrive] if late else []))
+    copies = [
+        pltpu.make_async_copy(held[count[0] + k], results[k], sems.at[count[0] + k]) for k in range(count[1])
+    ]
+    for copy in copies:
+        copy.start()
+    for copy in copies:
+        copy.wait()
+
+
+def call(kernel, shapes, *operands, scratch=(), late=(), free=(), vmem=40):
     shapes = [jax.ShapeDtypeStruct(shape, F32) for shape in shapes]
     size = sum(4 * array.size for array in shapes) + sum(array.size * array.dtype.itemsize for array in operands)
+    arrays = list(operands) + shapes
     return pl.pallas_call(
-        kernel,
-        out_shape=shapes,
-        scratch_shapes=list(scratch),
+        functools.partial(staged, kernel, (len(operands), len(shapes)), late),
+        in_specs=[
+            pl.BlockSpec(memory_space=pl.ANY if k in free else pltpu.HBM) for k in range(len(operands))
+        ],
+        out_specs=[pl.BlockSpec(memory_space=pltpu.HBM)] * len(shapes),
+        out_shape=[pltpu.HBM(array.shape, array.dtype) for array in shapes],
+        scratch_shapes=[pltpu.VMEM(array.shape, array.dtype) for array in arrays]
+        + [pltpu.SemaphoreType.DMA((len(arrays),))]
+        + list(scratch),
         compiler_params=pltpu.CompilerParams(vmem_limit_bytes=vmem * 2**20),
-        cost_estimate=pl.CostEstimate(flops=flops, bytes_accessed=int(size), transcendentals=0),
+        cost_estimate=pl.CostEstimate(flops=100_000_000, bytes_accessed=int(size), transcendentals=0),
         name=kernel.__name__,
-    )(*operands)
+    )(
+        *[
+            array if k in free else pltpu.with_memory_space_constraint(array, pltpu.HBM)
+            for k, array in enumerate(operands)
+        ]
+    )
 
 
 ROWS = 8
-
-
-def right_kernel(place, own_g, far_g, inverse_count, weight, left, high, low, out, weights, total):
+COST = 1000
+
+
+def right_kernel(
+    place, own_g, far_g, inverse_count, weight, left, left_far, high, low, out_0, out_1, out_2, out_3, weights, total
+):
     step = pl.program_id(0)
     x = place[0]
 
@@ -391,22 +476,23 @@
             rows, lanes = slice(row, row + FACTOR_WIDTH), slice(128 * k, 128 * k + 128)
             high[:, rows, :] = grads_high[:, lanes].reshape(FACTOR_WIDTH, FACTOR_WIDTH, 128)
             low[:, rows, :] = grads_low[:, lanes].reshape(FACTOR_WIDTH, FACTOR_WIDTH, 128)
-    l_high, l_low = split(left[...].T)
+    l_high, l_low = split(jnp.where(near, left[...], left_far[...]).T)
+    block = slice(None)
     stacked = jnp.concatenate([l_high, l_low], axis=0)
     for f in range(0, FACTOR_WIDTH, 2):
-        first = dot_nn(stacked, jnp.concatenate([high[f], high[f + 1]], axis=1))
-        second = dot_nn(l_high, jnp.concatenate([low[f], low[f + 1]], axis=1))
+        first = dot_nn(stacked, jnp.concatenate([high[f, block], high[f + 1, block]], axis=1))
+        second = dot_nn(l_high, jnp.concatenate([low[f, block], low[f + 1, block]], axis=1))
         total[:, 128 * f : 128 * f + 256] += first[:128] + first[128:] + second
 
     @pl.when(step == pl.num_programs(0) - 1)
     def _():
         for f in range(FACTOR_WIDTH):
             block = total[:, 128 * f : 128 * f + 128].T
-            for d in range(4):
-                out[d, f] = block[32 * d : 32 * d + 32]
-
-
-def right_products(place, pair_grad, far_grad, inverse_count, weight, left):
+            for d, out in enumerate((out_0, out_1, out_2, out_3)):
+                out[f] = block[32 * d : 32 * d + 32]
+
+
+def right_products(place, pair_grad, far_grad, inverse_count, weight, left, left_far):
     block = ROWS * FACTOR_WIDTH
     steps = 64 // ROWS
     half = steps // 2
@@ -418,13 +504,14 @@
             pl.BlockSpec((ROWS, 4, 32, 128), lambda t, s: (jnp.maximum(t - half, 0), 0, 0, 0)),
             pl.BlockSpec((ROWS, 128), lambda t, s: (t, 0)),
             pl.BlockSpec((1024, 128), lambda t, s: (0, 0)),
-            pl.BlockSpec((block, 128), lambda t, s: (t, 0)),
+            pl.BlockSpec((block, 128), lambda t, s: (jnp.minimum(t, half - 1), 0)),
+            pl.BlockSpec((block, 128), lambda t, s: (jnp.maximum(t - half, 0), 0)),
         ],
         out_specs=[
             pl.BlockSpec((FACTOR_WIDTH, block, 128), lambda t, s: (0, t, 0)),
             pl.BlockSpec((FACTOR_WIDTH, block, 128), lambda t, s: (0, t, 0)),
-            pl.BlockSpec((4, FACTOR_WIDTH, 32, 128), lambda t, s: (0, 0, 0, 0)),
-        ],
+        ]
+        + [whole((FACTOR_WIDTH, 32, 128))] * 4,
         scratch_shapes=[
             pltpu.VMEM((1024, 384), jnp.bfloat16),
             pltpu.VMEM((128, 4096), jnp.float32),
@@ -434,55 +521,66 @@
         right_kernel,
         grid_spec=grid_spec,
         out_shape=[
-            jax.ShapeDtypeStruct((FACTOR_WIDTH, 64 * FACTOR_WIDTH, 128), jnp.bfloat16),
-            jax.ShapeDtypeStruct((FACTOR_WIDTH, 64 * FACTOR_WIDTH, 128), jnp.bfloat16),
-            jax.ShapeDtypeStruct((4, FACTOR_WIDTH, 32, 128), jnp.float32),
-        ],
+            pltpu.HBM((FACTOR_WIDTH, 64 * FACTOR_WIDTH, 128), jnp.bfloat16),
+            pltpu.HBM((FACTOR_WIDTH, 64 * FACTOR_WIDTH, 128), jnp.bfloat16),
+        ]
+        + [pltpu.HBM((FACTOR_WIDTH, 32, 128), jnp.float32)] * 4,
         compiler_params=pltpu.CompilerParams(vmem_limit_bytes=48 * 2**20),
-        cost_estimate=pl.CostEstimate(flops=16_000_000_000, bytes_accessed=42_000_000, transcendentals=0),
+        cost_estimate=pl.CostEstimate(flops=COST, bytes_accessed=COST, transcendentals=0),
         name="right_products",
-    )(place, pair_grad, far_grad, inverse_count, weight, left)
-
-
-def left_kernel(high, low, right_0, right_1, right_2, right_3, out, weights):
-    @pl.when(pl.program_id(0) == 0)
+    )(place, pair_grad, far_grad, *[pltpu.with_memory_space_constraint(part, pltpu.HBM) for part in (inverse_count, weight, left)], left_far)
+
+
+def left_kernel(high, low, right_0, right_1, right_2, right_3, own, far, weights):
+    step = pl.program_id(0)
+
+    @pl.when(step == 0)
     def _():
         for f in range(FACTOR_WIDTH):
             for d, right in enumerate((right_0, right_1, right_2, right_3)):
                 r_high, r_low = split(right[f])
-                row = (f % 2) * 128 + d * 32
-                weights[f // 2, row : row + 32, 0:128] = r_high
-                weights[f // 2, row : row + 32, 128:256] = r_low
-
+                row = f * 128 + d * 32
+                weights[row : row + 32, 0:128] = r_high
+                weights[row : row + 32, 128:256] = r_low
+
+    block = slice(None)
     first = jnp.zeros((ROWS * FACTOR_WIDTH, 256), jnp.float32)
     second = jnp.zeros((ROWS * FACTOR_WIDTH, 128), jnp.float32)
     for f in range(0, FACTOR_WIDTH, 2):
-        first += dot_nn(jnp.concatenate([high[f], high[f + 1]], axis=1), weights[f // 2])
-        second += dot_nn(jnp.concatenate([low[f], low[f + 1]], axis=1), weights[f // 2, :, 0:128])
-    out[...] = first[:, :128] + first[:, 128:] + second
+        part = slice(128 * f, 128 * f + 256)
+        first += dot_nn(jnp.concatenate([high[f, block], high[f + 1, block]], axis=1), weights[part])
+        second += dot_nn(jnp.concatenate([low[f, block], low[f + 1, block]], axis=1), weights[part, 0:128])
+    found = first[:, :128] + first[:, 128:] + second
+    half = pl.num_programs(0) // 2
+
+    @pl.when(step < half)
+    def _():
+        far[...] = found
+
+    @pl.when(step >= half)
+    def _():
+        own[...] = found
 
 
 def left_products(high, low, rights):
     block = ROWS * FACTOR_WIDTH
-    whole = pl.BlockSpec((FACTOR_WIDTH, 32, 128), lambda t: (0, 0, 0))
+    steps = 64 // ROWS
+    half = steps // 2
+    rows = pl.BlockSpec((FACTOR_WIDTH, block, 128), lambda t: (0, lax.rem(t + half, steps), 0))
     return pl.pallas_call(
         left_kernel,
-        grid=(64 // ROWS,),
-        in_specs=[
-            pl.BlockSpec((FACTOR_WIDTH, block, 128), lambda t: (0, t, 0)),
-            pl.BlockSpec((FACTOR_WIDTH, block, 128), lambda t: (0, t, 0)),
-            whole,
-            whole,
-            whole,
-            whole,
+        grid=(steps,),
+        in_specs=[rows, rows] + [whole((FACTOR_WIDTH, 32, 128))] * 4,
+        out_specs=[
+            pl.BlockSpec((block, 128), lambda t: (jnp.maximum(t - half, 0), 0)),
+            pl.BlockSpec((block, 128), lambda t: (jnp.minimum(t, half - 1), 0)),
         ],
-        out_specs=pl.BlockSpec((block, 128), lambda t: (t, 0)),
-        out_shape=jax.ShapeDtypeStruct((64 * FACTOR_WIDTH, 128), jnp.float32),
-        scratch_shapes=[pltpu.VMEM((FACTOR_WIDTH // 2, 256, 256), jnp.bfloat16)],
+        out_shape=[pltpu.HBM((32 * FACTOR_WIDTH, 128), jnp.float32)] * 2,
+        scratch_shapes=[pltpu.VMEM((FACTOR_WIDTH * 128, 256), jnp.bfloat16)],
         compiler_params=pltpu.CompilerParams(vmem_limit_bytes=40 * 2**20),
-        cost_estimate=pl.CostEstimate(flops=9_000_000_000, bytes_accessed=37_000_000, transcendentals=0),
+        cost_estimate=pl.CostEstimate(flops=COST, bytes_accessed=COST, transcendentals=0),
         name="left_products",
-    )(high, low, *rights)
+    )(high, low, pltpu.with_memory_space_constraint(rights[0], pltpu.HBM), *rights[1:])
 
 
 def swap_core(values):
@@ -517,57 +615,63 @@
 ):
     peers = lax.axis_size("seq")
     share = 64 // peers
-    counted, shared = -(-(17 + share) // 8) * 8, -(-(32 + share) // 8) * 8
+    counted = -(-(17 + share) // 8) * 8
+    block = RES * 8 // peers
+    shared = 24 + block + (0 if share == 2 else share)
     x, core = lax.axis_index("x"), lax.axis_index("core")
     place = jnp.stack([x, core]).astype(jnp.int32)
     mask_core = swap_core(alignment_mask)
     mask_chips = [fetch_chip(alignment_mask, d) for d in (1, 2, 3)]
-    pair_grad = pair_update_gradient.reshape(32, 4, 2, 32, 128)
-    far_grad = swap_core(lax.dynamic_index_in_dim(pair_grad, 1 - core, 2, keepdims=False))
     weight = pair_weight.reshape(FACTOR_WIDTH, FACTOR_WIDTH, 128).swapaxes(0, 1).reshape(1024, 128)
     value_gate = jnp.concatenate([content_matrix, sigmoid_filter_matrix], axis=1).T
     key_value = jnp.concatenate([key_weight, content_matrix], axis=1)
     factors = jnp.concatenate([first_factor_matrix, second_factor_matrix], axis=1)
 
     flat, heads, stat = (RES * 64, SEQ), (RES * 8, SEQ), (RES, SEQ)
-    m0t, x0t, inverse, present, send = call(
-        norm_kernel, [flat, flat, stat, stat, (peers, counted, 128)], homolog_features, alignment_mask
-    )
-    (send,) = call(pair_kernel, [(peers, counted, 128)], send, alignment_mask, mask_core, *mask_chips)
+    x0t, inverse, present, send = call(
+        norm_kernel, [flat, stat, stat, (peers, counted, 128)], homolog_features, alignment_mask
+    )
+    (send,) = call(pair_kernel, [(peers, counted, 128)], send, alignment_mask, mask_core, *mask_chips, free=(2, 3, 4, 5))
     got = exchange(send)
-    keys, values, gate, slope_t = call(
-        project_kernel, [heads, heads, flat, flat], x0t, homolog_loss_slope, key_weight.T, value_gate
-    )
+    keys, values, gate, m0t, slope_t = call(
+        project_kernel, [heads, heads, flat, flat, flat],
+        x0t, homolog_features, homolog_loss_slope, key_weight.T, value_gate, free=(3, 4),
+    )
+    slope_t, pair_grad = lax.optimization_barrier((slope_t, pair_update_gradient.reshape(32, 4, 2, 32, 128)))
+    far_grad = swap_core(lax.dynamic_index_in_dim(pair_grad, 1 - core, 2, keepdims=False))
+    got, far_grad, weight, place = lax.optimization_barrier((got, far_grad, weight, place))
     raw, local, counts, query_blocks, send = call(
-        score_kernel, [heads, stat, stat, (RES * 8, RES * 8), (peers, shared, 128)], got, keys, values, present, asking_matrix
+        score_kernel,
+        [heads, (RES, 16), stat, (RES * 8, RES * 8), (peers, shared, 128)],
+        got, keys, values, present, asking_matrix, free=(0,),
     )
     got = exchange(send)
-    probs, attended, mixed, x1t, inverse_mid, left, right, inverse_count = call(
+    probs, attended, mixed, x1t, inverse_mid, left, right, inverse_count, moments = call(
         attend_kernel,
-        [heads, (RES, 64), flat, flat, stat, (RES * 32, SEQ), (FACTOR_WIDTH, RES, SEQ), (64, 128)],
-        got, local, raw, m0t, gate, present, final_mixing_matrix.T, factors.T,
+        [heads, (RES, 64), flat, flat, stat, (RES * 32, SEQ), (FACTOR_WIDTH, RES, SEQ), (64, 128), (block, 128)],
+        got, local, raw, m0t, gate, present, final_mixing_matrix.T, factors.T, late=(3, 4), free=(0, 6, 7),
         scratch=[pltpu.VMEM((RES * 32, SEQ), F32)],
     )
-    left_rows = jnp.concatenate([left, swap_core(left)], axis=0)
     rights = [right] + [fetch_chip(right, d) for d in (1, 2, 3)]
-    high, low, right_parts = right_products(place, pair_grad, far_grad, inverse_count, weight, left_rows)
-    right_sent = [send_chip(right_parts[d], d) for d in (1, 2, 3)]
-    left_parts = left_products(high, low, rights)
-    half = RES * FACTOR_WIDTH
+    high, low, right_own, right_1, right_2, right_3 = right_products(
+        place, pair_grad, far_grad, inverse_count, weight, left, swap_core(left)
+    )
+    right_sent = [send_chip(part, d) for d, part in ((2, right_2), (1, right_1), (3, right_3))]
+    left_own, left_far = left_products(high, low, rights)
+    left_far = [swap_core(part) for part in jnp.split(left_far, 2)]
     mid, out_grad, send = call(
-        middle_kernel, [flat, flat, (peers, 16, 128)],
-        left_parts[:half], swap_core(left_parts[half:]), right_parts[0], *right_sent,
-        x1t, inverse_mid, present, slope_t, gate, factors, final_mixing_matrix,
+        middle_kernel, [flat, flat, (peers, 16 + block, 128)],
+        left_own, *left_far, right_own, *right_sent,
+        moments, x1t, inverse_mid, present, slope_t, gate, factors, final_mixing_matrix, free=(1, 2, 4, 5, 6, 13),
         scratch=[pltpu.VMEM((RES * 32, SEQ), F32)],
     )
     got = exchange(send)
     (gate_grad,) = call(gate_back_kernel, [flat], out_grad, mixed, gate, sigmoid_filter_matrix)
-    score_grad, grad_blocks, send = call(
-        score_back_kernel, [heads, (RES * 8, RES * 8), (peers, 16, 128)], got, attended, probs, keys, values
-    )
-    got = exchange(send)
-    (x_grad,) = call(key_back_kernel, [flat], score_grad, grad_blocks, query_blocks, probs, gate_grad, key_value)
-    (out,) = call(final_kernel, [(SEQ, RES * 64)], got, counts, asking_matrix, present, x0t, inverse, x_grad, mid)
+    (out,) = call(
+        finish_kernel, [(SEQ, RES * 64)],
+        got, attended, probs, keys, values, query_blocks, gate_grad, key_value, counts, asking_matrix,
+        present, x0t, inverse, mid, late=(6, 11, 13), free=(0, 7),
+    )
     return out
 
 

time: 198 us -> 172 us (0.87)
  local copies, waits for them, and re-layouts: 33.4 us -> 8.83 us
  Pallas kernels: 57.2 us -> 78.2 us
  blocking collectives: 16.6 us -> 0 us
  waiting for transfers between devices: 52.9 us -> 46.2 us
  starting transfers between devices: 32.6 us -> 36.1 us
    unnamed x95 -> x21, local copies, waits for them, and re-layouts: 27 us -> 3.23 us
    ppermute x3, waiting for transfers between devices: 22.3 us -> 0.01 us  [send_chip(): lax.ppermute(values, 'x', [(i, (i + distance) % 4) for i in range(4)])]
    pallas_call x12 -> x10, Pallas kernels: 57.2 us -> 78.2 us  [the longest x8 37.9 us: call(): pl.pallas_call(functools.partial(staged, kernel, (len(operands), len(shap...]
    all_to_all x1 -> x0, blocking collectives: 16.6 us -> none  [exchange(): return lax.all_to_all(send, 'seq', 0, 0, tiled=True)]
    all_to_all x3, waiting for transfers between devices: 27.3 us -> 40 us  [exchange(): return lax.all_to_all(send, 'seq', 0, 0, tiled=True)]
  transfers between devices with their start and end apart: 16 -> 17, of which waited for: 8 -> 8; matrix products, arithmetic and copies ran while one was open for 6% -> 2% of each run, Pallas kernels for 16% -> 27%
where the time goes in v2:
time: 172 us; the launch traced here: 171 us
  Pallas kernels  78.2 us (45%)
  waiting for transfers between devices  46.2 us (27%)
  starting transfers between devices  36.1 us (21%)
  local copies, waits for them, and re-layouts  8.83 us (5%)
    all_to_all x3, waiting for transfers between devices, exchange(): return lax.all_to_all(send, 'seq', 0, 0, tiled=True)  40 us
    pallas_call x8, Pallas kernels, call(): pl.pallas_call(functools.partial(staged, kernel, (len(operands), len(shap...  37.9 us
    pallas_call x1, Pallas kernels, right_products(): pl.pallas_call(right_kernel, grid_spec=grid_spec, out_shape=[pltpu.HBM((F...  23.2 us
    all_to_all x3, starting transfers between devices, exchange(): return lax.all_to_all(send, 'seq', 0, 0, tiled=True)  20.9 us
    pallas_call x1, Pallas kernels, left_products(): pl.pallas_call(left_kernel, grid=(steps,), in_specs=[rows, rows] + [whole...  17.1 us
    ppermute x6, starting transfers between devices, fetch_chip(): lax.ppermute(values, 'x', [((i + distance) % 4, i) for i in range(4)])  7.42 us
    ppermute x3, starting transfers between devices, send_chip(): lax.ppermute(values, 'x', [(i, (i + distance) % 4) for i in range(4)])  6.59 us
    ppermute x6, waiting for transfers between devices, fetch_chip(): lax.ppermute(values, 'x', [((i + distance) % 4, i) for i in range(4)])  4.95 us
  transfers between devices with their start and end apart: 17, of which 8 were waited for; matrix products, arithmetic and copies ran while one was open for 2% of the time, Pallas kernels for 27%

profile of v2, /device:TPU:32, one launch (start us, length us, event | category | flops | bytes accessed | tf_op | source)
XLA Modules:
  0.0 170.7 jit_solution(6293515814309014164)
XLA Ops:
  0.0 1.4 copy.27.refs_1_
  1.4 0.8 copy.33
  2.3 3.2 %norm_kernel.1 = (f32[2048,128]{1,0:T(8,128)}, f32[32,128]{1,0:T(8,128)}, f32[32,128]{1,0:T(8,128)}, f32[32,24,128]{2,1,0:T(8,128)}) custom-call(f32[128,2048]{1,0:T(8,128)} %refs_1_.3, s32[128,32]{1,0:T(8,128)} %copy.27.refs_1_), custom_call_target="tpu_custom_call" | custom-call | flops 100000000 | bytes 2539520 | tf_op jit(solution)/shard_map/norm_kernel/pallas_call | solution.py:422
  5.5 0.7 maximum_bitcast_fusion.refs_4_
  6.2 0.7 copy-done
  6.9 4.6 %project_kernel.1 = (f32[256,128]{1,0:T(8,128)}, f32[256,128]{1,0:T(8,128)}, f32[2048,128]{1,0:T(8,128)}, f32[2048,128]{1,0:T(8,128)}, f32[2048,128]{1,0:T(8,128)}) custom-call(f32[2048,128]{1,0:T(8,128)} %get-tuple-element.46.refs_0_.refs_11_, f32[128,2048]{1,0:T(8,128)} %refs_1_.3, f32[128,2048]{1,0:T(8,128)} %refs_2_.1, f32[8,64]{1,0:T(8,128)S(1)} %bitcast.16, ...), custom_call_target="tpu_custom_call" | custom-call | flops 100000000 | bytes 6574080 | tf_op jit(solution)/shard_map/project_kernel/pallas_call | solution.py:422
  11.5 0.0 copy-start.5
  11.5 0.0 copy-start.6
  11.5 0.0 copy-start.4
  11.5 3.2 %dynamic-slice_bitcast_fusion = f32[32,4,32,128]{3,2,1,0:T(8,128)} fusion(f32[32,4,2,32,128]{4,3,2,1,0:T(8,128)} %bitcast.17, s32[]{:T(128)S(6)} %select_n.4), kind=kLoop, calls=%fused_computation | loop fusion | bytes 4194308 | tf_op jit(solution)/shard_map/jit(dynamic_index_in_dim)/squeeze | solution.py:641
  14.7 0.0 collective-permute-start.4
  14.8 0.5 collective-permute-start
  15.3 2.8 %collective-permute-start.1 = (s32[128,32]{1,0:T(8,128)S(1)}, s32[128,32]{1,0:T(8,128)S(1)}, u32[]{:S(2)}, u32[]{:S(2)}) collective-permute-start(s32[128,32]{1,0:T(8,128)S(1)} %copy-done.2), channel_id=1, source_target_pairs={{2,0},{4,2},{6,4},{0,6},{3,1},{5,3},{7,5},{1,7},{10,8},{12,10},{14... | collective-permute-start | bytes 49160 | tf_op jit(solution)/shard_map/ppermute | solution.py:591
  18.0 0.8 collective-permute-start.2
  18.8 0.9 collective-permute-start.3
  19.7 0.0 collective-permute-done.refs_2_
  19.7 0.7 collective-permute-done.1.refs_3_
  20.4 3.6 %collective-permute-done.2.refs_4_ = s32[128,32]{1,0:T(8,128)S(1)} collective-permute-done((s32[128,32]{1,0:T(8,128)S(1)}, s32[128,32]{1,0:T(8,128)S(1)}, u32[]{:S(2)}, u32[]{:S(2)}) %collective-permute-start.2) | collective-permute-done | bytes 16416 | tf_op jit(solution)/shard_map/ppermute | solution.py:591
  24.0 0.7 collective-permute-done.3.refs_5_
  24.6 2.0 %pair_kernel.1 = f32[32,24,128]{2,1,0:T(8,128)} custom-call(f32[32,24,128]{2,1,0:T(8,128)} %get-tuple-element.45.refs_0_, s32[128,32]{1,0:T(8,128)} %copy.27.refs_1_, s32[128,32]{1,0:T(8,128)S(1)} %collective-permute-done.refs_2_, s32[128,32]{1,0:T(8,128)S(1)} %collective-permute-done.1.refs_3_, s32[128,32]{1,0:T(8,128)S(1)} %collective-permute-done.2.refs_4_, ...), custom_call_target="tpu_custom_call" | custom-call | flops 100000000 | bytes 868352 | tf_op jit(solution)/shard_map/pair_kernel/pallas_call | solution.py:422
  26.7 11.4 %all-to-all-start = ((f32[32,24,128]{2,1,0:T(8,128)}), f32[32,24,128]{2,1,0:T(8,128)S(1)}, u32[]{:S(2)}, u32[]{:S(2)}) async-start(f32[32,24,128]{2,1,0:T(8,128)} %pair_kernel.1), calls=%async_computation | async-start | bytes 786432 | tf_op jit(solution)/shard_map/all_to_all | solution.py:599
  38.1 0.0 copy-done.3
  38.1 1.1 copy.34
  39.2 0.1 pad_add_fusion.place
  39.3 12.8 %all-to-all-done.refs_0_ = f32[32,24,128]{2,1,0:T(8,128)S(1)} async-done(((f32[32,24,128]{2,1,0:T(8,128)}), f32[32,24,128]{2,1,0:T(8,128)S(1)}, u32[]{:S(2)}, u32[]{:S(2)}) %all-to-all-start) | async-done | bytes 393248 | tf_op jit(solution)/shard_map/all_to_all | solution.py:599
  52.1 0.0 collective-permute-done.4.far_g
  52.1 6.0 %score_kernel.1 = (f32[256,128]{1,0:T(8,128)}, f32[32,16]{1,0:T(8,128)}, f32[32,128]{1,0:T(8,128)}, f32[256,256]{1,0:T(8,128)}, f32[32,32,128]{2,1,0:T(8,128)}) custom-call(f32[32,24,128]{2,1,0:T(8,128)S(1)} %all-to-all-done.refs_0_, f32[256,128]{1,0:T(8,128)} %get-tuple-element.52.refs_1_.refs_3_, f32[256,128]{1,0:T(8,128)} %get-tuple-element.53.refs_2_.refs_4_, ...), custom_call_target="tpu_custom_call" | custom-call | flops 100000000 | bytes 1624064 | tf_op jit(solution)/shard_map/score_kernel/pallas_call | solution.py:422
  58.1 4.7 %all-to-all-start.1 = ((f32[32,32,128]{2,1,0:T(8,128)}), f32[32,32,128]{2,1,0:T(8,128)S(1)}, u32[]{:S(2)}, u32[]{:S(2)}) async-start(f32[32,32,128]{2,1,0:T(8,128)} %get-tuple-element.55), calls=%async_computation.1 | async-start | bytes 1048576 | tf_op jit(solution)/shard_map/all_to_all | solution.py:599
  62.7 0.1 copy.36
  62.8 0.1 copy.37
  62.9 0.1 fusion.1
  63.0 0.1 copy.38.refs_7_
  63.1 0.0 copy-done.4
  63.1 0.1 copy.35
  63.2 15.3 %all-to-all-done.1.refs_0_ = f32[32,32,128]{2,1,0:T(8,128)S(1)} async-done(((f32[32,32,128]{2,1,0:T(8,128)}), f32[32,32,128]{2,1,0:T(8,128)S(1)}, u32[]{:S(2)}, u32[]{:S(2)}) %all-to-all-start.1) | async-done | bytes 524320 | tf_op jit(solution)/shard_map/all_to_all | solution.py:599
  78.5 5.3 %attend_kernel.1 = (f32[256,128]{1,0:T(8,128)}, f32[32,64]{1,0:T(8,128)}, f32[2048,128]{1,0:T(8,128)}, f32[2048,128]{1,0:T(8,128)}, f32[32,128]{1,0:T(8,128)}, /...) custom-call(f32[32,32,128]{2,1,0:T(8,128)S(1)} %all-to-all-done.1.refs_0_, ...), custom_call_target="tpu_custom_call" | custom-call | flops 100000000 | bytes 6141952 | tf_op jit(solution)/shard_map/attend_kernel/pallas_call | solution.py:422
  83.8 0.1 collective-permute-start.5
  83.9 0.6 collective-permute-start.6
  84.5 1.0 collective-permute-start.7
  85.6 1.3 collective-permute-start.8
  86.9 0.0 collective-permute-done.5.left_far
  86.9 23.2 %right_products.1 = (bf16[32,2048,128]{2,1,0:T(8,128)(2,1)}, bf16[32,2048,128]{2,1,0:T(8,128)(2,1)}, f32[32,32,128]{2,1,0:T(8,128)}, f32[32,32,128]{2,1,0:T(8,12...) custom-call(s32[2]{0:T(128)S(1)} %pad_add_fusion.place, f32[32,4,2,32,128]{4,3,2,1,0:T(8,128)} %bitcast.18, ...), custom_call_target="tpu_custom_call" | custom-call | flops 1000 | bytes 1000 | tf_op jit(solution)/shard_map/right_products/pallas_call | solution.py:520
  110.1 3.4 %collective-permute-start.11 = (f32[32,32,128]{2,1,0:T(8,128)}, f32[32,32,128]{2,1,0:T(8,128)S(1)}, u32[]{:S(2)}, u32[]{:S(2)}) collective-permute-start(f32[32,32,128]{2,1,0:T(8,128)} %get-tuple-element.69), channel_id=1, source_target_pairs={{0,4},{2,6},{4,0},{6,2},{1,5},{3,7},{5,1},{7,3},{8,12},{10,14},{12... | collective-permute-start | bytes 1572872 | tf_op jit(solution)/shard_map/ppermute | solution.py:595
  113.5 0.0 collective-permute-start.12
  113.5 0.0 collective-permute-done.6.right_1
  113.5 3.2 %collective-permute-start.13 = (f32[32,32,128]{2,1,0:T(8,128)}, f32[32,32,128]{2,1,0:T(8,128)S(1)}, u32[]{:S(2)}, u32[]{:S(2)}) collective-permute-start(f32[32,32,128]{2,1,0:T(8,128)} %get-tuple-element.71), channel_id=1, source_target_pairs={{0,6},{2,0},{4,2},{6,4},{1,7},{3,1},{5,3},{7,5},{8,14},{10,8},{12,... | collective-permute-start | bytes 1572872 | tf_op jit(solution)/shard_map/ppermute | solution.py:595
  116.7 0.0 collective-permute-done.7.right_2
  116.7 0.0 collective-permute-done.8.right_3
  116.7 17.1 %left_products.1 = (f32[1024,128]{1,0:T(8,128)}, f32[1024,128]{1,0:T(8,128)}) custom-call(bf16[32,2048,128]{2,1,0:T(8,128)(2,1)} %get-tuple-element.63.high, bf16[32,2048,128]{2,1,0:T(8,128)(2,1)} %get-tuple-element.64.low, f32[32,32,128]{2,1,0:T(8,128)} %get-tuple-element.65.right_0, f32[32,32,128]{2,1,0:T(8,128)S(1)} %collective-permute-done.6.right_1, ...), custom_call_target="tpu_custom_call" | custom-call | flops 1000 | bytes 1000 | tf_op jit(solution)/shard_map/left_products/pallas_call | solution.py:570
  133.9 1.1 fusion
  135.0 0.1 collective-permute-start.10
  135.1 0.5 collective-permute-start.9
  135.6 0.1 pad_maximum_fusion.refs_13_
  135.6 0.9 collective-permute-done.10.refs_2_
  136.6 0.4 collective-permute-done.9.refs_1_
  136.9 0.0 collective-permute-done.11.refs_4_
  137.0 0.0 collective-permute-done.12.refs_5_
  137.0 0.0 collective-permute-done.13.refs_6_
  137.0 7.5 %middle_kernel.1 = (f32[2048,128]{1,0:T(8,128)}, f32[2048,128]{1,0:T(8,128)}, f32[32,24,128]{2,1,0:T(8,128)}) custom-call(f32[1024,128]{1,0:T(8,128)} %get-tuple-element.66.refs_0_, f32[512,128]{1,0:T(8,128)S(1)} %collective-permute-done.9.refs_1_, f32[512,128]{1,0:T(8,128)S(1)} %collective-permute-done.10.refs_2_, ...), custom_call_target="tpu_custom_call" | custom-call | flops 100000000 | bytes 8851456 | tf_op jit(solution)/shard_map/middle_kernel/pallas_call | solution.py:422
  144.5 4.9 %all-to-all-start.2 = ((f32[32,24,128]{2,1,0:T(8,128)}), f32[32,24,128]{2,1,0:T(8,128)S(1)}, u32[]{:S(2)}, u32[]{:S(2)}) async-start(f32[32,24,128]{2,1,0:T(8,128)} %get-tuple-element.76), calls=%async_computation.2 | async-start | bytes 786432 | tf_op jit(solution)/shard_map/all_to_all | solution.py:599
  149.4 0.1 copy.39.refs_7_
  149.5 3.3 %gate_back_kernel.1.refs_6_ = f32[2048,128]{1,0:T(8,128)} custom-call(f32[2048,128]{1,0:T(8,128)} %get-tuple-element.80.refs_0_, f32[2048,128]{1,0:T(8,128)} %get-tuple-element.81.refs_1_, f32[2048,128]{1,0:T(8,128)} %get-tuple-element.59.refs_4_.refs_12_.refs_2_, f32[64,64]{1,0:T(8,128)} %refs_3_.1), custom_call_target="tpu_custom_call" | custom-call | flops 100000000 | bytes 4210688 | tf_op jit(solution)/shard_map/gate_back_kernel/pallas_call | solution.py:422
  152.8 11.8 %all-to-all-done.2.refs_0_ = f32[32,24,128]{2,1,0:T(8,128)S(1)} async-done(((f32[32,24,128]{2,1,0:T(8,128)}), f32[32,24,128]{2,1,0:T(8,128)S(1)}, u32[]{:S(2)}, u32[]{:S(2)}) %all-to-all-start.2) | async-done | bytes 393248 | tf_op jit(solution)/shard_map/all_to_all | solution.py:599
  164.6 5.9 %finish_kernel.1 = f32[128,2048]{1,0:T(8,128)} custom-call(f32[32,24,128]{2,1,0:T(8,128)S(1)} %all-to-all-done.2.refs_0_, f32[32,64]{1,0:T(8,128)} %get-tuple-element.77.refs_1_, f32[256,128]{1,0:T(8,128)} %get-tuple-element.78.refs_2_, f32[256,128]{1,0:T(8,128)} %get-tuple-element.52.refs_1_.refs_3_, f32[256,128]{1,0:T(8,128)} %get-tuple-element.53.refs_2_.refs_4_, ...), custom_call_target="tpu_custom_call" | custom-call | flops 100000000 | bytes 5320704 | tf_op jit(solution)/shard_map/finish_kernel/pallas_call | solution.py:422
  (11 shorter events, 0.0 us)
Async XLA Ops:
  2.3 12.5 %copy-start.2 = (s32[128,32]{1,0:T(8,128)S(1)}, s32[128,32]{1,0:T(8,128)}, u32[]{:S(2)}) copy-start(s32[128,32]{1,0:T(8,128)} %copy.27.refs_1_) | copy-start | bytes 49156
  6.2 0.7 copy-start
  6.9 31.2 %copy-start.3 = (f32[1024,128]{1,0:T(8,128)S(1)}, f32[1024,128]{1,0:T(8,128)}, u32[]{:S(2)}) copy-start(f32[1024,128]{1,0:T(8,128)} %param.23) | copy-start | bytes 1572868
  11.5 51.3 %copy-start.5 = (f32[64,32]{0,1:T(8,128)S(1)}, f32[64,32]{0,1:T(8,128)}, u32[]{:S(2)}) copy-start(f32[64,32]{0,1:T(8,128)} %param.21) | copy-start | bytes 24580
  11.5 51.4 %copy-start.6 = (f32[64,32]{0,1:T(8,128)S(1)}, f32[64,32]{0,1:T(8,128)}, u32[]{:S(2)}) copy-start(f32[64,32]{0,1:T(8,128)} %param.22) | copy-start | bytes 24580
  11.5 51.6 %copy-start.4 = (f32[64,64]{1,0:T(8,128)S(1)}, f32[64,64]{1,0:T(8,128)}, u32[]{:S(2)}) copy-start(f32[64,64]{1,0:T(8,128)} %refs_14_.1) | copy-start | bytes 49156
  14.7 37.3 %collective-permute-start.4 = (f32[32,4,32,128]{3,2,1,0:T(8,128)}, f32[32,4,32,128]{3,2,1,0:T(8,128)S(1)}, u32[]{:S(2)}, u32[]{:S(2)}) collective-permute-start(f32[32,4,32,128]{3,2,1,0:T(8,128)} %dynamic-slice_bitcast_fusion), channel_id=1, source_target_pairs={{0,1},{1,0},{2,3},{3,2},{4,5},{5,4},{6,7},{7,6},{8,9},{9,8},{10,11... | collective-permute-start | bytes 6291464 | tf_op jit(solution)/shard_map/ppermute | solution.py:587
  14.8 5.0 %collective-permute-start = (s32[128,32]{1,0:T(8,128)S(1)}, s32[128,32]{1,0:T(8,128)S(1)}, u32[]{:S(2)}, u32[]{:S(2)}) collective-permute-start(s32[128,32]{1,0:T(8,128)S(1)} %copy-done.2), channel_id=1, source_target_pairs={{0,1},{1,0},{2,3},{3,2},{4,5},{5,4},{6,7},{7,6},{8,9},{9,8},{10,11... | collective-permute-start | bytes 49160 | tf_op jit(solution)/shard_map/ppermute | solution.py:587
  15.3 5.2 %collective-permute-start.1 = (s32[128,32]{1,0:T(8,128)S(1)}, s32[128,32]{1,0:T(8,128)S(1)}, u32[]{:S(2)}, u32[]{:S(2)}) collective-permute-start(s32[128,32]{1,0:T(8,128)S(1)} %copy-done.2), channel_id=1, source_target_pairs={{2,0},{4,2},{6,4},{0,6},{3,1},{5,3},{7,5},{1,7},{10,8},{12,10},{14... | collective-permute-start | bytes 49160 | tf_op jit(solution)/shard_map/ppermute | solution.py:591
  18.0 6.0 %collective-permute-start.2 = (s32[128,32]{1,0:T(8,128)S(1)}, s32[128,32]{1,0:T(8,128)S(1)}, u32[]{:S(2)}, u32[]{:S(2)}) collective-permute-start(s32[128,32]{1,0:T(8,128)S(1)} %copy-done.2), channel_id=1, source_target_pairs={{4,0},{6,2},{0,4},{2,6},{5,1},{7,3},{1,5},{3,7},{12,8},{14,10},{8,... | collective-permute-start | bytes 49160 | tf_op jit(solution)/shard_map/ppermute | solution.py:591
  18.8 5.8 %collective-permute-start.3 = (s32[128,32]{1,0:T(8,128)S(1)}, s32[128,32]{1,0:T(8,128)S(1)}, u32[]{:S(2)}, u32[]{:S(2)}) collective-permute-start(s32[128,32]{1,0:T(8,128)S(1)} %copy-done.2), channel_id=1, source_target_pairs={{6,0},{0,2},{2,4},{4,6},{7,1},{1,3},{3,5},{5,7},{14,8},{8,10},{10,... | collective-permute-start | bytes 49160 | tf_op jit(solution)/shard_map/ppermute | solution.py:591
  26.7 25.4 %all-to-all-start = ((f32[32,24,128]{2,1,0:T(8,128)}), f32[32,24,128]{2,1,0:T(8,128)S(1)}, u32[]{:S(2)}, u32[]{:S(2)}) async-start(f32[32,24,128]{2,1,0:T(8,128)} %pair_kernel.1), calls=%async_computation | async-start | bytes 786432 | tf_op jit(solution)/shard_map/all_to_all | solution.py:599
  58.1 20.4 %all-to-all-start.1 = ((f32[32,32,128]{2,1,0:T(8,128)}), f32[32,32,128]{2,1,0:T(8,128)S(1)}, u32[]{:S(2)}, u32[]{:S(2)}) async-start(f32[32,32,128]{2,1,0:T(8,128)} %get-tuple-element.55), calls=%async_computation.1 | async-start | bytes 1048576 | tf_op jit(solution)/shard_map/all_to_all | solution.py:599
  83.8 3.1 %collective-permute-start.5 = (f32[1024,128]{1,0:T(8,128)}, f32[1024,128]{1,0:T(8,128)S(1)}, u32[]{:S(2)}, u32[]{:S(2)}) collective-permute-start(f32[1024,128]{1,0:T(8,128)} %get-tuple-element.62.left), channel_id=1, source_target_pairs={{0,1},{1,0},{2,3},{3,2},{4,5},{5,4},{6,7},{7,6},{8,9},{9,8},{10,11... | collective-permute-start | bytes 1572872 | tf_op jit(solution)/shard_map/ppermute | solution.py:587
  83.9 29.6 %collective-permute-start.6 = (f32[32,32,128]{2,1,0:T(8,128)}, f32[32,32,128]{2,1,0:T(8,128)S(1)}, u32[]{:S(2)}, u32[]{:S(2)}) collective-permute-start(f32[32,32,128]{2,1,0:T(8,128)} %get-tuple-element.65.right_0), channel_id=1, source_target_pairs={{2,0},{4,2},{6,4},{0,6},{3,1},{5,3},{7,5},{1,7},{10,8},{12,10},{14... | collective-permute-start | bytes 1572872 | tf_op jit(solution)/shard_map/ppermute | solution.py:591
  84.5 32.2 %collective-permute-start.7 = (f32[32,32,128]{2,1,0:T(8,128)}, f32[32,32,128]{2,1,0:T(8,128)S(1)}, u32[]{:S(2)}, u32[]{:S(2)}) collective-permute-start(f32[32,32,128]{2,1,0:T(8,128)} %get-tuple-element.65.right_0), channel_id=1, source_target_pairs={{4,0},{6,2},{0,4},{2,6},{5,1},{7,3},{1,5},{3,7},{12,8},{14,10},{8,... | collective-permute-start | bytes 1572872 | tf_op jit(solution)/shard_map/ppermute | solution.py:591
  85.6 31.2 %collective-permute-start.8 = (f32[32,32,128]{2,1,0:T(8,128)}, f32[32,32,128]{2,1,0:T(8,128)S(1)}, u32[]{:S(2)}, u32[]{:S(2)}) collective-permute-start(f32[32,32,128]{2,1,0:T(8,128)} %get-tuple-element.65.right_0), channel_id=1, source_target_pairs={{6,0},{0,2},{2,4},{4,6},{7,1},{1,3},{3,5},{5,7},{14,8},{8,10},{10,... | collective-permute-start | bytes 1572872 | tf_op jit(solution)/shard_map/ppermute | solution.py:591
  110.1 26.8 %collective-permute-start.11 = (f32[32,32,128]{2,1,0:T(8,128)}, f32[32,32,128]{2,1,0:T(8,128)S(1)}, u32[]{:S(2)}, u32[]{:S(2)}) collective-permute-start(f32[32,32,128]{2,1,0:T(8,128)} %get-tuple-element.69), channel_id=1, source_target_pairs={{0,4},{2,6},{4,0},{6,2},{1,5},{3,7},{5,1},{7,3},{8,12},{10,14},{12... | collective-permute-start | bytes 1572872 | tf_op jit(solution)/shard_map/ppermute | solution.py:595
  113.5 23.5 %collective-permute-start.12 = (f32[32,32,128]{2,1,0:T(8,128)}, f32[32,32,128]{2,1,0:T(8,128)S(1)}, u32[]{:S(2)}, u32[]{:S(2)}) collective-permute-start(f32[32,32,128]{2,1,0:T(8,128)} %get-tuple-element.70), channel_id=1, source_target_pairs={{0,2},{2,4},{4,6},{6,0},{1,3},{3,5},{5,7},{7,1},{8,10},{10,12},{12... | collective-permute-start | bytes 1572872 | tf_op jit(solution)/shard_map/ppermute | solution.py:595
  113.5 23.5 %collective-permute-start.13 = (f32[32,32,128]{2,1,0:T(8,128)}, f32[32,32,128]{2,1,0:T(8,128)S(1)}, u32[]{:S(2)}, u32[]{:S(2)}) collective-permute-start(f32[32,32,128]{2,1,0:T(8,128)} %get-tuple-element.71), channel_id=1, source_target_pairs={{0,6},{2,0},{4,2},{6,4},{1,7},{3,1},{5,3},{7,5},{8,14},{10,8},{12,... | collective-permute-start | bytes 1572872 | tf_op jit(solution)/shard_map/ppermute | solution.py:595
  133.9 15.5 %copy-start.1 = (f32[64,8]{0,1:T(8,128)S(1)}, f32[64,8]{0,1:T(8,128)}, u32[]{:S(2)}) copy-start(f32[64,8]{0,1:T(8,128)} %param.17) | copy-start | bytes 6148
  133.9 15.5 %copy-start.7 = (f32[64,8]{0,1:T(8,128)S(1)}, f32[64,8]{0,1:T(8,128)}, u32[]{:S(2)}) copy-start(f32[64,8]{0,1:T(8,128)} %param.18) | copy-start | bytes 6148
  135.0 1.6 collective-permute-start.10
  135.1 1.9 %collective-permute-start.9 = (f32[512,128]{1,0:T(8,128)S(1)}, f32[512,128]{1,0:T(8,128)S(1)}, u32[]{:S(2)}, u32[]{:S(2)}) collective-permute-start(f32[512,128]{1,0:T(8,128)S(1)} %get-tuple-element.86), channel_id=1, source_target_pairs={{0,1},{1,0},{2,3},{3,2},{4,5},{5,4},{6,7},{7,6},{8,9},{9,8},{10,11... | collective-permute-start | bytes 786440 | tf_op jit(solution)/shard_map/ppermute | solution.py:587
  144.5 20.2 %all-to-all-start.2 = ((f32[32,24,128]{2,1,0:T(8,128)}), f32[32,24,128]{2,1,0:T(8,128)S(1)}, u32[]{:S(2)}, u32[]{:S(2)}) async-start(f32[32,24,128]{2,1,0:T(8,128)} %get-tuple-element.76), calls=%async_computation.2 | async-start | bytes 786432 | tf_op jit(solution)/shard_map/all_to_all | solution.py:599

commit v3 on v2

--- a/solution.py
+++ b/solution.py
@@ -459,17 +459,16 @@
         total[...] = jnp.zeros_like(total)
 
     near = step < pl.num_programs(0) // 2
+    inverse_column = inverse_count[...].T
     for pair in range(ROWS // 2):
         blocks = []
         for row in (2 * pair, 2 * pair + 1):
             for d in range(4):
                 chip = lax.rem(x + d, 4)
-                blocks.append(jnp.where(near, own_g[row, chip, 0], far_g[row, chip]))
+                scale = inverse_column[32 * d : 32 * d + 32, row : row + 1]
+                blocks.append(scale * jnp.where(near, own_g[row, chip, 0], far_g[row, chip, 0]))
         g_high, g_low = split(jnp.concatenate(blocks, axis=0))
         grads = dot_nt(weights[...], jnp.concatenate([g_high, g_high, g_low], axis=1))
-        grads = grads * jnp.concatenate(
-            [inverse_count[2 * pair : 2 * pair + 1], inverse_count[2 * pair + 1 : 2 * pair + 2]], axis=1
-        )
         grads_high, grads_low = split(grads)
         for k in range(2):
             row = (2 * pair + k) * FACTOR_WIDTH
@@ -501,7 +500,7 @@
         grid=(steps,),
         in_specs=[
             pl.BlockSpec((ROWS, 4, 1, 32, 128), lambda t, s: (jnp.minimum(t, half - 1), 0, s[1], 0, 0)),
-            pl.BlockSpec((ROWS, 4, 32, 128), lambda t, s: (jnp.maximum(t - half, 0), 0, 0, 0)),
+            pl.BlockSpec((ROWS, 4, 1, 32, 128), lambda t, s: (jnp.maximum(t - half, 0), 0, s[1], 0, 0)),
             pl.BlockSpec((ROWS, 128), lambda t, s: (t, 0)),
             pl.BlockSpec((1024, 128), lambda t, s: (0, 0)),
             pl.BlockSpec((block, 128), lambda t, s: (jnp.minimum(t, half - 1), 0)),
@@ -531,7 +530,7 @@
     )(place, pair_grad, far_grad, *[pltpu.with_memory_space_constraint(part, pltpu.HBM) for part in (inverse_count, weight, left)], left_far)
 
 
-def left_kernel(high, low, right_0, right_1, right_2, right_3, own, far, weights):
+def left_kernel(high, low, right_0, right_1, right_2, right_3, own, far_0, far_1, weights):
     step = pl.program_id(0)
 
     @pl.when(step == 0)
@@ -553,9 +552,13 @@
     found = first[:, :128] + first[:, 128:] + second
     half = pl.num_programs(0) // 2
 
-    @pl.when(step < half)
+    @pl.when(step < half // 2)
     def _():
-        far[...] = found
+        far_0[...] = found
+
+    @pl.when((step >= half // 2) & (step < half))
+    def _():
+        far_1[...] = found
 
     @pl.when(step >= half)
     def _():
@@ -573,9 +576,11 @@
         in_specs=[rows, rows] + [whole((FACTOR_WIDTH, 32, 128))] * 4,
         out_specs=[
             pl.BlockSpec((block, 128), lambda t: (jnp.maximum(t - half, 0), 0)),
-            pl.BlockSpec((block, 128), lambda t: (jnp.minimum(t, half - 1), 0)),
+            pl.BlockSpec((block, 128), lambda t: (jnp.minimum(t, half // 2 - 1), 0)),
+            pl.BlockSpec((block, 128), lambda t: (jnp.clip(t - half // 2, 0, half // 2 - 1), 0)),
         ],
-        out_shape=[pltpu.HBM((32 * FACTOR_WIDTH, 128), jnp.float32)] * 2,
+        out_shape=[pltpu.HBM((32 * FACTOR_WIDTH, 128), jnp.float32)]
+        + [pltpu.HBM((16 * FACTOR_WIDTH, 128), jnp.float32)] * 2,
         scratch_shapes=[pltpu.VMEM((FACTOR_WIDTH * 128, 256), jnp.bfloat16)],
         compiler_params=pltpu.CompilerParams(vmem_limit_bytes=40 * 2**20),
         cost_estimate=pl.CostEstimate(flops=COST, bytes_accessed=COST, transcendentals=0),
@@ -632,13 +637,14 @@
         norm_kernel, [flat, stat, stat, (peers, counted, 128)], homolog_features, alignment_mask
     )
     (send,) = call(pair_kernel, [(peers, counted, 128)], send, alignment_mask, mask_core, *mask_chips, free=(2, 3, 4, 5))
+    x0t, send, pair_grad = lax.optimization_barrier((x0t, send, pair_update_gradient))
+    far_grad = swap_core(pair_grad).reshape(32, 4, 2, 32, 128)
+    pair_grad = pair_grad.reshape(32, 4, 2, 32, 128)
     got = exchange(send)
     keys, values, gate, m0t, slope_t = call(
         project_kernel, [heads, heads, flat, flat, flat],
         x0t, homolog_features, homolog_loss_slope, key_weight.T, value_gate, free=(3, 4),
     )
-    slope_t, pair_grad = lax.optimization_barrier((slope_t, pair_update_gradient.reshape(32, 4, 2, 32, 128)))
-    far_grad = swap_core(lax.dynamic_index_in_dim(pair_grad, 1 - core, 2, keepdims=False))
     got, far_grad, weight, place = lax.optimization_barrier((got, far_grad, weight, place))
     raw, local, counts, query_blocks, send = call(
         score_kernel,
@@ -657,8 +663,8 @@
         place, pair_grad, far_grad, inverse_count, weight, left, swap_core(left)
     )
     right_sent = [send_chip(part, d) for d, part in ((2, right_2), (1, right_1), (3, right_3))]
-    left_own, left_far = left_products(high, low, rights)
-    left_far = [swap_core(part) for part in jnp.split(left_far, 2)]
+    left_own, *left_far = left_products(high, low, rights)
+    left_far = [swap_core(part) for part in left_far]
     mid, out_grad, send = call(
         middle_kernel, [flat, flat, (peers, 16 + block, 128)],
         left_own, *left_far, right_own, *right_sent,

time: 172 us -> 165 us (0.959)
  waiting for transfers between devices: 46.2 us -> 37.5 us
    all_to_all x3, waiting for transfers between devices: 40 us -> 33.2 us  [exchange(): return lax.all_to_all(send, 'seq', 0, 0, tiled=True)]
    unnamed x21 -> x15, local copies, waits for them, and re-layouts: 3.23 us -> 6.98 us
    squeeze x1 -> x0, local copies, waits for them, and re-layouts: 3.24 us -> none  [body(): lax.dynamic_index_in_dim(pair_grad, 1 - core, 2, keepdims=False)]
    ppermute x6, waiting for transfers between devices: 4.95 us -> 2.2 us  [fetch_chip(): lax.ppermute(values, 'x', [((i + distance) % 4, i) for i in range(4)])]
  transfers between devices with their start and end apart: 17 -> 17, of which waited for: 8 -> 8; matrix products, arithmetic and copies ran while one was open for 2% -> 4% of each run, Pallas kernels for 27% -> 32%
where the time goes in v3:
time: 165 us; the launch traced here: 164 us
  Pallas kernels  79.8 us (48%)
  waiting for transfers between devices  37.5 us (23%)
  starting transfers between devices  36.1 us (22%)
  local copies, waits for them, and re-layouts  9.29 us (6%)
    pallas_call x8, Pallas kernels, call(): pl.pallas_call(functools.partial(staged, kernel, (len(operands), len(shap...  37.9 us
    all_to_all x3, waiting for transfers between devices, exchange(): return lax.all_to_all(send, 'seq', 0, 0, tiled=True)  33.2 us
    pallas_call x1, Pallas kernels, right_products(): pl.pallas_call(right_kernel, grid_spec=grid_spec, out_shape=[pltpu.HBM((F...  24.7 us
    all_to_all x3, starting transfers between devices, exchange(): return lax.all_to_all(send, 'seq', 0, 0, tiled=True)  21 us
    pallas_call x1, Pallas kernels, left_products(): pl.pallas_call(left_kernel, grid=(steps,), in_specs=[rows, rows] + [whole...  17.2 us
    ppermute x3, starting transfers between devices, send_chip(): lax.ppermute(values, 'x', [(i, (i + distance) % 4) for i in range(4)])  7.1 us
    ppermute x6, starting transfers between devices, fetch_chip(): lax.ppermute(values, 'x', [((i + distance) % 4, i) for i in range(4)])  6.98 us
    unnamed x15, local copies, waits for them, and re-layouts  6.98 us
  transfers between devices with their start and end apart: 17, of which 8 were waited for; matrix products, arithmetic and copies ran while one was open for 4% of the time, Pallas kernels for 32%

profile of v3, /device:TPU:32, one launch (start us, length us, event | category | flops | bytes accessed | tf_op | source)
XLA Modules:
  0.0 163.9 jit_solution(5423917240920318543)
XLA Ops:
  0.0 0.8 copy.27.refs_1_
  0.8 0.0 copy-start.3
  0.8 0.1 collective-permute-start
  0.9 2.8 %collective-permute-start.1 = (s32[128,32]{1,0:T(8,128)S(1)}, s32[128,32]{1,0:T(8,128)S(1)}, u32[]{:S(2)}, u32[]{:S(2)}) collective-permute-start(s32[128,32]{1,0:T(8,128)S(1)} %copy.27.refs_1_), channel_id=1, source_target_pairs={{2,0},{4,2},{6,4},{0,6},{3,1},{5,3},{7,5},{1,7},{10,8},{12,10},{14... | collective-permute-start | bytes 49160 | tf_op jit(solution)/shard_map/ppermute | solution.py:596
  3.8 0.8 collective-permute-start.2
  4.6 0.9 collective-permute-start.3
  5.4 0.0 copy-done.3
  5.4 3.1 %norm_kernel.1 = (f32[2048,128]{1,0:T(8,128)}, f32[32,128]{1,0:T(8,128)}, f32[32,128]{1,0:T(8,128)}, f32[32,24,128]{2,1,0:T(8,128)}) custom-call(f32[128,2048]{1,0:T(8,128)} %refs_1_.3, s32[128,32]{1,0:T(8,128)} %copy-done.3), custom_call_target="tpu_custom_call" | custom-call | flops 100000000 | bytes 2539520 | tf_op jit(solution)/shard_map/norm_kernel/pallas_call | solution.py:422
  8.6 0.0 collective-permute-done.refs_2_
  8.6 0.0 collective-permute-done.1.refs_3_
  8.6 1.5 collective-permute-done.2.refs_4_
  10.1 0.7 collective-permute-done.3.refs_5_
  10.8 2.1 %pair_kernel.1 = f32[32,24,128]{2,1,0:T(8,128)} custom-call(f32[32,24,128]{2,1,0:T(8,128)} %get-tuple-element.48.refs_0_, s32[128,32]{1,0:T(8,128)} %copy-done.3, s32[128,32]{1,0:T(8,128)S(1)} %collective-permute-done.refs_2_, s32[128,32]{1,0:T(8,128)S(1)} %collective-permute-done.1.refs_3_, s32[128,32]{1,0:T(8,128)S(1)} %collective-permute-done.2.refs_4_, ...), custom_call_target="tpu_custom_call" | custom-call | flops 100000000 | bytes 868352 | tf_op jit(solution)/shard_map/pair_kernel/pallas_call | solution.py:422
  12.9 0.1 collective-permute-start.4
  13.0 11.4 %all-to-all-start = ((f32[32,24,128]{2,1,0:T(8,128)}), f32[32,24,128]{2,1,0:T(8,128)S(1)}, u32[]{:S(2)}, u32[]{:S(2)}) async-start(f32[32,24,128]{2,1,0:T(8,128)} %pair_kernel.1), calls=%async_computation | async-start | bytes 786432 | tf_op jit(solution)/shard_map/all_to_all | solution.py:604
  24.4 2.2 %copy.33 = f32[32,32,128]{2,0,1:T(8,128)} copy(f32[32,32,128]{2,1,0:T(8,128)} %bitcast.18) | data formatting | bytes 1048576 | tf_op jit(solution)/shard_map/reshape | solution.py:630
  26.5 0.8 copy.34
  27.4 0.1 pad_add_fusion.place
  27.4 0.7 maximum_bitcast_fusion.refs_4_
  28.1 0.0 copy-start.1
  28.1 0.7 copy-done.1
  28.8 4.5 %project_kernel.1 = (f32[256,128]{1,0:T(8,128)}, f32[256,128]{1,0:T(8,128)}, f32[2048,128]{1,0:T(8,128)}, f32[2048,128]{1,0:T(8,128)}, f32[2048,128]{1,0:T(8,128)}) custom-call(f32[2048,128]{1,0:T(8,128)} %get-tuple-element.54.refs_0_.refs_11_, f32[128,2048]{1,0:T(8,128)} %refs_1_.3, f32[128,2048]{1,0:T(8,128)} %refs_2_.1, f32[8,64]{1,0:T(8,128)S(1)} %bitcast.16, ...), custom_call_target="tpu_custom_call" | custom-call | flops 100000000 | bytes 6574080 | tf_op jit(solution)/shard_map/project_kernel/pallas_call | solution.py:422
  33.4 6.5 %all-to-all-done.refs_0_ = f32[32,24,128]{2,1,0:T(8,128)S(1)} async-done(((f32[32,24,128]{2,1,0:T(8,128)}), f32[32,24,128]{2,1,0:T(8,128)S(1)}, u32[]{:S(2)}, u32[]{:S(2)}) %all-to-all-start) | async-done | bytes 393248 | tf_op jit(solution)/shard_map/all_to_all | solution.py:604
  39.9 0.0 collective-permute-done.4
  39.9 6.0 %score_kernel.1 = (f32[256,128]{1,0:T(8,128)}, f32[32,16]{1,0:T(8,128)}, f32[32,128]{1,0:T(8,128)}, f32[256,256]{1,0:T(8,128)}, f32[32,32,128]{2,1,0:T(8,128)}) custom-call(f32[32,24,128]{2,1,0:T(8,128)S(1)} %all-to-all-done.refs_0_, f32[256,128]{1,0:T(8,128)} %get-tuple-element.55.refs_1_.refs_3_, f32[256,128]{1,0:T(8,128)} %get-tuple-element.56.refs_2_.refs_4_, ...), custom_call_target="tpu_custom_call" | custom-call | flops 100000000 | bytes 1624064 | tf_op jit(solution)/shard_map/score_kernel/pallas_call | solution.py:422
  45.9 4.8 %all-to-all-start.1 = ((f32[32,32,128]{2,1,0:T(8,128)}), f32[32,32,128]{2,1,0:T(8,128)S(1)}, u32[]{:S(2)}, u32[]{:S(2)}) async-start(f32[32,32,128]{2,1,0:T(8,128)} %get-tuple-element.58), calls=%async_computation.1 | async-start | bytes 1048576 | tf_op jit(solution)/shard_map/all_to_all | solution.py:604
  50.7 0.8 copy.36
  51.5 0.8 copy.37
  52.3 0.1 fusion
  52.4 0.1 copy.38.refs_7_
  52.5 0.8 copy.35
  53.3 14.9 %all-to-all-done.1.refs_0_ = f32[32,32,128]{2,1,0:T(8,128)S(1)} async-done(((f32[32,32,128]{2,1,0:T(8,128)}), f32[32,32,128]{2,1,0:T(8,128)S(1)}, u32[]{:S(2)}, u32[]{:S(2)}) %all-to-all-start.1) | async-done | bytes 524320 | tf_op jit(solution)/shard_map/all_to_all | solution.py:604
  68.3 5.4 %attend_kernel.1 = (f32[256,128]{1,0:T(8,128)}, f32[32,64]{1,0:T(8,128)}, f32[2048,128]{1,0:T(8,128)}, f32[2048,128]{1,0:T(8,128)}, f32[32,128]{1,0:T(8,128)}, /...) custom-call(f32[32,32,128]{2,1,0:T(8,128)S(1)} %all-to-all-done.1.refs_0_, ...), custom_call_target="tpu_custom_call" | custom-call | flops 100000000 | bytes 6141952 | tf_op jit(solution)/shard_map/attend_kernel/pallas_call | solution.py:422
  73.6 0.3 collective-permute-start.5
  73.9 0.6 collective-permute-start.6
  74.6 1.1 collective-permute-start.7
  75.7 0.7 collective-permute-start.8
  76.4 0.0 collective-permute-done.5.left_far
  76.4 2.2 %copy-done = f32[32,256,128]{2,1,0:T(8,128)S(1)} copy-done((f32[32,256,128]{2,1,0:T(8,128)S(1)}, f32[32,256,128]{2,1,0:T(8,128)}, u32[]{:S(2)}) %copy-start) | copy-done | bytes 4194328
  78.6 24.7 %right_products.1 = (bf16[32,2048,128]{2,1,0:T(8,128)(2,1)}, bf16[32,2048,128]{2,1,0:T(8,128)(2,1)}, f32[32,32,128]{2,1,0:T(8,128)}, f32[32,32,128]{2,1,0:T(8,12...) custom-call(s32[2]{0:T(128)S(1)} %pad_add_fusion.place, f32[32,4,2,32,128]{4,3,2,1,0:T(8,128)S(1)} %bitcast.14, ...), custom_call_target="tpu_custom_call" | custom-call | flops 1000 | bytes 1000 | tf_op jit(solution)/shard_map/right_products/pallas_call | solution.py:519
  103.3 3.9 %collective-permute-start.11 = (f32[32,32,128]{2,1,0:T(8,128)}, f32[32,32,128]{2,1,0:T(8,128)S(1)}, u32[]{:S(2)}, u32[]{:S(2)}) collective-permute-start(f32[32,32,128]{2,1,0:T(8,128)} %get-tuple-element.73), channel_id=1, source_target_pairs={{0,4},{2,6},{4,0},{6,2},{1,5},{3,7},{5,1},{7,3},{8,12},{10,14},{12... | collective-permute-start | bytes 1572872 | tf_op jit(solution)/shard_map/ppermute | solution.py:600
  107.1 0.0 collective-permute-start.12
  107.1 0.0 collective-permute-done.6.right_1
  107.1 3.2 %collective-permute-start.13 = (f32[32,32,128]{2,1,0:T(8,128)}, f32[32,32,128]{2,1,0:T(8,128)S(1)}, u32[]{:S(2)}, u32[]{:S(2)}) collective-permute-start(f32[32,32,128]{2,1,0:T(8,128)} %get-tuple-element.75), channel_id=1, source_target_pairs={{0,6},{2,0},{4,2},{6,4},{1,7},{3,1},{5,3},{7,5},{8,14},{10,8},{12,... | collective-permute-start | bytes 1572872 | tf_op jit(solution)/shard_map/ppermute | solution.py:600
  110.4 0.0 collective-permute-done.7.right_2
  110.4 0.0 collective-permute-done.8.right_3
  110.4 0.0 copy-start.4
  110.4 17.2 %left_products.1 = (f32[1024,128]{1,0:T(8,128)}, f32[512,128]{1,0:T(8,128)}, f32[512,128]{1,0:T(8,128)}) custom-call(bf16[32,2048,128]{2,1,0:T(8,128)(2,1)} %get-tuple-element.66.high, bf16[32,2048,128]{2,1,0:T(8,128)(2,1)} %get-tuple-element.67.low, f32[32,32,128]{2,1,0:T(8,128)} %get-tuple-element.68.right_0, ...), custom_call_target="tpu_custom_call" | custom-call | flops 1000 | bytes 1000 | tf_op jit(solution)/shard_map/left_products/pallas_call | solution.py:573
  127.6 0.0 collective-permute-start.10
  127.6 0.5 collective-permute-start.9
  128.1 0.1 pad_maximum_fusion.refs_13_
  128.2 1.2 collective-permute-done.10.refs_2_
  129.4 0.4 collective-permute-done.9.refs_1_
  129.7 0.0 collective-permute-done.11.refs_4_
  129.7 0.5 collective-permute-done.12.refs_5_
  130.3 0.0 collective-permute-done.13.refs_6_
  130.3 7.5 %middle_kernel.1 = (f32[2048,128]{1,0:T(8,128)}, f32[2048,128]{1,0:T(8,128)}, f32[32,24,128]{2,1,0:T(8,128)}) custom-call(f32[1024,128]{1,0:T(8,128)} %get-tuple-element.69.refs_0_, f32[512,128]{1,0:T(8,128)S(1)} %collective-permute-done.9.refs_1_, f32[512,128]{1,0:T(8,128)S(1)} %collective-permute-done.10.refs_2_, ...), custom_call_target="tpu_custom_call" | custom-call | flops 100000000 | bytes 8851456 | tf_op jit(solution)/shard_map/middle_kernel/pallas_call | solution.py:422
  137.7 4.9 %all-to-all-start.2 = ((f32[32,24,128]{2,1,0:T(8,128)}), f32[32,24,128]{2,1,0:T(8,128)S(1)}, u32[]{:S(2)}, u32[]{:S(2)}) async-start(f32[32,24,128]{2,1,0:T(8,128)} %get-tuple-element.80), calls=%async_computation.2 | async-start | bytes 786432 | tf_op jit(solution)/shard_map/all_to_all | solution.py:604
  142.6 0.0 copy-done.2
  142.6 0.0 copy-done.4
  142.6 0.1 copy.39.refs_7_
  142.7 3.3 %gate_back_kernel.1.refs_6_ = f32[2048,128]{1,0:T(8,128)} custom-call(f32[2048,128]{1,0:T(8,128)} %get-tuple-element.84.refs_0_, f32[2048,128]{1,0:T(8,128)} %get-tuple-element.85.refs_1_, f32[2048,128]{1,0:T(8,128)} %get-tuple-element.62.refs_4_.refs_12_.refs_2_, f32[64,64]{1,0:T(8,128)} %refs_3_.1), custom_call_target="tpu_custom_call" | custom-call | flops 100000000 | bytes 4210688 | tf_op jit(solution)/shard_map/gate_back_kernel/pallas_call | solution.py:422
  146.1 11.7 %all-to-all-done.2.refs_0_ = f32[32,24,128]{2,1,0:T(8,128)S(1)} async-done(((f32[32,24,128]{2,1,0:T(8,128)}), f32[32,24,128]{2,1,0:T(8,128)S(1)}, u32[]{:S(2)}, u32[]{:S(2)}) %all-to-all-start.2) | async-done | bytes 393248 | tf_op jit(solution)/shard_map/all_to_all | solution.py:604
  157.8 5.9 %finish_kernel.1 = f32[128,2048]{1,0:T(8,128)} custom-call(f32[32,24,128]{2,1,0:T(8,128)S(1)} %all-to-all-done.2.refs_0_, f32[32,64]{1,0:T(8,128)} %get-tuple-element.81.refs_1_, f32[256,128]{1,0:T(8,128)} %get-tuple-element.82.refs_2_, f32[256,128]{1,0:T(8,128)} %get-tuple-element.55.refs_1_.refs_3_, f32[256,128]{1,0:T(8,128)} %get-tuple-element.56.refs_2_.refs_4_, ...), custom_call_target="tpu_custom_call" | custom-call | flops 100000000 | bytes 5320704 | tf_op jit(solution)/shard_map/finish_kernel/pallas_call | solution.py:422
  (3 shorter events, 0.0 us)
Async XLA Ops:
  0.8 4.6 %copy-start.3 = (s32[128,32]{1,0:T(8,128)}, s32[128,32]{1,0:T(8,128)S(1)}, u32[]{:S(2)}) copy-start(s32[128,32]{1,0:T(8,128)S(1)} %copy.27.refs_1_) | copy-start | bytes 49156
  0.8 7.8 %collective-permute-start = (s32[128,32]{1,0:T(8,128)S(1)}, s32[128,32]{1,0:T(8,128)S(1)}, u32[]{:S(2)}, u32[]{:S(2)}) collective-permute-start(s32[128,32]{1,0:T(8,128)S(1)} %copy.27.refs_1_), channel_id=1, source_target_pairs={{0,1},{1,0},{2,3},{3,2},{4,5},{5,4},{6,7},{7,6},{8,9},{9,8},{10,11... | collective-permute-start | bytes 49160 | tf_op jit(solution)/shard_map/ppermute | solution.py:592
  0.9 7.7 %collective-permute-start.1 = (s32[128,32]{1,0:T(8,128)S(1)}, s32[128,32]{1,0:T(8,128)S(1)}, u32[]{:S(2)}, u32[]{:S(2)}) collective-permute-start(s32[128,32]{1,0:T(8,128)S(1)} %copy.27.refs_1_), channel_id=1, source_target_pairs={{2,0},{4,2},{6,4},{0,6},{3,1},{5,3},{7,5},{1,7},{10,8},{12,10},{14... | collective-permute-start | bytes 49160 | tf_op jit(solution)/shard_map/ppermute | solution.py:596
  3.8 6.4 %collective-permute-start.2 = (s32[128,32]{1,0:T(8,128)S(1)}, s32[128,32]{1,0:T(8,128)S(1)}, u32[]{:S(2)}, u32[]{:S(2)}) collective-permute-start(s32[128,32]{1,0:T(8,128)S(1)} %copy.27.refs_1_), channel_id=1, source_target_pairs={{4,0},{6,2},{0,4},{2,6},{5,1},{7,3},{1,5},{3,7},{12,8},{14,10},{8,... | collective-permute-start | bytes 49160 | tf_op jit(solution)/shard_map/ppermute | solution.py:596
  4.6 6.3 %collective-permute-start.3 = (s32[128,32]{1,0:T(8,128)S(1)}, s32[128,32]{1,0:T(8,128)S(1)}, u32[]{:S(2)}, u32[]{:S(2)}) collective-permute-start(s32[128,32]{1,0:T(8,128)S(1)} %copy.27.refs_1_), channel_id=1, source_target_pairs={{6,0},{0,2},{2,4},{4,6},{7,1},{1,3},{3,5},{5,7},{14,8},{8,10},{10,... | collective-permute-start | bytes 49160 | tf_op jit(solution)/shard_map/ppermute | solution.py:596
  12.9 27.0 %collective-permute-start.4 = (f32[32,256,128]{2,1,0:T(8,128)}, f32[32,256,128]{2,1,0:T(8,128)}, u32[]{:S(2)}, u32[]{:S(2)}) collective-permute-start(f32[32,256,128]{2,1,0:T(8,128)} %param.14), channel_id=1, source_target_pairs={{0,1},{1,0},{2,3},{3,2},{4,5},{5,4},{6,7},{7,6},{8,9},{9,8},{10,11... | collective-permute-start | bytes 12582920 | tf_op jit(solution)/shard_map/ppermute | solution.py:592
  13.0 26.9 %all-to-all-start = ((f32[32,24,128]{2,1,0:T(8,128)}), f32[32,24,128]{2,1,0:T(8,128)S(1)}, u32[]{:S(2)}, u32[]{:S(2)}) async-start(f32[32,24,128]{2,1,0:T(8,128)} %pair_kernel.1), calls=%async_computation | async-start | bytes 786432 | tf_op jit(solution)/shard_map/all_to_all | solution.py:604
  28.1 0.7 copy-start.1
  45.9 22.3 %all-to-all-start.1 = ((f32[32,32,128]{2,1,0:T(8,128)}), f32[32,32,128]{2,1,0:T(8,128)S(1)}, u32[]{:S(2)}, u32[]{:S(2)}) async-start(f32[32,32,128]{2,1,0:T(8,128)} %get-tuple-element.58), calls=%async_computation.1 | async-start | bytes 1048576 | tf_op jit(solution)/shard_map/all_to_all | solution.py:604
  73.6 2.7 %collective-permute-start.5 = (f32[1024,128]{1,0:T(8,128)}, f32[1024,128]{1,0:T(8,128)S(1)}, u32[]{:S(2)}, u32[]{:S(2)}) collective-permute-start(f32[1024,128]{1,0:T(8,128)} %get-tuple-element.65.left), channel_id=1, source_target_pairs={{0,1},{1,0},{2,3},{3,2},{4,5},{5,4},{6,7},{7,6},{8,9},{9,8},{10,11... | collective-permute-start | bytes 1572872 | tf_op jit(solution)/shard_map/ppermute | solution.py:592
  73.9 33.2 %collective-permute-start.6 = (f32[32,32,128]{2,1,0:T(8,128)}, f32[32,32,128]{2,1,0:T(8,128)S(1)}, u32[]{:S(2)}, u32[]{:S(2)}) collective-permute-start(f32[32,32,128]{2,1,0:T(8,128)} %get-tuple-element.68.right_0), channel_id=1, source_target_pairs={{2,0},{4,2},{6,4},{0,6},{3,1},{5,3},{7,5},{1,7},{10,8},{12,10},{14... | collective-permute-start | bytes 1572872 | tf_op jit(solution)/shard_map/ppermute | solution.py:596
  74.6 35.8 %collective-permute-start.7 = (f32[32,32,128]{2,1,0:T(8,128)}, f32[32,32,128]{2,1,0:T(8,128)S(1)}, u32[]{:S(2)}, u32[]{:S(2)}) collective-permute-start(f32[32,32,128]{2,1,0:T(8,128)} %get-tuple-element.68.right_0), channel_id=1, source_target_pairs={{4,0},{6,2},{0,4},{2,6},{5,1},{7,3},{1,5},{3,7},{12,8},{14,10},{8,... | collective-permute-start | bytes 1572872 | tf_op jit(solution)/shard_map/ppermute | solution.py:596
  75.7 34.7 %collective-permute-start.8 = (f32[32,32,128]{2,1,0:T(8,128)}, f32[32,32,128]{2,1,0:T(8,128)S(1)}, u32[]{:S(2)}, u32[]{:S(2)}) collective-permute-start(f32[32,32,128]{2,1,0:T(8,128)} %get-tuple-element.68.right_0), channel_id=1, source_target_pairs={{6,0},{0,2},{2,4},{4,6},{7,1},{1,3},{3,5},{5,7},{14,8},{8,10},{10,... | collective-permute-start | bytes 1572872 | tf_op jit(solution)/shard_map/ppermute | solution.py:596
  76.4 2.2 %copy-start = (f32[32,256,128]{2,1,0:T(8,128)S(1)}, f32[32,256,128]{2,1,0:T(8,128)}, u32[]{:S(2)}) copy-start(f32[32,256,128]{2,1,0:T(8,128)} %param.14) | copy-start | bytes 12582916
  103.3 26.5 %collective-permute-start.11 = (f32[32,32,128]{2,1,0:T(8,128)}, f32[32,32,128]{2,1,0:T(8,128)S(1)}, u32[]{:S(2)}, u32[]{:S(2)}) collective-permute-start(f32[32,32,128]{2,1,0:T(8,128)} %get-tuple-element.73), channel_id=1, source_target_pairs={{0,4},{2,6},{4,0},{6,2},{1,5},{3,7},{5,1},{7,3},{8,12},{10,14},{12... | collective-permute-start | bytes 1572872 | tf_op jit(solution)/shard_map/ppermute | solution.py:600
  107.1 23.1 %collective-permute-start.12 = (f32[32,32,128]{2,1,0:T(8,128)}, f32[32,32,128]{2,1,0:T(8,128)S(1)}, u32[]{:S(2)}, u32[]{:S(2)}) collective-permute-start(f32[32,32,128]{2,1,0:T(8,128)} %get-tuple-element.74), channel_id=1, source_target_pairs={{0,2},{2,4},{4,6},{6,0},{1,3},{3,5},{5,7},{7,1},{8,10},{10,12},{12... | collective-permute-start | bytes 1572872 | tf_op jit(solution)/shard_map/ppermute | solution.py:600
  107.1 23.1 %collective-permute-start.13 = (f32[32,32,128]{2,1,0:T(8,128)}, f32[32,32,128]{2,1,0:T(8,128)S(1)}, u32[]{:S(2)}, u32[]{:S(2)}) collective-permute-start(f32[32,32,128]{2,1,0:T(8,128)} %get-tuple-element.75), channel_id=1, source_target_pairs={{0,6},{2,0},{4,2},{6,4},{1,7},{3,1},{5,3},{7,5},{8,14},{10,8},{12,... | collective-permute-start | bytes 1572872 | tf_op jit(solution)/shard_map/ppermute | solution.py:600
  110.4 32.2 %copy-start.2 = (f32[64,8]{0,1:T(8,128)S(1)}, f32[64,8]{0,1:T(8,128)}, u32[]{:S(2)}) copy-start(f32[64,8]{0,1:T(8,128)} %param.17) | copy-start | bytes 6148
  110.4 32.2 %copy-start.4 = (f32[64,8]{0,1:T(8,128)S(1)}, f32[64,8]{0,1:T(8,128)}, u32[]{:S(2)}) copy-start(f32[64,8]{0,1:T(8,128)} %param.18) | copy-start | bytes 6148
  127.6 1.7 %collective-permute-start.10 = (f32[512,128]{1,0:T(8,128)}, f32[512,128]{1,0:T(8,128)S(1)}, u32[]{:S(2)}, u32[]{:S(2)}) collective-permute-start(f32[512,128]{1,0:T(8,128)} %get-tuple-element.71), channel_id=1, source_target_pairs={{0,1},{1,0},{2,3},{3,2},{4,5},{5,4},{6,7},{7,6},{8,9},{9,8},{10,11... | collective-permute-start | bytes 786440 | tf_op jit(solution)/shard_map/ppermute | solution.py:592
  127.6 2.1 %collective-permute-start.9 = (f32[512,128]{1,0:T(8,128)}, f32[512,128]{1,0:T(8,128)S(1)}, u32[]{:S(2)}, u32[]{:S(2)}) collective-permute-start(f32[512,128]{1,0:T(8,128)} %get-tuple-element.70), channel_id=1, source_target_pairs={{0,1},{1,0},{2,3},{3,2},{4,5},{5,4},{6,7},{7,6},{8,9},{9,8},{10,11... | collective-permute-start | bytes 786440 | tf_op jit(solution)/shard_map/ppermute | solution.py:592
  137.7 20.1 %all-to-all-start.2 = ((f32[32,24,128]{2,1,0:T(8,128)}), f32[32,24,128]{2,1,0:T(8,128)S(1)}, u32[]{:S(2)}, u32[]{:S(2)}) async-start(f32[32,24,128]{2,1,0:T(8,128)} %get-tuple-element.80), calls=%async_computation.2 | async-start | bytes 786432 | tf_op jit(solution)/shard_map/all_to_all | solution.py:604

commit v4 on v3

--- a/solution.py
+++ b/solution.py
@@ -114,10 +114,12 @@
     send[:, rows, :] = jnp.broadcast_to(values[None], (send.shape[0],) + values.shape)
 
 
-def norm_kernel(m0, mask, x0t, inverse, present, send):
+def norm_kernel(m0, mask, x0t, inverse, present, send, arrive, depart):
     shown = mask[...].astype(F32).T
     present[...] = shown
     for pair in range(RES // 2):
+        if pair % 4 == 0:
+            arrive(pair // 4)
         block = m0[:, 128 * pair : 128 * pair + 128].T
         for k in range(2):
             part = block[64 * k : 64 * k + 64]
@@ -126,6 +128,8 @@
             row = 2 * pair + k
             inverse[row : row + 1] = scale
             x0t[64 * row : 64 * row + 64] = center * scale
+        if pair % 4 == 3:
+            depart(pair // 4)
     ones = shown.astype(jnp.bfloat16)
     sums = own_blocks(sum_lanes_01(ones, x0t[...]))
     counts = dot_nt(jnp.ones((16, SEQ), jnp.bfloat16), ones)
@@ -225,7 +229,7 @@
 
 def attend_kernel(
     got, local, raw, m0t, gate, present, mixing, factors,
-    probs, attended, mixed, x1t, inverse_mid, left, right, inverse_count, moments, scratch, arrive,
+    probs, attended, mixed, x1t, inverse_mid, left, right, inverse_count, moments, scratch, arrive, depart,
 ):
     peers = got.shape[0]
     share = 64 // peers
@@ -258,8 +262,9 @@
     heads_t = heads.T
     mixing_parts = lhs_parts(mixing[...])
     factor_parts = lhs_parts(factors[...])
-    arrive()
     for pair in range(RES // 2):
+        if pair % 4 == 0:
+            arrive(pair // 4)
         shown, used, base = [], [], []
         for k in range(2):
             i = 2 * pair + k
@@ -281,21 +286,27 @@
             inverse_mid[i : i + 1] = scale[:, lanes]
             left[32 * i : 32 * i + 32] = found[:32, lanes]
             scratch[32 * i : 32 * i + 32] = found[32:, lanes]
+        if pair % 4 == 3:
+            depart(pair // 4)
     for f in range(FACTOR_WIDTH):
         right[f] = scratch[pl.ds(f, RES, stride=FACTOR_WIDTH), :]
 
 
 def middle_kernel(
     left_own, left_far_0, left_far_1, right_own, right_1, right_2, right_3, moments, x1t, inverse_mid, present, slope_t, gate,
-    factors_back, mixing_back, mid, out_grad, send, scratch,
+    factors_back, mixing_back, mid, out_grad, send, scratch, arrive, depart,
 ):
-    for f in range(FACTOR_WIDTH):
-        scratch[32 * f : 32 * f + 32] = (right_own[f] + right_1[f]) + (right_2[f] + right_3[f])
     parts = lhs_parts(factors_back[...])
     mixing_parts = lhs_parts(mixing_back[...])
     ones = jnp.ones((16, SEQ), jnp.bfloat16)
     sums = []
     for pair in range(RES // 2):
+        if pair % 4 == 0:
+            arrive(pair // 4)
+            rows = slice(2 * pair, 2 * pair + 8)
+            for f in range(FACTOR_WIDTH):
+                part = (right_own[f, rows] + right_1[f, rows]) + (right_2[f, rows] + right_3[f, rows])
+                scratch[32 * f + 2 * pair : 32 * f + 2 * pair + 8] = part
         grads = []
         for k in range(2):
             i = 2 * pair + k
@@ -326,6 +337,8 @@
             mid[rows] = back[:, lanes]
             out_grad[rows] = grad[:, lanes]
             gated.append(grad[:, lanes] * gate[rows])
+        if pair % 4 == 3:
+            depart(pair // 4)
         sums.append(sum_lanes_01(ones, jnp.concatenate(gated, axis=0)))
     sums = [jnp.concatenate([part, part], axis=0) for part in sums]
     send_all(send, slice(0, 16), pack(own_blocks(jnp.concatenate(sums, axis=1))))
@@ -345,7 +358,7 @@
 
 
 def finish_kernel(
-    got, attended, probs, keys, values, query_blocks, partial, key_value, counts, asking, present, x0t, inverse, mid, out, arrive
+    got, attended, probs, keys, values, query_blocks, partial, key_value, counts, asking, present, x0t, inverse, mid, out, arrive, depart
 ):
     att_grad = unpack(jnp.sum(got[:, 0:16, :], axis=0))
     moments = got[:, 16:, :].reshape(RES * 8, 128)
@@ -365,8 +378,9 @@
     key_grad = exact_nn(query_blocks[...].T, score_grad)
     value_grad = exact_nn(blocks.T, probs[...])
     parts = lhs_parts(key_value[...])
-    arrive()
     for pair in range(RES // 2):
+        if pair % 4 == 0:
+            arrive(pair // 4)
         both = []
         for k in range(2):
             rows = slice(16 * pair + 8 * k, 16 * pair + 8 * k + 8)
@@ -383,51 +397,80 @@
             )
             done.append(mid[rows] + back)
         out[:, 128 * pair : 128 * pair + 128] = jnp.concatenate(done, axis=0).T
+        if pair % 4 == 3:
+            depart(pair // 4)
 
 
 def whole(shape):
     return pl.BlockSpec(shape, lambda *_: (0,) * len(shape))
 
 
-def staged(kernel, count, late, *refs):
+GROUPS = 4
+
+
+def portion(ref, group):
+    axis = 1 if len(ref.shape) == 3 or ref.shape[1] > 128 else 0
+    size = ref.shape[axis] // GROUPS
+    window = slice(group * size, group * size + size)
+    return ref.at[:, window] if axis else ref.at[window]
+
+
+def staged(kernel, count, late, early, *refs):
     operands, rest = refs[: count[0]], refs[count[0] :]
     results, rest = rest[: count[1]], rest[count[1] :]
     total = count[0] + count[1]
     held, sems, scratch = rest[:total], rest[total], rest[total + 1 :]
-    copies = [pltpu.make_async_copy(operands[k], held[k], sems.at[k]) for k in range(count[0])]
-    for copy in copies:
+    whole_in = [k for k in range(count[0]) if k not in late]
+    copies = [pltpu.make_async_copy(operands[k], held[k], sems.at[k, 0]) for k in whole_in]
+    groups = [
+        [
+            pltpu.make_async_copy(portion(operands[k], group), portion(held[k], group), sems.at[k, group])
+            for k in late
+        ]
+        for group in range(GROUPS)
+    ]
+    for copy in copies + sum(groups, []):
         copy.start()
 
-    def arrive():
-        for k in late:
-            copies[k].wait()
-
-    for k in range(count[0]):
-        if k not in late:
-            copies[k].wait()
-    kernel(*held, *scratch, *([arrive] if late else []))
-    copies = [
-        pltpu.make_async_copy(held[count[0] + k], results[k], sems.at[count[0] + k]) for k in range(count[1])
-    ]
-    for copy in copies:
-        copy.start()
+    def arrive(group):
+        for copy in groups[group]:
+            copy.wait()
+
+    leaving = []
+
+    def depart(group):
+        for k in early:
+            at = count[0] + k
+            copy = pltpu.make_async_copy(portion(held[at], group), portion(results[k], group), sems.at[at, group])
+            copy.start()
+            leaving.append(copy)
+
     for copy in copies:
         copy.wait()
-
-
-def call(kernel, shapes, *operands, scratch=(), late=(), free=(), vmem=40):
+    kernel(*held, *scratch, *([arrive, depart] if late else []))
+    for k in range(count[1]):
+        if k not in early:
+            at = count[0] + k
+            copy = pltpu.make_async_copy(held[at], results[k], sems.at[at, 0])
+            copy.start()
+            leaving.append(copy)
+    for copy in leaving:
+        copy.wait()
+
+
+def call(kernel, shapes, *operands, scratch=(), late=(), early=(), free=(), vmem=40):
     shapes = [jax.ShapeDtypeStruct(shape, F32) for shape in shapes]
     size = sum(4 * array.size for array in shapes) + sum(array.size * array.dtype.itemsize for array in operands)
     arrays = list(operands) + shapes
     return pl.pallas_call(
-        functools.partial(staged, kernel, (len(operands), len(shapes)), late),
+        functools.partial(staged, kernel, (len(operands), len(shapes)), late, early),
         in_specs=[
             pl.BlockSpec(memory_space=pl.ANY if k in free else pltpu.HBM) for k in range(len(operands))
         ],
         out_specs=[pl.BlockSpec(memory_space=pltpu.HBM)] * len(shapes),
         out_shape=[pltpu.HBM(array.shape, array.dtype) for array in shapes],
         scratch_shapes=[pltpu.VMEM(array.shape, array.dtype) for array in arrays]
-        + [pltpu.SemaphoreType.DMA((len(arrays),))]
+        + [pltpu.SemaphoreType.DMA((len(arrays), GROUPS))]
         + list(scratch),
         compiler_params=pltpu.CompilerParams(vmem_limit_bytes=vmem * 2**20),
         cost_estimate=pl.CostEstimate(flops=100_000_000, bytes_accessed=int(size), transcendentals=0),
@@ -459,16 +502,17 @@
         total[...] = jnp.zeros_like(total)
 
     near = step < pl.num_programs(0) // 2
-    inverse_column = inverse_count[...].T
     for pair in range(ROWS // 2):
         blocks = []
         for row in (2 * pair, 2 * pair + 1):
             for d in range(4):
                 chip = lax.rem(x + d, 4)
-                scale = inverse_column[32 * d : 32 * d + 32, row : row + 1]
-                blocks.append(scale * jnp.where(near, own_g[row, chip, 0], far_g[row, chip, 0]))
+                blocks.append(jnp.where(near, own_g[row, chip, 0], far_g[row, chip, 0]))
         g_high, g_low = split(jnp.concatenate(blocks, axis=0))
         grads = dot_nt(weights[...], jnp.concatenate([g_high, g_high, g_low], axis=1))
+        grads = grads * jnp.concatenate(
+            [inverse_count[2 * pair : 2 * pair + 1], inverse_count[2 * pair + 1 : 2 * pair + 2]], axis=1
+        )
         grads_high, grads_low = split(grads)
         for k in range(2):
             row = (2 * pair + k) * FACTOR_WIDTH
@@ -527,7 +571,14 @@
         compiler_params=pltpu.CompilerParams(vmem_limit_bytes=48 * 2**20),
         cost_estimate=pl.CostEstimate(flops=COST, bytes_accessed=COST, transcendentals=0),
         name="right_products",
-    )(place, pair_grad, far_grad, *[pltpu.with_memory_space_constraint(part, pltpu.HBM) for part in (inverse_count, weight, left)], left_far)
+    )(
+        place,
+        *[
+            pltpu.with_memory_space_constraint(part, pltpu.HBM)
+            for part in (pair_grad, far_grad, inverse_count, weight, left)
+        ],
+        left_far,
+    )
 
 
 def left_kernel(high, low, right_0, right_1, right_2, right_3, own, far_0, far_1, weights):
@@ -634,7 +685,7 @@
 
     flat, heads, stat = (RES * 64, SEQ), (RES * 8, SEQ), (RES, SEQ)
     x0t, inverse, present, send = call(
-        norm_kernel, [flat, stat, stat, (peers, counted, 128)], homolog_features, alignment_mask
+        norm_kernel, [flat, stat, stat, (peers, counted, 128)], homolog_features, alignment_mask, late=(0,), early=(0,)
     )
     (send,) = call(pair_kernel, [(peers, counted, 128)], send, alignment_mask, mask_core, *mask_chips, free=(2, 3, 4, 5))
     x0t, send, pair_grad = lax.optimization_barrier((x0t, send, pair_update_gradient))
@@ -655,7 +706,7 @@
     probs, attended, mixed, x1t, inverse_mid, left, right, inverse_count, moments = call(
         attend_kernel,
         [heads, (RES, 64), flat, flat, stat, (RES * 32, SEQ), (FACTOR_WIDTH, RES, SEQ), (64, 128), (block, 128)],
-        got, local, raw, m0t, gate, present, final_mixing_matrix.T, factors.T, late=(3, 4), free=(0, 6, 7),
+        got, local, raw, m0t, gate, present, final_mixing_matrix.T, factors.T, late=(3, 4), early=(2, 3, 5), free=(0, 6, 7),
         scratch=[pltpu.VMEM((RES * 32, SEQ), F32)],
     )
     rights = [right] + [fetch_chip(right, d) for d in (1, 2, 3)]
@@ -668,7 +719,7 @@
     mid, out_grad, send = call(
         middle_kernel, [flat, flat, (peers, 16 + block, 128)],
         left_own, *left_far, right_own, *right_sent,
-        moments, x1t, inverse_mid, present, slope_t, gate, factors, final_mixing_matrix, free=(1, 2, 4, 5, 6, 13),
+        moments, x1t, inverse_mid, present, slope_t, gate, factors, final_mixing_matrix, late=(0, 3, 4, 5, 6, 8, 11, 12), early=(0, 1), free=(1, 2, 4, 5, 6, 13),
         scratch=[pltpu.VMEM((RES * 32, SEQ), F32)],
     )
     got = exchange(send)
@@ -676,7 +727,7 @@
     (out,) = call(
         finish_kernel, [(SEQ, RES * 64)],
         got, attended, probs, keys, values, query_blocks, gate_grad, key_value, counts, asking_matrix,
-        present, x0t, inverse, mid, late=(6, 11, 13), free=(0, 7),
+        present, x0t, inverse, mid, late=(6, 11, 13), early=(0,), free=(0, 7),
     )
     return out
 

time: 165 us -> 163 us (0.988)
  local copies, waits for them, and re-layouts: 9.29 us -> 7.1 us
    unnamed x15 -> x13, local copies, waits for them, and re-layouts: 6.98 us -> 4.79 us
    pallas_call x8, Pallas kernels: 37.9 us -> 39.7 us  [call(): pl.pallas_call(functools.partial(staged, kernel, (len(operands), len(shap...]
where the time goes in v4:
time: 163 us; the launch traced here: 162 us
  Pallas kernels  80.5 us (49%)
  waiting for transfers between devices  36.9 us (23%)
  starting transfers between devices  35.9 us (22%)
  local copies, waits for them, and re-layouts  7.1 us (4%)
    pallas_call x8, Pallas kernels, call(): pl.pallas_call(functools.partial(staged, kernel, (len(operands), len(shap...  39.7 us
    all_to_all x3, waiting for transfers between devices, exchange(): return lax.all_to_all(send, 'seq', 0, 0, tiled=True)  32.8 us
    pallas_call x1, Pallas kernels, right_products(): pl.pallas_call(right_kernel, grid_spec=grid_spec, out_shape=[pltpu.HBM((F...  23.5 us
    all_to_all x3, starting transfers between devices, exchange(): return lax.all_to_all(send, 'seq', 0, 0, tiled=True)  21 us
    pallas_call x1, Pallas kernels, left_products(): pl.pallas_call(left_kernel, grid=(steps,), in_specs=[rows, rows] + [whole...  17.2 us
    ppermute x3, starting transfers between devices, send_chip(): lax.ppermute(values, 'x', [(i, (i + distance) % 4) for i in range(4)])  7.1 us
    ppermute x6, starting transfers between devices, fetch_chip(): lax.ppermute(values, 'x', [((i + distance) % 4, i) for i in range(4)])  6.98 us
    unnamed x13, local copies, waits for them, and re-layouts  4.79 us
  transfers between devices with their start and end apart: 17, of which 8 were waited for; matrix products, arithmetic and copies ran while one was open for 4% of the time, Pallas kernels for 32%

profile of v4, /device:TPU:32, one launch (start us, length us, event | category | flops | bytes accessed | tf_op | source)
XLA Modules:
  0.0 161.7 jit_solution(12063557170101777928)
XLA Ops:
  0.0 0.8 copy.27.refs_1_
  0.8 0.0 copy-start.2
  0.8 0.1 collective-permute-start
  0.9 2.8 %collective-permute-start.1 = (s32[128,32]{1,0:T(8,128)S(1)}, s32[128,32]{1,0:T(8,128)S(1)}, u32[]{:S(2)}, u32[]{:S(2)}) collective-permute-start(s32[128,32]{1,0:T(8,128)S(1)} %copy.27.refs_1_), channel_id=1, source_target_pairs={{2,0},{4,2},{6,4},{0,6},{3,1},{5,3},{7,5},{1,7},{10,8},{12,10},{14... | collective-permute-start | bytes 49160 | tf_op jit(solution)/shard_map/ppermute | solution.py:647
  3.8 0.8 collective-permute-start.2
  4.6 0.9 collective-permute-start.3
  5.4 0.0 copy-done.2
  5.4 3.3 %norm_kernel.1 = (f32[2048,128]{1,0:T(8,128)}, f32[32,128]{1,0:T(8,128)}, f32[32,128]{1,0:T(8,128)}, f32[32,24,128]{2,1,0:T(8,128)}) custom-call(f32[128,2048]{1,0:T(8,128)} %refs_1_.3, s32[128,32]{1,0:T(8,128)} %copy-done.2), custom_call_target="tpu_custom_call" | custom-call | flops 100000000 | bytes 2539520 | tf_op jit(solution)/shard_map/norm_kernel/pallas_call | solution.py:465
  8.7 0.0 collective-permute-done.refs_2_
  8.8 0.0 collective-permute-done.1.refs_3_
  8.8 1.4 collective-permute-done.2.refs_4_
  10.1 0.7 collective-permute-done.3.refs_5_
  10.8 2.2 %pair_kernel.1 = f32[32,24,128]{2,1,0:T(8,128)} custom-call(f32[32,24,128]{2,1,0:T(8,128)} %get-tuple-element.48.refs_0_, s32[128,32]{1,0:T(8,128)} %copy-done.2, s32[128,32]{1,0:T(8,128)S(1)} %collective-permute-done.refs_2_, s32[128,32]{1,0:T(8,128)S(1)} %collective-permute-done.1.refs_3_, s32[128,32]{1,0:T(8,128)S(1)} %collective-permute-done.2.refs_4_, ...), custom_call_target="tpu_custom_call" | custom-call | flops 100000000 | bytes 868352 | tf_op jit(solution)/shard_map/pair_kernel/pallas_call | solution.py:465
  13.1 0.1 collective-permute-start.4
  13.2 11.4 %all-to-all-start = ((f32[32,24,128]{2,1,0:T(8,128)}), f32[32,24,128]{2,1,0:T(8,128)S(1)}, u32[]{:S(2)}, u32[]{:S(2)}) async-start(f32[32,24,128]{2,1,0:T(8,128)} %pair_kernel.1), calls=%async_computation | async-start | bytes 786432 | tf_op jit(solution)/shard_map/all_to_all | solution.py:655
  24.5 2.2 %copy.33 = f32[32,32,128]{2,0,1:T(8,128)} copy(f32[32,32,128]{2,1,0:T(8,128)} %bitcast.18) | data formatting | bytes 1048576 | tf_op jit(solution)/shard_map/reshape | solution.py:681
  26.7 0.8 copy.34
  27.5 0.1 pad_add_fusion.place
  27.6 0.7 maximum_bitcast_fusion.refs_4_
  28.3 0.0 copy-start
  28.3 0.7 copy-done
  29.0 4.8 %project_kernel.1 = (f32[256,128]{1,0:T(8,128)}, f32[256,128]{1,0:T(8,128)}, f32[2048,128]{1,0:T(8,128)}, f32[2048,128]{1,0:T(8,128)}, f32[2048,128]{1,0:T(8,128)}) custom-call(f32[2048,128]{1,0:T(8,128)} %get-tuple-element.54.refs_0_.refs_11_, f32[128,2048]{1,0:T(8,128)} %refs_1_.3, f32[128,2048]{1,0:T(8,128)} %refs_2_.1, f32[8,64]{1,0:T(8,128)S(1)} %bitcast.15, ...), custom_call_target="tpu_custom_call" | custom-call | flops 100000000 | bytes 6574080 | tf_op jit(solution)/shard_map/project_kernel/pallas_call | solution.py:465
  33.8 6.3 %all-to-all-done.refs_0_ = f32[32,24,128]{2,1,0:T(8,128)S(1)} async-done(((f32[32,24,128]{2,1,0:T(8,128)}), f32[32,24,128]{2,1,0:T(8,128)S(1)}, u32[]{:S(2)}, u32[]{:S(2)}) %all-to-all-start) | async-done | bytes 393248 | tf_op jit(solution)/shard_map/all_to_all | solution.py:655
  40.1 0.0 collective-permute-done.4
  40.1 6.3 %score_kernel.1 = (f32[256,128]{1,0:T(8,128)}, f32[32,16]{1,0:T(8,128)}, f32[32,128]{1,0:T(8,128)}, f32[256,256]{1,0:T(8,128)}, f32[32,32,128]{2,1,0:T(8,128)}) custom-call(f32[32,24,128]{2,1,0:T(8,128)S(1)} %all-to-all-done.refs_0_, f32[256,128]{1,0:T(8,128)} %get-tuple-element.55.refs_1_.refs_3_, f32[256,128]{1,0:T(8,128)} %get-tuple-element.56.refs_2_.refs_4_, ...), custom_call_target="tpu_custom_call" | custom-call | flops 100000000 | bytes 1624064 | tf_op jit(solution)/shard_map/score_kernel/pallas_call | solution.py:465
  46.4 4.8 %all-to-all-start.1 = ((f32[32,32,128]{2,1,0:T(8,128)}), f32[32,32,128]{2,1,0:T(8,128)S(1)}, u32[]{:S(2)}, u32[]{:S(2)}) async-start(f32[32,32,128]{2,1,0:T(8,128)} %get-tuple-element.58), calls=%async_computation.1 | async-start | bytes 1048576 | tf_op jit(solution)/shard_map/all_to_all | solution.py:655
  51.1 0.8 copy.36
  51.9 0.8 copy.37
  52.7 0.1 fusion
  52.8 0.1 copy.38.refs_7_
  52.9 0.8 copy.35
  53.8 14.9 %all-to-all-done.1.refs_0_ = f32[32,32,128]{2,1,0:T(8,128)S(1)} async-done(((f32[32,32,128]{2,1,0:T(8,128)}), f32[32,32,128]{2,1,0:T(8,128)S(1)}, u32[]{:S(2)}, u32[]{:S(2)}) %all-to-all-start.1) | async-done | bytes 524320 | tf_op jit(solution)/shard_map/all_to_all | solution.py:655
  68.7 6.0 %attend_kernel.1 = (f32[256,128]{1,0:T(8,128)}, f32[32,64]{1,0:T(8,128)}, f32[2048,128]{1,0:T(8,128)}, f32[2048,128]{1,0:T(8,128)}, f32[32,128]{1,0:T(8,128)}, /...) custom-call(f32[32,32,128]{2,1,0:T(8,128)S(1)} %all-to-all-done.1.refs_0_, ...), custom_call_target="tpu_custom_call" | custom-call | flops 100000000 | bytes 6141952 | tf_op jit(solution)/shard_map/attend_kernel/pallas_call | solution.py:465
  74.7 0.1 collective-permute-start.5
  74.8 0.6 collective-permute-start.6
  75.5 1.3 collective-permute-start.7
  76.8 0.5 collective-permute-start.8
  77.3 0.0 collective-permute-done.5.left_far
  77.3 23.5 %right_products.1 = (bf16[32,2048,128]{2,1,0:T(8,128)(2,1)}, bf16[32,2048,128]{2,1,0:T(8,128)(2,1)}, f32[32,32,128]{2,1,0:T(8,128)}, f32[32,32,128]{2,1,0:T(8,12...) custom-call(s32[2]{0:T(128)S(1)} %pad_add_fusion.place, f32[32,4,2,32,128]{4,3,2,1,0:T(8,128)} %bitcast.16, ...), custom_call_target="tpu_custom_call" | custom-call | flops 1000 | bytes 1000 | tf_op jit(solution)/shard_map/right_products/pallas_call | solution.py:563
  100.8 3.9 %collective-permute-start.11 = (f32[32,32,128]{2,1,0:T(8,128)}, f32[32,32,128]{2,1,0:T(8,128)S(1)}, u32[]{:S(2)}, u32[]{:S(2)}) collective-permute-start(f32[32,32,128]{2,1,0:T(8,128)} %get-tuple-element.73), channel_id=1, source_target_pairs={{0,4},{2,6},{4,0},{6,2},{1,5},{3,7},{5,1},{7,3},{8,12},{10,14},{12... | collective-permute-start | bytes 1572872 | tf_op jit(solution)/shard_map/ppermute | solution.py:651
  104.7 0.0 collective-permute-start.12
  104.7 0.0 collective-permute-done.6.right_1
  104.7 3.2 %collective-permute-start.13 = (f32[32,32,128]{2,1,0:T(8,128)}, f32[32,32,128]{2,1,0:T(8,128)S(1)}, u32[]{:S(2)}, u32[]{:S(2)}) collective-permute-start(f32[32,32,128]{2,1,0:T(8,128)} %get-tuple-element.75), channel_id=1, source_target_pairs={{0,6},{2,0},{4,2},{6,4},{1,7},{3,1},{5,3},{7,5},{8,14},{10,8},{12,... | collective-permute-start | bytes 1572872 | tf_op jit(solution)/shard_map/ppermute | solution.py:651
  107.9 0.0 collective-permute-done.7.right_2
  108.0 0.0 collective-permute-done.8.right_3
  108.0 0.0 copy-start.1
  108.0 0.0 copy-start.3
  108.0 17.2 %left_products.1 = (f32[1024,128]{1,0:T(8,128)}, f32[512,128]{1,0:T(8,128)}, f32[512,128]{1,0:T(8,128)}) custom-call(bf16[32,2048,128]{2,1,0:T(8,128)(2,1)} %get-tuple-element.66.high, bf16[32,2048,128]{2,1,0:T(8,128)(2,1)} %get-tuple-element.67.low, f32[32,32,128]{2,1,0:T(8,128)} %get-tuple-element.68.right_0, ...), custom_call_target="tpu_custom_call" | custom-call | flops 1000 | bytes 1000 | tf_op jit(solution)/shard_map/left_products/pallas_call | solution.py:624
  125.2 0.0 collective-permute-start.10
  125.2 0.5 collective-permute-start.9
  125.7 0.1 pad_maximum_fusion.refs_13_
  125.8 1.2 collective-permute-done.10.refs_2_
  126.9 0.4 collective-permute-done.9.refs_1_
  127.3 0.0 collective-permute-done.11.refs_4_
  127.3 0.5 collective-permute-done.12.refs_5_
  127.8 0.0 collective-permute-done.13.refs_6_
  127.8 7.5 %middle_kernel.1 = (f32[2048,128]{1,0:T(8,128)}, f32[2048,128]{1,0:T(8,128)}, f32[32,24,128]{2,1,0:T(8,128)}) custom-call(f32[1024,128]{1,0:T(8,128)} %get-tuple-element.69.refs_0_, f32[512,128]{1,0:T(8,128)S(1)} %collective-permute-done.9.refs_1_, f32[512,128]{1,0:T(8,128)S(1)} %collective-permute-done.10.refs_2_, ...), custom_call_target="tpu_custom_call" | custom-call | flops 100000000 | bytes 8851456 | tf_op jit(solution)/shard_map/middle_kernel/pallas_call | solution.py:465
  135.3 4.9 %all-to-all-start.2 = ((f32[32,24,128]{2,1,0:T(8,128)}), f32[32,24,128]{2,1,0:T(8,128)S(1)}, u32[]{:S(2)}, u32[]{:S(2)}) async-start(f32[32,24,128]{2,1,0:T(8,128)} %get-tuple-element.80), calls=%async_computation.2 | async-start | bytes 786432 | tf_op jit(solution)/shard_map/all_to_all | solution.py:655
  140.2 0.0 copy-done.1
  140.2 0.0 copy-done.3
  140.2 0.1 copy.39.refs_7_
  140.3 3.5 %gate_back_kernel.1.refs_6_ = f32[2048,128]{1,0:T(8,128)} custom-call(f32[2048,128]{1,0:T(8,128)} %get-tuple-element.84.refs_0_, f32[2048,128]{1,0:T(8,128)} %get-tuple-element.85.refs_1_, f32[2048,128]{1,0:T(8,128)} %get-tuple-element.62.refs_4_.refs_12_.refs_2_, f32[64,64]{1,0:T(8,128)} %refs_3_.1), custom_call_target="tpu_custom_call" | custom-call | flops 100000000 | bytes 4210688 | tf_op jit(solution)/shard_map/gate_back_kernel/pallas_call | solution.py:465
  143.8 11.6 %all-to-all-done.2.refs_0_ = f32[32,24,128]{2,1,0:T(8,128)S(1)} async-done(((f32[32,24,128]{2,1,0:T(8,128)}), f32[32,24,128]{2,1,0:T(8,128)S(1)}, u32[]{:S(2)}, u32[]{:S(2)}) %all-to-all-start.2) | async-done | bytes 393248 | tf_op jit(solution)/shard_map/all_to_all | solution.py:655
  155.4 6.1 %finish_kernel.1 = f32[128,2048]{1,0:T(8,128)} custom-call(f32[32,24,128]{2,1,0:T(8,128)S(1)} %all-to-all-done.2.refs_0_, f32[32,64]{1,0:T(8,128)} %get-tuple-element.81.refs_1_, f32[256,128]{1,0:T(8,128)} %get-tuple-element.82.refs_2_, f32[256,128]{1,0:T(8,128)} %get-tuple-element.55.refs_1_.refs_3_, f32[256,128]{1,0:T(8,128)} %get-tuple-element.56.refs_2_.refs_4_, ...), custom_call_target="tpu_custom_call" | custom-call | flops 100000000 | bytes 5320704 | tf_op jit(solution)/shard_map/finish_kernel/pallas_call | solution.py:465
  (1 shorter events, 0.0 us)
Async XLA Ops:
  0.8 4.6 %copy-start.2 = (s32[128,32]{1,0:T(8,128)}, s32[128,32]{1,0:T(8,128)S(1)}, u32[]{:S(2)}) copy-start(s32[128,32]{1,0:T(8,128)S(1)} %copy.27.refs_1_) | copy-start | bytes 49156
  0.8 7.9 %collective-permute-start = (s32[128,32]{1,0:T(8,128)S(1)}, s32[128,32]{1,0:T(8,128)S(1)}, u32[]{:S(2)}, u32[]{:S(2)}) collective-permute-start(s32[128,32]{1,0:T(8,128)S(1)} %copy.27.refs_1_), channel_id=1, source_target_pairs={{0,1},{1,0},{2,3},{3,2},{4,5},{5,4},{6,7},{7,6},{8,9},{9,8},{10,11... | collective-permute-start | bytes 49160 | tf_op jit(solution)/shard_map/ppermute | solution.py:643
  0.9 7.8 %collective-permute-start.1 = (s32[128,32]{1,0:T(8,128)S(1)}, s32[128,32]{1,0:T(8,128)S(1)}, u32[]{:S(2)}, u32[]{:S(2)}) collective-permute-start(s32[128,32]{1,0:T(8,128)S(1)} %copy.27.refs_1_), channel_id=1, source_target_pairs={{2,0},{4,2},{6,4},{0,6},{3,1},{5,3},{7,5},{1,7},{10,8},{12,10},{14... | collective-permute-start | bytes 49160 | tf_op jit(solution)/shard_map/ppermute | solution.py:647
  3.8 6.4 %collective-permute-start.2 = (s32[128,32]{1,0:T(8,128)S(1)}, s32[128,32]{1,0:T(8,128)S(1)}, u32[]{:S(2)}, u32[]{:S(2)}) collective-permute-start(s32[128,32]{1,0:T(8,128)S(1)} %copy.27.refs_1_), channel_id=1, source_target_pairs={{4,0},{6,2},{0,4},{2,6},{5,1},{7,3},{1,5},{3,7},{12,8},{14,10},{8,... | collective-permute-start | bytes 49160 | tf_op jit(solution)/shard_map/ppermute | solution.py:647
  4.6 6.3 %collective-permute-start.3 = (s32[128,32]{1,0:T(8,128)S(1)}, s32[128,32]{1,0:T(8,128)S(1)}, u32[]{:S(2)}, u32[]{:S(2)}) collective-permute-start(s32[128,32]{1,0:T(8,128)S(1)} %copy.27.refs_1_), channel_id=1, source_target_pairs={{6,0},{0,2},{2,4},{4,6},{7,1},{1,3},{3,5},{5,7},{14,8},{8,10},{10,... | collective-permute-start | bytes 49160 | tf_op jit(solution)/shard_map/ppermute | solution.py:647
  13.1 27.0 %collective-permute-start.4 = (f32[32,256,128]{2,1,0:T(8,128)}, f32[32,256,128]{2,1,0:T(8,128)}, u32[]{:S(2)}, u32[]{:S(2)}) collective-permute-start(f32[32,256,128]{2,1,0:T(8,128)} %param.14), channel_id=1, source_target_pairs={{0,1},{1,0},{2,3},{3,2},{4,5},{5,4},{6,7},{7,6},{8,9},{9,8},{10,11... | collective-permute-start | bytes 12582920 | tf_op jit(solution)/shard_map/ppermute | solution.py:643
  13.2 26.9 %all-to-all-start = ((f32[32,24,128]{2,1,0:T(8,128)}), f32[32,24,128]{2,1,0:T(8,128)S(1)}, u32[]{:S(2)}, u32[]{:S(2)}) async-start(f32[32,24,128]{2,1,0:T(8,128)} %pair_kernel.1), calls=%async_computation | async-start | bytes 786432 | tf_op jit(solution)/shard_map/all_to_all | solution.py:655
  28.3 0.7 copy-start
  46.4 22.3 %all-to-all-start.1 = ((f32[32,32,128]{2,1,0:T(8,128)}), f32[32,32,128]{2,1,0:T(8,128)S(1)}, u32[]{:S(2)}, u32[]{:S(2)}) async-start(f32[32,32,128]{2,1,0:T(8,128)} %get-tuple-element.58), calls=%async_computation.1 | async-start | bytes 1048576 | tf_op jit(solution)/shard_map/all_to_all | solution.py:655
  74.7 2.6 %collective-permute-start.5 = (f32[1024,128]{1,0:T(8,128)}, f32[1024,128]{1,0:T(8,128)S(1)}, u32[]{:S(2)}, u32[]{:S(2)}) collective-permute-start(f32[1024,128]{1,0:T(8,128)} %get-tuple-element.65.left), channel_id=1, source_target_pairs={{0,1},{1,0},{2,3},{3,2},{4,5},{5,4},{6,7},{7,6},{8,9},{9,8},{10,11... | collective-permute-start | bytes 1572872 | tf_op jit(solution)/shard_map/ppermute | solution.py:643
  74.8 29.9 %collective-permute-start.6 = (f32[32,32,128]{2,1,0:T(8,128)}, f32[32,32,128]{2,1,0:T(8,128)S(1)}, u32[]{:S(2)}, u32[]{:S(2)}) collective-permute-start(f32[32,32,128]{2,1,0:T(8,128)} %get-tuple-element.68.right_0), channel_id=1, source_target_pairs={{2,0},{4,2},{6,4},{0,6},{3,1},{5,3},{7,5},{1,7},{10,8},{12,10},{14... | collective-permute-start | bytes 1572872 | tf_op jit(solution)/shard_map/ppermute | solution.py:647
  75.5 32.5 %collective-permute-start.7 = (f32[32,32,128]{2,1,0:T(8,128)}, f32[32,32,128]{2,1,0:T(8,128)S(1)}, u32[]{:S(2)}, u32[]{:S(2)}) collective-permute-start(f32[32,32,128]{2,1,0:T(8,128)} %get-tuple-element.68.right_0), channel_id=1, source_target_pairs={{4,0},{6,2},{0,4},{2,6},{5,1},{7,3},{1,5},{3,7},{12,8},{14,10},{8,... | collective-permute-start | bytes 1572872 | tf_op jit(solution)/shard_map/ppermute | solution.py:647
  76.8 31.2 %collective-permute-start.8 = (f32[32,32,128]{2,1,0:T(8,128)}, f32[32,32,128]{2,1,0:T(8,128)S(1)}, u32[]{:S(2)}, u32[]{:S(2)}) collective-permute-start(f32[32,32,128]{2,1,0:T(8,128)} %get-tuple-element.68.right_0), channel_id=1, source_target_pairs={{6,0},{0,2},{2,4},{4,6},{7,1},{1,3},{3,5},{5,7},{14,8},{8,10},{10,... | collective-permute-start | bytes 1572872 | tf_op jit(solution)/shard_map/ppermute | solution.py:647
  100.8 26.5 %collective-permute-start.11 = (f32[32,32,128]{2,1,0:T(8,128)}, f32[32,32,128]{2,1,0:T(8,128)S(1)}, u32[]{:S(2)}, u32[]{:S(2)}) collective-permute-start(f32[32,32,128]{2,1,0:T(8,128)} %get-tuple-element.73), channel_id=1, source_target_pairs={{0,4},{2,6},{4,0},{6,2},{1,5},{3,7},{5,1},{7,3},{8,12},{10,14},{12... | collective-permute-start | bytes 1572872 | tf_op jit(solution)/shard_map/ppermute | solution.py:651
  104.7 23.1 %collective-permute-start.12 = (f32[32,32,128]{2,1,0:T(8,128)}, f32[32,32,128]{2,1,0:T(8,128)S(1)}, u32[]{:S(2)}, u32[]{:S(2)}) collective-permute-start(f32[32,32,128]{2,1,0:T(8,128)} %get-tuple-element.74), channel_id=1, source_target_pairs={{0,2},{2,4},{4,6},{6,0},{1,3},{3,5},{5,7},{7,1},{8,10},{10,12},{12... | collective-permute-start | bytes 1572872 | tf_op jit(solution)/shard_map/ppermute | solution.py:651
  104.7 23.1 %collective-permute-start.13 = (f32[32,32,128]{2,1,0:T(8,128)}, f32[32,32,128]{2,1,0:T(8,128)S(1)}, u32[]{:S(2)}, u32[]{:S(2)}) collective-permute-start(f32[32,32,128]{2,1,0:T(8,128)} %get-tuple-element.75), channel_id=1, source_target_pairs={{0,6},{2,0},{4,2},{6,4},{1,7},{3,1},{5,3},{7,5},{8,14},{10,8},{12,... | collective-permute-start | bytes 1572872 | tf_op jit(solution)/shard_map/ppermute | solution.py:651
  108.0 32.2 %copy-start.1 = (f32[64,8]{0,1:T(8,128)S(1)}, f32[64,8]{0,1:T(8,128)}, u32[]{:S(2)}) copy-start(f32[64,8]{0,1:T(8,128)} %param.17) | copy-start | bytes 6148
  108.0 32.2 %copy-start.3 = (f32[64,8]{0,1:T(8,128)S(1)}, f32[64,8]{0,1:T(8,128)}, u32[]{:S(2)}) copy-start(f32[64,8]{0,1:T(8,128)} %param.18) | copy-start | bytes 6148
  125.2 1.7 %collective-permute-start.10 = (f32[512,128]{1,0:T(8,128)}, f32[512,128]{1,0:T(8,128)S(1)}, u32[]{:S(2)}, u32[]{:S(2)}) collective-permute-start(f32[512,128]{1,0:T(8,128)} %get-tuple-element.71), channel_id=1, source_target_pairs={{0,1},{1,0},{2,3},{3,2},{4,5},{5,4},{6,7},{7,6},{8,9},{9,8},{10,11... | collective-permute-start | bytes 786440 | tf_op jit(solution)/shard_map/ppermute | solution.py:643
  125.2 2.1 %collective-permute-start.9 = (f32[512,128]{1,0:T(8,128)}, f32[512,128]{1,0:T(8,128)S(1)}, u32[]{:S(2)}, u32[]{:S(2)}) collective-permute-start(f32[512,128]{1,0:T(8,128)} %get-tuple-element.70), channel_id=1, source_target_pairs={{0,1},{1,0},{2,3},{3,2},{4,5},{5,4},{6,7},{7,6},{8,9},{9,8},{10,11... | collective-permute-start | bytes 786440 | tf_op jit(solution)/shard_map/ppermute | solution.py:643
  135.3 20.1 %all-to-all-start.2 = ((f32[32,24,128]{2,1,0:T(8,128)}), f32[32,24,128]{2,1,0:T(8,128)S(1)}, u32[]{:S(2)}, u32[]{:S(2)}) async-start(f32[32,24,128]{2,1,0:T(8,128)} %get-tuple-element.80), calls=%async_computation.2 | async-start | bytes 786432 | tf_op jit(solution)/shard_map/all_to_all | solution.py:655

commit v5 on v3

--- a/solution.py
+++ b/solution.py
@@ -13,6 +13,7 @@
 HEAD_SIZE = 8
 FACTOR_WIDTH = 32
 RES = 32
+SIDE = 4
 SEQ = 128
 
 EPSILON = 1e-05
@@ -41,6 +42,27 @@
 
 def exact_nt(a, b):
     return lax.dot_general(a, b, (((1,), (1,)), ((), ())), preferred_element_type=F32, precision=PRECISE)
+
+
+def near_nn(a, b):
+    a_high, a_low = split(a)
+    b_high, b_low = split(b)
+    return dot_nn(a_high, b_high) + (dot_nn(a_high, b_low) + dot_nn(a_low, b_high))
+
+
+def near_nt(a, b):
+    a_high, a_low = split(a)
+    b_high, b_low = split(b)
+    return dot_nt(
+        jnp.concatenate([a_high, a_high, a_low], axis=1), jnp.concatenate([b_high, b_low, b_high], axis=1)
+    )
+
+
+def pick_nn(values, ones):
+    high, low = split(values)
+    rest = values - high.astype(F32) - low.astype(F32)
+    ones = ones.astype(jnp.bfloat16)
+    return dot_nn(high, ones) + (dot_nn(low, ones) + dot_nn(rest.astype(jnp.bfloat16), ones))
 
 
 def lhs_parts(weight):
@@ -94,7 +116,7 @@
     rows, lanes = row_lane((RES * 8, 64))
     picked = jnp.where(rows % 8 == lanes // 8, over_heads(values), 0.0)
     r, c = row_lane((64, RES * 8))
-    spread = exact_nn(picked, (r % 8 == c % 8).astype(F32))
+    spread = pick_nn(picked, (r % 8 == c % 8).astype(F32))
     rows, lanes = row_lane((RES * 8, RES * 8))
     return jnp.where(rows // 8 == lanes // 8, spread, 0.0)
 
@@ -103,7 +125,7 @@
     rows, lanes = row_lane((RES * 8, RES * 8))
     r, c = row_lane((RES * 8, 128))
     fold = jnp.where((r % 8 == c % 8) & (c < 64), 1.0, 0.0)
-    return exact_nn(jnp.where(rows // 8 == lanes // 8, values, 0.0), fold)
+    return pick_nn(jnp.where(rows // 8 == lanes // 8, values, 0.0), fold)
 
 
 def sum_heads(values):
@@ -150,19 +172,20 @@
 def project_kernel(x0t, m0, slope, key, value_gate, keys, values, gate, m0t, slope_t):
     parts = lhs_parts(value_gate[...])
     for pair in range(RES // 2):
-        m0t[128 * pair : 128 * pair + 128] = m0[:, 128 * pair : 128 * pair + 128].T
-        slope_t[128 * pair : 128 * pair + 128] = slope[:, 128 * pair : 128 * pair + 128].T
-        row = 128 * pair
-        both = jnp.concatenate([x0t[row : row + 64], x0t[row + 64 : row + 128]], axis=1)
+        block = slice(128 * pair, 128 * pair + 128)
+        m0t[block] = m0[:, block].T
+        slope_t[block] = slope[:, block].T
+    for first in range(0, RES, SIDE):
+        both = jnp.concatenate([x0t[64 * i : 64 * i + 64] for i in range(first, first + SIDE)], axis=1)
         found = project(parts, both)
         key_rows = exact_nn(key[...], both)
         gates = jax.nn.sigmoid(found[8:72])
-        for k in range(2):
+        for k in range(SIDE):
+            i = first + k
             lanes = slice(SEQ * k, SEQ * k + SEQ)
-            head = 8 * (2 * pair + k)
-            keys[head : head + 8] = key_rows[:, lanes]
-            values[head : head + 8] = found[0:8, lanes]
-            gate[row + 64 * k : row + 64 * k + 64] = gates[:, lanes]
+            keys[8 * i : 8 * i + 8] = key_rows[:, lanes]
+            values[8 * i : 8 * i + 8] = found[0:8, lanes]
+            gate[64 * i : 64 * i + 64] = gates[:, lanes]
 
 
 def score_kernel(got, keys, values, present, asking, weights, local, counts, query_blocks, send):
@@ -181,7 +204,7 @@
     total = jnp.sum(raw, axis=1, keepdims=True)
     rows, lanes = row_lane((RES * 8, 64))
     own_head = rows % 8 == lanes // 8
-    weighted = sum_heads(jnp.where(own_head, fold_blocks(exact_nt(raw, values[...]))[:, :64], 0.0))
+    weighted = sum_heads(jnp.where(own_head, fold_blocks(near_nt(raw, values[...]))[:, :64], 0.0))
     send_all(send, slice(0, 16), pack(weighted))
     rows, lanes = row_lane((RES * 8, 16))
     stats = jnp.where(lanes == rows % 8, top, jnp.where(lanes == 8 + rows % 8, total, 0.0))
@@ -215,7 +238,7 @@
         spread = jnp.where(rows[:, :64] % 8 == lanes[:, :64] // 8, spread, 0.0)
         moments.append(jnp.sum(spread.reshape(half * 8, 8, 64), axis=1))
     moments = jnp.concatenate(moments, axis=0)
-    firsts = fold_blocks(exact_nt(raw, keys[...]))
+    firsts = fold_blocks(near_nt(raw, keys[...]))
     rows, lanes = row_lane((RES * 8, 64))
     rest = jnp.where(lanes < 8, firsts[:, :64], jnp.where(lanes == 8, top, jnp.where(lanes == 9, total, 0.0)))
     block = jnp.concatenate([moments, rest], axis=1)
@@ -259,10 +282,10 @@
     mixing_parts = lhs_parts(mixing[...])
     factor_parts = lhs_parts(factors[...])
     arrive()
-    for pair in range(RES // 2):
+    for first in range(0, RES, SIDE):
         shown, used, base = [], [], []
-        for k in range(2):
-            i = 2 * pair + k
+        for k in range(SIDE):
+            i = first + k
             rows = slice(64 * i, 64 * i + 64)
             use = gate[rows] * heads_t[:, i : i + 1]
             mixed[rows] = use
@@ -274,8 +297,8 @@
         scale = lax.rsqrt(jnp.mean(center * center, axis=0, keepdims=True) + EPSILON)
         normed = center * scale
         found = project(factor_parts, normed) * jnp.concatenate(shown, axis=1)
-        for k in range(2):
-            i = 2 * pair + k
+        for k in range(SIDE):
+            i = first + k
             lanes = slice(SEQ * k, SEQ * k + SEQ)
             x1t[64 * i : 64 * i + 64] = normed[:, lanes]
             inverse_mid[i : i + 1] = scale[:, lanes]
@@ -295,10 +318,10 @@
     mixing_parts = lhs_parts(mixing_back[...])
     ones = jnp.ones((16, SEQ), jnp.bfloat16)
     sums = []
-    for pair in range(RES // 2):
+    for first in range(0, RES, SIDE):
         grads = []
-        for k in range(2):
-            i = 2 * pair + k
+        for k in range(SIDE):
+            i = first + k
             rows = slice(32 * i, 32 * i + 32)
             left_far = left_far_0 if i < RES // 2 else left_far_1
             near = slice(32 * (i % 16), 32 * (i % 16) + 32)
@@ -307,26 +330,25 @@
             )
             grads.append(both * present[i : i + 1])
         mid_in = project(parts, jnp.concatenate(grads, axis=1))
-        rows = slice(128 * pair, 128 * pair + 128)
-        normed = jnp.concatenate([x1t[128 * pair : 128 * pair + 64], x1t[128 * pair + 64 : 128 * pair + 128]], axis=1)
-        scale = jnp.concatenate([inverse_mid[2 * pair : 2 * pair + 1], inverse_mid[2 * pair + 1 : 2 * pair + 2]], axis=1)
+        group = range(first, first + SIDE)
+        normed = jnp.concatenate([x1t[64 * i : 64 * i + 64] for i in group], axis=1)
+        scale = jnp.concatenate([inverse_mid[i : i + 1] for i in group], axis=1)
         back = scale * (
             mid_in
             - jnp.mean(mid_in, axis=0, keepdims=True)
             - normed * jnp.mean(mid_in * normed, axis=0, keepdims=True)
         )
-        back = back + jnp.concatenate(
-            [slope_t[128 * pair : 128 * pair + 64], slope_t[128 * pair + 64 : 128 * pair + 128]], axis=1
-        )
+        back = back + jnp.concatenate([slope_t[64 * i : 64 * i + 64] for i in group], axis=1)
         grad = project(mixing_parts, back)
         gated = []
-        for k in range(2):
+        for k in range(SIDE):
             lanes = slice(SEQ * k, SEQ * k + SEQ)
-            rows = slice(128 * pair + 64 * k, 128 * pair + 64 * k + 64)
+            rows = slice(64 * (first + k), 64 * (first + k) + 64)
             mid[rows] = back[:, lanes]
             out_grad[rows] = grad[:, lanes]
             gated.append(grad[:, lanes] * gate[rows])
-        sums.append(sum_lanes_01(ones, jnp.concatenate(gated, axis=0)))
+        high, low = split(jnp.concatenate(gated, axis=0))
+        sums.append(dot_nt(ones, high) + dot_nt(ones, low))
     sums = [jnp.concatenate([part, part], axis=0) for part in sums]
     send_all(send, slice(0, 16), pack(own_blocks(jnp.concatenate(sums, axis=1))))
     send_all(send, slice(16, 16 + moments.shape[0]), moments[...])
@@ -334,14 +356,14 @@
 
 def gate_back_kernel(out_grad, mixed, gate, filter_weight, x_grad):
     parts = lhs_parts(filter_weight[...])
-    for pair in range(RES // 2):
+    for first in range(0, RES, SIDE):
         both = []
-        for k in range(2):
-            rows = slice(128 * pair + 64 * k, 128 * pair + 64 * k + 64)
+        for i in range(first, first + SIDE):
+            rows = slice(64 * i, 64 * i + 64)
             both.append(out_grad[rows] * mixed[rows] * (1.0 - gate[rows]))
         found = project(parts, jnp.concatenate(both, axis=1))
-        for k in range(2):
-            x_grad[128 * pair + 64 * k : 128 * pair + 64 * k + 64] = found[:, SEQ * k : SEQ * k + SEQ]
+        for k in range(SIDE):
+            x_grad[64 * (first + k) : 64 * (first + k) + 64] = found[:, SEQ * k : SEQ * k + SEQ]
 
 
 def finish_kernel(
@@ -353,7 +375,7 @@
     own_head = rows % 8 == lanes // 8
     along = jnp.sum(jnp.where(own_head, over_heads(att_grad * attended[...]), 0.0), axis=1, keepdims=True)
     r, c = row_lane((64, 64))
-    spread = exact_nn(jnp.where(own_head, over_heads(att_grad), 0.0), (r % 8 == c // 8).astype(F32))
+    spread = pick_nn(jnp.where(own_head, over_heads(att_grad), 0.0), (r % 8 == c // 8).astype(F32))
     both = jnp.concatenate([spread * moments[:, :64], -along * moments[:, 64:]], axis=1)
     r, c = row_lane((128, 64))
     query_grad = exact_nn(both, jnp.where((r < 72) & (r % 8 == c % 8), 1.0, 0.0))
@@ -361,20 +383,20 @@
     mean_grad = (exact_nt(query_grad, asking[...]) / counts[:, :64]).T
 
     blocks = head_blocks(att_grad)
-    score_grad = probs[...] * (exact_nn(blocks, values[...]) - along)
-    key_grad = exact_nn(query_blocks[...].T, score_grad)
-    value_grad = exact_nn(blocks.T, probs[...])
+    score_grad = probs[...] * (near_nn(blocks, values[...]) - along)
+    key_grad = near_nn(query_blocks[...].T, score_grad)
+    value_grad = near_nn(blocks.T, probs[...])
     parts = lhs_parts(key_value[...])
     arrive()
-    for pair in range(RES // 2):
+    for first in range(0, RES, SIDE):
         both = []
-        for k in range(2):
-            rows = slice(16 * pair + 8 * k, 16 * pair + 8 * k + 8)
+        for i in range(first, first + SIDE):
+            rows = slice(8 * i, 8 * i + 8)
             both.append(jnp.concatenate([key_grad[rows], value_grad[rows]], axis=0))
         found = project(parts, jnp.concatenate(both, axis=1))
         done = []
-        for k in range(2):
-            i = 2 * pair + k
+        for k in range(SIDE):
+            i = first + k
             rows = slice(64 * i, 64 * i + 64)
             grad = partial[rows] + found[:, SEQ * k : SEQ * k + SEQ] + mean_grad[:, i : i + 1] * present[i : i + 1]
             normed = x0t[rows]
@@ -382,7 +404,9 @@
                 grad - jnp.mean(grad, axis=0, keepdims=True) - normed * jnp.mean(grad * normed, axis=0, keepdims=True)
             )
             done.append(mid[rows] + back)
-        out[:, 128 * pair : 128 * pair + 128] = jnp.concatenate(done, axis=0).T
+        for k in range(0, SIDE, 2):
+            column = 64 * (first + k)
+            out[:, column : column + 128] = jnp.concatenate(done[k : k + 2], axis=0).T
 
 
 def whole(shape):
@@ -459,16 +483,17 @@
         total[...] = jnp.zeros_like(total)
 
     near = step < pl.num_programs(0) // 2
-    inverse_column = inverse_count[...].T
     for pair in range(ROWS // 2):
         blocks = []
         for row in (2 * pair, 2 * pair + 1):
             for d in range(4):
                 chip = lax.rem(x + d, 4)
-                scale = inverse_column[32 * d : 32 * d + 32, row : row + 1]
-                blocks.append(scale * jnp.where(near, own_g[row, chip, 0], far_g[row, chip, 0]))
+                blocks.append(jnp.where(near, own_g[row, chip, 0], far_g[row, chip, 0]))
         g_high, g_low = split(jnp.concatenate(blocks, axis=0))
         grads = dot_nt(weights[...], jnp.concatenate([g_high, g_high, g_low], axis=1))
+        grads = grads * jnp.concatenate(
+            [inverse_count[2 * pair : 2 * pair + 1], inverse_count[2 * pair + 1 : 2 * pair + 2]], axis=1
+        )
         grads_high, grads_low = split(grads)
         for k in range(2):
             row = (2 * pair + k) * FACTOR_WIDTH
@@ -527,7 +552,14 @@
         compiler_params=pltpu.CompilerParams(vmem_limit_bytes=48 * 2**20),
         cost_estimate=pl.CostEstimate(flops=COST, bytes_accessed=COST, transcendentals=0),
         name="right_products",
-    )(place, pair_grad, far_grad, *[pltpu.with_memory_space_constraint(part, pltpu.HBM) for part in (inverse_count, weight, left)], left_far)
+    )(
+        place,
+        *[
+            pltpu.with_memory_space_constraint(part, pltpu.HBM)
+            for part in (pair_grad, far_grad, inverse_count, weight, left)
+        ],
+        left_far,
+    )
 
 
 def left_kernel(high, low, right_0, right_1, right_2, right_3, own, far_0, far_1, weights):

time: 165 us -> 159 us (0.964)
  Pallas kernels: 79.8 us -> 76 us
  local copies, waits for them, and re-layouts: 9.29 us -> 7.1 us
    pallas_call x8, Pallas kernels: 37.9 us -> 35.2 us  [call(): pl.pallas_call(functools.partial(staged, kernel, (len(operands), len(shap...]
    unnamed x15 -> x13, local copies, waits for them, and re-layouts: 6.98 us -> 4.79 us
  transfers between devices with their start and end apart: 17 -> 17, of which waited for: 8 -> 8; matrix products, arithmetic and copies ran while one was open for 4% -> 4% of each run, Pallas kernels for 32% -> 33%
where the time goes in v5:
time: 159 us; the launch traced here: 158 us
  Pallas kernels  76 us (48%)
  waiting for transfers between devices  37.1 us (23%)
  starting transfers between devices  36.1 us (23%)
  local copies, waits for them, and re-layouts  7.1 us (4%)
    pallas_call x8, Pallas kernels, call(): pl.pallas_call(functools.partial(staged, kernel, (len(operands), len(shap...  35.2 us
    all_to_all x3, waiting for transfers between devices, exchange(): return lax.all_to_all(send, 'seq', 0, 0, tiled=True)  33 us
    pallas_call x1, Pallas kernels, right_products(): pl.pallas_call(right_kernel, grid_spec=grid_spec, out_shape=[pltpu.HBM((F...  23.5 us
    all_to_all x3, starting transfers between devices, exchange(): return lax.all_to_all(send, 'seq', 0, 0, tiled=True)  21 us
    pallas_call x1, Pallas kernels, left_products(): pl.pallas_call(left_kernel, grid=(steps,), in_specs=[rows, rows] + [whole...  17.2 us
    ppermute x6, starting transfers between devices, fetch_chip(): lax.ppermute(values, 'x', [((i + distance) % 4, i) for i in range(4)])  7.16 us
    ppermute x3, starting transfers between devices, send_chip(): lax.ppermute(values, 'x', [(i, (i + distance) % 4) for i in range(4)])  7.1 us
    unnamed x13, local copies, waits for them, and re-layouts  4.79 us
  transfers between devices with their start and end apart: 17, of which 8 were waited for; matrix products, arithmetic and copies ran while one was open for 4% of the time, Pallas kernels for 33%

profile of v5, /device:TPU:32, one launch (start us, length us, event | category | flops | bytes accessed | tf_op | source)
XLA Modules:
  0.0 157.5 jit_solution(16776569673474906502)
XLA Ops:
  0.0 0.8 copy.27.refs_1_
  0.8 0.0 copy-start.2
  0.8 0.1 collective-permute-start
  0.9 2.8 %collective-permute-start.1 = (s32[128,32]{1,0:T(8,128)S(1)}, s32[128,32]{1,0:T(8,128)S(1)}, u32[]{:S(2)}, u32[]{:S(2)}) collective-permute-start(s32[128,32]{1,0:T(8,128)S(1)} %copy.27.refs_1_), channel_id=1, source_target_pairs={{2,0},{4,2},{6,4},{0,6},{3,1},{5,3},{7,5},{1,7},{10,8},{12,10},{14... | collective-permute-start | bytes 49160 | tf_op jit(solution)/shard_map/ppermute | solution.py:628
  3.8 0.8 collective-permute-start.2
  4.6 0.9 collective-permute-start.3
  5.4 0.0 copy-done.2
  5.4 3.1 %norm_kernel.1 = (f32[2048,128]{1,0:T(8,128)}, f32[32,128]{1,0:T(8,128)}, f32[32,128]{1,0:T(8,128)}, f32[32,24,128]{2,1,0:T(8,128)}) custom-call(f32[128,2048]{1,0:T(8,128)} %refs_1_.3, s32[128,32]{1,0:T(8,128)} %copy-done.2), custom_call_target="tpu_custom_call" | custom-call | flops 100000000 | bytes 2539520 | tf_op jit(solution)/shard_map/norm_kernel/pallas_call | solution.py:446
  8.6 0.0 collective-permute-done.refs_2_
  8.6 0.0 collective-permute-done.1.refs_3_
  8.6 1.5 collective-permute-done.2.refs_4_
  10.1 0.7 collective-permute-done.3.refs_5_
  10.8 2.0 %pair_kernel.1 = f32[32,24,128]{2,1,0:T(8,128)} custom-call(f32[32,24,128]{2,1,0:T(8,128)} %get-tuple-element.48.refs_0_, s32[128,32]{1,0:T(8,128)} %copy-done.2, s32[128,32]{1,0:T(8,128)S(1)} %collective-permute-done.refs_2_, s32[128,32]{1,0:T(8,128)S(1)} %collective-permute-done.1.refs_3_, s32[128,32]{1,0:T(8,128)S(1)} %collective-permute-done.2.refs_4_, ...), custom_call_target="tpu_custom_call" | custom-call | flops 100000000 | bytes 868352 | tf_op jit(solution)/shard_map/pair_kernel/pallas_call | solution.py:446
  12.9 0.1 collective-permute-start.4
  13.0 11.4 %all-to-all-start = ((f32[32,24,128]{2,1,0:T(8,128)}), f32[32,24,128]{2,1,0:T(8,128)S(1)}, u32[]{:S(2)}, u32[]{:S(2)}) async-start(f32[32,24,128]{2,1,0:T(8,128)} %pair_kernel.1), calls=%async_computation | async-start | bytes 786432 | tf_op jit(solution)/shard_map/all_to_all | solution.py:636
  24.4 2.2 %copy.33 = f32[32,32,128]{2,0,1:T(8,128)} copy(f32[32,32,128]{2,1,0:T(8,128)} %bitcast.18) | data formatting | bytes 1048576 | tf_op jit(solution)/shard_map/reshape | solution.py:662
  26.5 0.8 copy.34
  27.3 0.1 pad_add_fusion.place
  27.4 0.7 maximum_bitcast_fusion.refs_4_
  28.1 0.0 copy-start
  28.1 0.7 copy-done
  28.8 4.7 %project_kernel.1 = (f32[256,128]{1,0:T(8,128)}, f32[256,128]{1,0:T(8,128)}, f32[2048,128]{1,0:T(8,128)}, f32[2048,128]{1,0:T(8,128)}, f32[2048,128]{1,0:T(8,128)}) custom-call(f32[2048,128]{1,0:T(8,128)} %get-tuple-element.54.refs_0_.refs_11_, f32[128,2048]{1,0:T(8,128)} %refs_1_.3, f32[128,2048]{1,0:T(8,128)} %refs_2_.1, f32[8,64]{1,0:T(8,128)S(1)} %bitcast.15, ...), custom_call_target="tpu_custom_call" | custom-call | flops 100000000 | bytes 6574080 | tf_op jit(solution)/shard_map/project_kernel/pallas_call | solution.py:446
  33.5 6.4 %all-to-all-done.refs_0_ = f32[32,24,128]{2,1,0:T(8,128)S(1)} async-done(((f32[32,24,128]{2,1,0:T(8,128)}), f32[32,24,128]{2,1,0:T(8,128)S(1)}, u32[]{:S(2)}, u32[]{:S(2)}) %all-to-all-start) | async-done | bytes 393248 | tf_op jit(solution)/shard_map/all_to_all | solution.py:636
  39.9 0.0 collective-permute-done.4
  39.9 4.8 %score_kernel.1 = (f32[256,128]{1,0:T(8,128)}, f32[32,16]{1,0:T(8,128)}, f32[32,128]{1,0:T(8,128)}, f32[256,256]{1,0:T(8,128)}, f32[32,32,128]{2,1,0:T(8,128)}) custom-call(f32[32,24,128]{2,1,0:T(8,128)S(1)} %all-to-all-done.refs_0_, f32[256,128]{1,0:T(8,128)} %get-tuple-element.55.refs_1_.refs_3_, f32[256,128]{1,0:T(8,128)} %get-tuple-element.56.refs_2_.refs_4_, ...), custom_call_target="tpu_custom_call" | custom-call | flops 100000000 | bytes 1624064 | tf_op jit(solution)/shard_map/score_kernel/pallas_call | solution.py:446
  44.7 4.8 %all-to-all-start.1 = ((f32[32,32,128]{2,1,0:T(8,128)}), f32[32,32,128]{2,1,0:T(8,128)S(1)}, u32[]{:S(2)}, u32[]{:S(2)}) async-start(f32[32,32,128]{2,1,0:T(8,128)} %get-tuple-element.58), calls=%async_computation.1 | async-start | bytes 1048576 | tf_op jit(solution)/shard_map/all_to_all | solution.py:636
  49.5 0.8 copy.36
  50.3 0.8 copy.37
  51.1 0.1 fusion
  51.2 0.1 copy.38.refs_7_
  51.3 0.8 copy.35
  52.1 14.9 %all-to-all-done.1.refs_0_ = f32[32,32,128]{2,1,0:T(8,128)S(1)} async-done(((f32[32,32,128]{2,1,0:T(8,128)}), f32[32,32,128]{2,1,0:T(8,128)S(1)}, u32[]{:S(2)}, u32[]{:S(2)}) %all-to-all-start.1) | async-done | bytes 524320 | tf_op jit(solution)/shard_map/all_to_all | solution.py:636
  67.1 5.7 %attend_kernel.1 = (f32[256,128]{1,0:T(8,128)}, f32[32,64]{1,0:T(8,128)}, f32[2048,128]{1,0:T(8,128)}, f32[2048,128]{1,0:T(8,128)}, f32[32,128]{1,0:T(8,128)}, /...) custom-call(f32[32,32,128]{2,1,0:T(8,128)S(1)} %all-to-all-done.1.refs_0_, ...), custom_call_target="tpu_custom_call" | custom-call | flops 100000000 | bytes 6141952 | tf_op jit(solution)/shard_map/attend_kernel/pallas_call | solution.py:446
  72.8 0.1 collective-permute-start.5
  72.9 0.8 collective-permute-start.6
  73.7 1.1 collective-permute-start.7
  74.9 0.7 collective-permute-start.8
  75.6 0.0 collective-permute-done.5.left_far
  75.6 23.5 %right_products.1 = (bf16[32,2048,128]{2,1,0:T(8,128)(2,1)}, bf16[32,2048,128]{2,1,0:T(8,128)(2,1)}, f32[32,32,128]{2,1,0:T(8,128)}, f32[32,32,128]{2,1,0:T(8,12...) custom-call(s32[2]{0:T(128)S(1)} %pad_add_fusion.place, f32[32,4,2,32,128]{4,3,2,1,0:T(8,128)} %bitcast.16, ...), custom_call_target="tpu_custom_call" | custom-call | flops 1000 | bytes 1000 | tf_op jit(solution)/shard_map/right_products/pallas_call | solution.py:544
  99.1 3.9 %collective-permute-start.11 = (f32[32,32,128]{2,1,0:T(8,128)}, f32[32,32,128]{2,1,0:T(8,128)S(1)}, u32[]{:S(2)}, u32[]{:S(2)}) collective-permute-start(f32[32,32,128]{2,1,0:T(8,128)} %get-tuple-element.73), channel_id=1, source_target_pairs={{0,4},{2,6},{4,0},{6,2},{1,5},{3,7},{5,1},{7,3},{8,12},{10,14},{12... | collective-permute-start | bytes 1572872 | tf_op jit(solution)/shard_map/ppermute | solution.py:632
  103.0 0.0 collective-permute-start.12
  103.0 0.0 collective-permute-done.6.right_1
  103.0 3.2 %collective-permute-start.13 = (f32[32,32,128]{2,1,0:T(8,128)}, f32[32,32,128]{2,1,0:T(8,128)S(1)}, u32[]{:S(2)}, u32[]{:S(2)}) collective-permute-start(f32[32,32,128]{2,1,0:T(8,128)} %get-tuple-element.75), channel_id=1, source_target_pairs={{0,6},{2,0},{4,2},{6,4},{1,7},{3,1},{5,3},{7,5},{8,14},{10,8},{12,... | collective-permute-start | bytes 1572872 | tf_op jit(solution)/shard_map/ppermute | solution.py:632
  106.2 0.0 collective-permute-done.7.right_2
  106.2 0.0 collective-permute-done.8.right_3
  106.2 0.0 copy-start.1
  106.2 0.0 copy-start.3
  106.2 17.2 %left_products.1 = (f32[1024,128]{1,0:T(8,128)}, f32[512,128]{1,0:T(8,128)}, f32[512,128]{1,0:T(8,128)}) custom-call(bf16[32,2048,128]{2,1,0:T(8,128)(2,1)} %get-tuple-element.66.high, bf16[32,2048,128]{2,1,0:T(8,128)(2,1)} %get-tuple-element.67.low, f32[32,32,128]{2,1,0:T(8,128)} %get-tuple-element.68.right_0, ...), custom_call_target="tpu_custom_call" | custom-call | flops 1000 | bytes 1000 | tf_op jit(solution)/shard_map/left_products/pallas_call | solution.py:605
  123.4 0.0 collective-permute-start.10
  123.5 0.5 collective-permute-start.9
  124.0 0.1 pad_maximum_fusion.refs_13_
  124.0 1.2 collective-permute-done.10.refs_2_
  125.2 0.4 collective-permute-done.9.refs_1_
  125.6 0.0 collective-permute-done.11.refs_4_
  125.6 0.3 collective-permute-done.12.refs_5_
  125.9 0.0 collective-permute-done.13.refs_6_
  125.9 6.0 %middle_kernel.1 = (f32[2048,128]{1,0:T(8,128)}, f32[2048,128]{1,0:T(8,128)}, f32[32,24,128]{2,1,0:T(8,128)}) custom-call(f32[1024,128]{1,0:T(8,128)} %get-tuple-element.69.refs_0_, f32[512,128]{1,0:T(8,128)S(1)} %collective-permute-done.9.refs_1_, f32[512,128]{1,0:T(8,128)S(1)} %collective-permute-done.10.refs_2_, ...), custom_call_target="tpu_custom_call" | custom-call | flops 100000000 | bytes 8851456 | tf_op jit(solution)/shard_map/middle_kernel/pallas_call | solution.py:446
  131.9 4.9 %all-to-all-start.2 = ((f32[32,24,128]{2,1,0:T(8,128)}), f32[32,24,128]{2,1,0:T(8,128)S(1)}, u32[]{:S(2)}, u32[]{:S(2)}) async-start(f32[32,24,128]{2,1,0:T(8,128)} %get-tuple-element.80), calls=%async_computation.2 | async-start | bytes 786432 | tf_op jit(solution)/shard_map/all_to_all | solution.py:636
  136.7 0.0 copy-done.1
  136.7 0.0 copy-done.3
  136.8 0.1 copy.39.refs_7_
  136.8 3.4 %gate_back_kernel.1.refs_6_ = f32[2048,128]{1,0:T(8,128)} custom-call(f32[2048,128]{1,0:T(8,128)} %get-tuple-element.84.refs_0_, f32[2048,128]{1,0:T(8,128)} %get-tuple-element.85.refs_1_, f32[2048,128]{1,0:T(8,128)} %get-tuple-element.62.refs_4_.refs_12_.refs_2_, f32[64,64]{1,0:T(8,128)} %refs_3_.1), custom_call_target="tpu_custom_call" | custom-call | flops 100000000 | bytes 4210688 | tf_op jit(solution)/shard_map/gate_back_kernel/pallas_call | solution.py:446
  140.2 11.7 %all-to-all-done.2.refs_0_ = f32[32,24,128]{2,1,0:T(8,128)S(1)} async-done(((f32[32,24,128]{2,1,0:T(8,128)}), f32[32,24,128]{2,1,0:T(8,128)S(1)}, u32[]{:S(2)}, u32[]{:S(2)}) %all-to-all-start.2) | async-done | bytes 393248 | tf_op jit(solution)/shard_map/all_to_all | solution.py:636
  151.9 5.4 %finish_kernel.1 = f32[128,2048]{1,0:T(8,128)} custom-call(f32[32,24,128]{2,1,0:T(8,128)S(1)} %all-to-all-done.2.refs_0_, f32[32,64]{1,0:T(8,128)} %get-tuple-element.81.refs_1_, f32[256,128]{1,0:T(8,128)} %get-tuple-element.82.refs_2_, f32[256,128]{1,0:T(8,128)} %get-tuple-element.55.refs_1_.refs_3_, f32[256,128]{1,0:T(8,128)} %get-tuple-element.56.refs_2_.refs_4_, ...), custom_call_target="tpu_custom_call" | custom-call | flops 100000000 | bytes 5320704 | tf_op jit(solution)/shard_map/finish_kernel/pallas_call | solution.py:446
  (1 shorter events, 0.0 us)
Async XLA Ops:
  0.8 4.6 %copy-start.2 = (s32[128,32]{1,0:T(8,128)}, s32[128,32]{1,0:T(8,128)S(1)}, u32[]{:S(2)}) copy-start(s32[128,32]{1,0:T(8,128)S(1)} %copy.27.refs_1_) | copy-start | bytes 49156
  0.8 7.8 %collective-permute-start = (s32[128,32]{1,0:T(8,128)S(1)}, s32[128,32]{1,0:T(8,128)S(1)}, u32[]{:S(2)}, u32[]{:S(2)}) collective-permute-start(s32[128,32]{1,0:T(8,128)S(1)} %copy.27.refs_1_), channel_id=1, source_target_pairs={{0,1},{1,0},{2,3},{3,2},{4,5},{5,4},{6,7},{7,6},{8,9},{9,8},{10,11... | collective-permute-start | bytes 49160 | tf_op jit(solution)/shard_map/ppermute | solution.py:624
  0.9 7.7 %collective-permute-start.1 = (s32[128,32]{1,0:T(8,128)S(1)}, s32[128,32]{1,0:T(8,128)S(1)}, u32[]{:S(2)}, u32[]{:S(2)}) collective-permute-start(s32[128,32]{1,0:T(8,128)S(1)} %copy.27.refs_1_), channel_id=1, source_target_pairs={{2,0},{4,2},{6,4},{0,6},{3,1},{5,3},{7,5},{1,7},{10,8},{12,10},{14... | collective-permute-start | bytes 49160 | tf_op jit(solution)/shard_map/ppermute | solution.py:628
  3.8 6.4 %collective-permute-start.2 = (s32[128,32]{1,0:T(8,128)S(1)}, s32[128,32]{1,0:T(8,128)S(1)}, u32[]{:S(2)}, u32[]{:S(2)}) collective-permute-start(s32[128,32]{1,0:T(8,128)S(1)} %copy.27.refs_1_), channel_id=1, source_target_pairs={{4,0},{6,2},{0,4},{2,6},{5,1},{7,3},{1,5},{3,7},{12,8},{14,10},{8,... | collective-permute-start | bytes 49160 | tf_op jit(solution)/shard_map/ppermute | solution.py:628
  4.6 6.3 %collective-permute-start.3 = (s32[128,32]{1,0:T(8,128)S(1)}, s32[128,32]{1,0:T(8,128)S(1)}, u32[]{:S(2)}, u32[]{:S(2)}) collective-permute-start(s32[128,32]{1,0:T(8,128)S(1)} %copy.27.refs_1_), channel_id=1, source_target_pairs={{6,0},{0,2},{2,4},{4,6},{7,1},{1,3},{3,5},{5,7},{14,8},{8,10},{10,... | collective-permute-start | bytes 49160 | tf_op jit(solution)/shard_map/ppermute | solution.py:628
  12.9 27.0 %collective-permute-start.4 = (f32[32,256,128]{2,1,0:T(8,128)}, f32[32,256,128]{2,1,0:T(8,128)}, u32[]{:S(2)}, u32[]{:S(2)}) collective-permute-start(f32[32,256,128]{2,1,0:T(8,128)} %param.14), channel_id=1, source_target_pairs={{0,1},{1,0},{2,3},{3,2},{4,5},{5,4},{6,7},{7,6},{8,9},{9,8},{10,11... | collective-permute-start | bytes 12582920 | tf_op jit(solution)/shard_map/ppermute | solution.py:624
  13.0 26.9 %all-to-all-start = ((f32[32,24,128]{2,1,0:T(8,128)}), f32[32,24,128]{2,1,0:T(8,128)S(1)}, u32[]{:S(2)}, u32[]{:S(2)}) async-start(f32[32,24,128]{2,1,0:T(8,128)} %pair_kernel.1), calls=%async_computation | async-start | bytes 786432 | tf_op jit(solution)/shard_map/all_to_all | solution.py:636
  28.1 0.7 copy-start
  44.7 22.3 %all-to-all-start.1 = ((f32[32,32,128]{2,1,0:T(8,128)}), f32[32,32,128]{2,1,0:T(8,128)S(1)}, u32[]{:S(2)}, u32[]{:S(2)}) async-start(f32[32,32,128]{2,1,0:T(8,128)} %get-tuple-element.58), calls=%async_computation.1 | async-start | bytes 1048576 | tf_op jit(solution)/shard_map/all_to_all | solution.py:636
  72.8 2.7 %collective-permute-start.5 = (f32[1024,128]{1,0:T(8,128)}, f32[1024,128]{1,0:T(8,128)S(1)}, u32[]{:S(2)}, u32[]{:S(2)}) collective-permute-start(f32[1024,128]{1,0:T(8,128)} %get-tuple-element.65.left), channel_id=1, source_target_pairs={{0,1},{1,0},{2,3},{3,2},{4,5},{5,4},{6,7},{7,6},{8,9},{9,8},{10,11... | collective-permute-start | bytes 1572872 | tf_op jit(solution)/shard_map/ppermute | solution.py:624
  72.9 30.1 %collective-permute-start.6 = (f32[32,32,128]{2,1,0:T(8,128)}, f32[32,32,128]{2,1,0:T(8,128)S(1)}, u32[]{:S(2)}, u32[]{:S(2)}) collective-permute-start(f32[32,32,128]{2,1,0:T(8,128)} %get-tuple-element.68.right_0), channel_id=1, source_target_pairs={{2,0},{4,2},{6,4},{0,6},{3,1},{5,3},{7,5},{1,7},{10,8},{12,10},{14... | collective-permute-start | bytes 1572872 | tf_op jit(solution)/shard_map/ppermute | solution.py:628
  73.7 32.5 %collective-permute-start.7 = (f32[32,32,128]{2,1,0:T(8,128)}, f32[32,32,128]{2,1,0:T(8,128)S(1)}, u32[]{:S(2)}, u32[]{:S(2)}) collective-permute-start(f32[32,32,128]{2,1,0:T(8,128)} %get-tuple-element.68.right_0), channel_id=1, source_target_pairs={{4,0},{6,2},{0,4},{2,6},{5,1},{7,3},{1,5},{3,7},{12,8},{14,10},{8,... | collective-permute-start | bytes 1572872 | tf_op jit(solution)/shard_map/ppermute | solution.py:628
  74.9 31.3 %collective-permute-start.8 = (f32[32,32,128]{2,1,0:T(8,128)}, f32[32,32,128]{2,1,0:T(8,128)S(1)}, u32[]{:S(2)}, u32[]{:S(2)}) collective-permute-start(f32[32,32,128]{2,1,0:T(8,128)} %get-tuple-element.68.right_0), channel_id=1, source_target_pairs={{6,0},{0,2},{2,4},{4,6},{7,1},{1,3},{3,5},{5,7},{14,8},{8,10},{10,... | collective-permute-start | bytes 1572872 | tf_op jit(solution)/shard_map/ppermute | solution.py:628
  99.1 26.5 %collective-permute-start.11 = (f32[32,32,128]{2,1,0:T(8,128)}, f32[32,32,128]{2,1,0:T(8,128)S(1)}, u32[]{:S(2)}, u32[]{:S(2)}) collective-permute-start(f32[32,32,128]{2,1,0:T(8,128)} %get-tuple-element.73), channel_id=1, source_target_pairs={{0,4},{2,6},{4,0},{6,2},{1,5},{3,7},{5,1},{7,3},{8,12},{10,14},{12... | collective-permute-start | bytes 1572872 | tf_op jit(solution)/shard_map/ppermute | solution.py:632
  103.0 22.9 %collective-permute-start.12 = (f32[32,32,128]{2,1,0:T(8,128)}, f32[32,32,128]{2,1,0:T(8,128)S(1)}, u32[]{:S(2)}, u32[]{:S(2)}) collective-permute-start(f32[32,32,128]{2,1,0:T(8,128)} %get-tuple-element.74), channel_id=1, source_target_pairs={{0,2},{2,4},{4,6},{6,0},{1,3},{3,5},{5,7},{7,1},{8,10},{10,12},{12... | collective-permute-start | bytes 1572872 | tf_op jit(solution)/shard_map/ppermute | solution.py:632
  103.0 22.9 %collective-permute-start.13 = (f32[32,32,128]{2,1,0:T(8,128)}, f32[32,32,128]{2,1,0:T(8,128)S(1)}, u32[]{:S(2)}, u32[]{:S(2)}) collective-permute-start(f32[32,32,128]{2,1,0:T(8,128)} %get-tuple-element.75), channel_id=1, source_target_pairs={{0,6},{2,0},{4,2},{6,4},{1,7},{3,1},{5,3},{7,5},{8,14},{10,8},{12,... | collective-permute-start | bytes 1572872 | tf_op jit(solution)/shard_map/ppermute | solution.py:632
  106.2 30.5 %copy-start.1 = (f32[64,8]{0,1:T(8,128)S(1)}, f32[64,8]{0,1:T(8,128)}, u32[]{:S(2)}) copy-start(f32[64,8]{0,1:T(8,128)} %param.17) | copy-start | bytes 6148
  106.2 30.5 %copy-start.3 = (f32[64,8]{0,1:T(8,128)S(1)}, f32[64,8]{0,1:T(8,128)}, u32[]{:S(2)}) copy-start(f32[64,8]{0,1:T(8,128)} %param.18) | copy-start | bytes 6148
  123.4 1.7 %collective-permute-start.10 = (f32[512,128]{1,0:T(8,128)}, f32[512,128]{1,0:T(8,128)S(1)}, u32[]{:S(2)}, u32[]{:S(2)}) collective-permute-start(f32[512,128]{1,0:T(8,128)} %get-tuple-element.71), channel_id=1, source_target_pairs={{0,1},{1,0},{2,3},{3,2},{4,5},{5,4},{6,7},{7,6},{8,9},{9,8},{10,11... | collective-permute-start | bytes 786440 | tf_op jit(solution)/shard_map/ppermute | solution.py:624
  123.5 2.1 %collective-permute-start.9 = (f32[512,128]{1,0:T(8,128)}, f32[512,128]{1,0:T(8,128)S(1)}, u32[]{:S(2)}, u32[]{:S(2)}) collective-permute-start(f32[512,128]{1,0:T(8,128)} %get-tuple-element.70), channel_id=1, source_target_pairs={{0,1},{1,0},{2,3},{3,2},{4,5},{5,4},{6,7},{7,6},{8,9},{9,8},{10,11... | collective-permute-start | bytes 786440 | tf_op jit(solution)/shard_map/ppermute | solution.py:624
  131.9 20.1 %all-to-all-start.2 = ((f32[32,24,128]{2,1,0:T(8,128)}), f32[32,24,128]{2,1,0:T(8,128)S(1)}, u32[]{:S(2)}, u32[]{:S(2)}) async-start(f32[32,24,128]{2,1,0:T(8,128)} %get-tuple-element.80), calls=%async_computation.2 | async-start | bytes 786432 | tf_op jit(solution)/shard_map/all_to_all | solution.py:636

commit v6 on v5

--- a/solution.py
+++ b/solution.py
@@ -137,7 +137,7 @@
 
 
 def norm_kernel(m0, mask, x0t, inverse, present, send):
-    shown = mask[...].astype(F32).T
+    shown = mask[...].astype(F32)
     present[...] = shown
     for pair in range(RES // 2):
         block = m0[:, 128 * pair : 128 * pair + 128].T
@@ -158,10 +158,10 @@
 
 def pair_kernel(sent, mask, mask_core, mask_1, mask_2, mask_3, send):
     send[...] = sent[...]
-    own = mask[...].astype(F32).T.astype(jnp.bfloat16)
-    rows = jnp.concatenate([own, mask_core[...].astype(F32).T.astype(jnp.bfloat16)], axis=0)
+    own = mask[...].astype(F32).astype(jnp.bfloat16)
+    rows = jnp.concatenate([own, mask_core[...].astype(F32).astype(jnp.bfloat16)], axis=0)
     columns = jnp.concatenate(
-        [own] + [part[...].astype(F32).T.astype(jnp.bfloat16) for part in (mask_1, mask_2, mask_3)], axis=0
+        [own] + [part[...].astype(F32).astype(jnp.bfloat16) for part in (mask_1, mask_2, mask_3)], axis=0
     )
     count = dot_nt(rows, columns)
     share = 64 // send.shape[0]
@@ -248,7 +248,7 @@
 
 def attend_kernel(
     got, local, raw, m0t, gate, present, mixing, factors,
-    probs, attended, mixed, x1t, inverse_mid, left, right, inverse_count, moments, scratch, arrive,
+    probs, attended, x1t, inverse_mid, left, right, inverse_count, moments, scratch, arrive,
 ):
     peers = got.shape[0]
     share = 64 // peers
@@ -282,13 +282,12 @@
     mixing_parts = lhs_parts(mixing[...])
     factor_parts = lhs_parts(factors[...])
     arrive()
-    for first in range(0, RES, SIDE):
+    for first in range(0, RES, 2):
         shown, used, base = [], [], []
-        for k in range(SIDE):
+        for k in range(2):
             i = first + k
             rows = slice(64 * i, 64 * i + 64)
             use = gate[rows] * heads_t[:, i : i + 1]
-            mixed[rows] = use
             used.append(use)
             base.append(m0t[rows])
             shown.append(present[i : i + 1])
@@ -297,7 +296,7 @@
         scale = lax.rsqrt(jnp.mean(center * center, axis=0, keepdims=True) + EPSILON)
         normed = center * scale
         found = project(factor_parts, normed) * jnp.concatenate(shown, axis=1)
-        for k in range(SIDE):
+        for k in range(2):
             i = first + k
             lanes = slice(SEQ * k, SEQ * k + SEQ)
             x1t[64 * i : 64 * i + 64] = normed[:, lanes]
@@ -310,7 +309,7 @@
 
 def middle_kernel(
     left_own, left_far_0, left_far_1, right_own, right_1, right_2, right_3, moments, x1t, inverse_mid, present, slope_t, gate,
-    factors_back, mixing_back, mid, out_grad, send, scratch,
+    factors_back, mixing_back, mid, send, scratch,
 ):
     for f in range(FACTOR_WIDTH):
         scratch[32 * f : 32 * f + 32] = (right_own[f] + right_1[f]) + (right_2[f] + right_3[f])
@@ -345,7 +344,6 @@
             lanes = slice(SEQ * k, SEQ * k + SEQ)
             rows = slice(64 * (first + k), 64 * (first + k) + 64)
             mid[rows] = back[:, lanes]
-            out_grad[rows] = grad[:, lanes]
             gated.append(grad[:, lanes] * gate[rows])
         high, low = split(jnp.concatenate(gated, axis=0))
         sums.append(dot_nt(ones, high) + dot_nt(ones, low))
@@ -354,20 +352,27 @@
     send_all(send, slice(16, 16 + moments.shape[0]), moments[...])
 
 
-def gate_back_kernel(out_grad, mixed, gate, filter_weight, x_grad):
+def gate_back_kernel(mid, attended, gate, mixing_back, filter_weight, x0t, inverse, base):
     parts = lhs_parts(filter_weight[...])
+    mixing_parts = lhs_parts(mixing_back[...])
+    heads_t = attended[...].T
     for first in range(0, RES, SIDE):
-        both = []
-        for i in range(first, first + SIDE):
-            rows = slice(64 * i, 64 * i + 64)
-            both.append(out_grad[rows] * mixed[rows] * (1.0 - gate[rows]))
-        found = project(parts, jnp.concatenate(both, axis=1))
+        group = range(first, first + SIDE)
+        above = jnp.concatenate([mid[64 * i : 64 * i + 64] for i in group], axis=1)
+        gates = jnp.concatenate([gate[64 * i : 64 * i + 64] for i in group], axis=1)
+        used = jnp.concatenate([gate[64 * i : 64 * i + 64] * heads_t[:, i : i + 1] for i in group], axis=1)
+        grad = project(parts, project(mixing_parts, above) * used * (1.0 - gates))
+        normed = jnp.concatenate([x0t[64 * i : 64 * i + 64] for i in group], axis=1)
+        scale = jnp.concatenate([inverse[i : i + 1] for i in group], axis=1)
+        total = above + scale * (
+            grad - jnp.mean(grad, axis=0, keepdims=True) - normed * jnp.mean(grad * normed, axis=0, keepdims=True)
+        )
         for k in range(SIDE):
-            x_grad[64 * (first + k) : 64 * (first + k) + 64] = found[:, SEQ * k : SEQ * k + SEQ]
+            base[64 * (first + k) : 64 * (first + k) + 64] = total[:, SEQ * k : SEQ * k + SEQ]
 
 
 def finish_kernel(
-    got, attended, probs, keys, values, query_blocks, partial, key_value, counts, asking, present, x0t, inverse, mid, out, arrive
+    got, attended, probs, keys, values, query_blocks, base, key_value, counts, asking, present, x0t, inverse, out, arrive
 ):
     att_grad = unpack(jnp.sum(got[:, 0:16, :], axis=0))
     moments = got[:, 16:, :].reshape(RES * 8, 128)
@@ -398,12 +403,12 @@
         for k in range(SIDE):
             i = first + k
             rows = slice(64 * i, 64 * i + 64)
-            grad = partial[rows] + found[:, SEQ * k : SEQ * k + SEQ] + mean_grad[:, i : i + 1] * present[i : i + 1]
+            grad = found[:, SEQ * k : SEQ * k + SEQ] + mean_grad[:, i : i + 1] * present[i : i + 1]
             normed = x0t[rows]
             back = inverse[i : i + 1] * (
                 grad - jnp.mean(grad, axis=0, keepdims=True) - normed * jnp.mean(grad * normed, axis=0, keepdims=True)
             )
-            done.append(mid[rows] + back)
+            done.append(base[rows] + back)
         for k in range(0, SIDE, 2):
             column = 64 * (first + k)
             out[:, column : column + 128] = jnp.concatenate(done[k : k + 2], axis=0).T
@@ -657,8 +662,9 @@
     shared = 24 + block + (0 if share == 2 else share)
     x, core = lax.axis_index("x"), lax.axis_index("core")
     place = jnp.stack([x, core]).astype(jnp.int32)
-    mask_core = swap_core(alignment_mask)
-    mask_chips = [fetch_chip(alignment_mask, d) for d in (1, 2, 3)]
+    mask = alignment_mask.T
+    mask_core = swap_core(mask)
+    mask_chips = [fetch_chip(mask, d) for d in (1, 2, 3)]
     weight = pair_weight.reshape(FACTOR_WIDTH, FACTOR_WIDTH, 128).swapaxes(0, 1).reshape(1024, 128)
     value_gate = jnp.concatenate([content_matrix, sigmoid_filter_matrix], axis=1).T
     key_value = jnp.concatenate([key_weight, content_matrix], axis=1)
@@ -666,9 +672,9 @@
 
     flat, heads, stat = (RES * 64, SEQ), (RES * 8, SEQ), (RES, SEQ)
     x0t, inverse, present, send = call(
-        norm_kernel, [flat, stat, stat, (peers, counted, 128)], homolog_features, alignment_mask
-    )
-    (send,) = call(pair_kernel, [(peers, counted, 128)], send, alignment_mask, mask_core, *mask_chips, free=(2, 3, 4, 5))
+        norm_kernel, [flat, stat, stat, (peers, counted, 128)], homolog_features, mask
+    )
+    (send,) = call(pair_kernel, [(peers, counted, 128)], send, mask, mask_core, *mask_chips, free=(2, 3, 4, 5))
     x0t, send, pair_grad = lax.optimization_barrier((x0t, send, pair_update_gradient))
     far_grad = swap_core(pair_grad).reshape(32, 4, 2, 32, 128)
     pair_grad = pair_grad.reshape(32, 4, 2, 32, 128)
@@ -684,9 +690,9 @@
         got, keys, values, present, asking_matrix, free=(0,),
     )
     got = exchange(send)
-    probs, attended, mixed, x1t, inverse_mid, left, right, inverse_count, moments = call(
+    probs, attended, x1t, inverse_mid, left, right, inverse_count, moments = call(
         attend_kernel,
-        [heads, (RES, 64), flat, flat, stat, (RES * 32, SEQ), (FACTOR_WIDTH, RES, SEQ), (64, 128), (block, 128)],
+        [heads, (RES, 64), flat, stat, (RES * 32, SEQ), (FACTOR_WIDTH, RES, SEQ), (64, 128), (block, 128)],
         got, local, raw, m0t, gate, present, final_mixing_matrix.T, factors.T, late=(3, 4), free=(0, 6, 7),
         scratch=[pltpu.VMEM((RES * 32, SEQ), F32)],
     )
@@ -697,18 +703,20 @@
     right_sent = [send_chip(part, d) for d, part in ((2, right_2), (1, right_1), (3, right_3))]
     left_own, *left_far = left_products(high, low, rights)
     left_far = [swap_core(part) for part in left_far]
-    mid, out_grad, send = call(
-        middle_kernel, [flat, flat, (peers, 16 + block, 128)],
+    mid, send = call(
+        middle_kernel, [flat, (peers, 16 + block, 128)],
         left_own, *left_far, right_own, *right_sent,
         moments, x1t, inverse_mid, present, slope_t, gate, factors, final_mixing_matrix, free=(1, 2, 4, 5, 6, 13),
         scratch=[pltpu.VMEM((RES * 32, SEQ), F32)],
     )
     got = exchange(send)
-    (gate_grad,) = call(gate_back_kernel, [flat], out_grad, mixed, gate, sigmoid_filter_matrix)
+    (base,) = call(
+        gate_back_kernel, [flat], mid, attended, gate, final_mixing_matrix, sigmoid_filter_matrix, x0t, inverse
+    )
     (out,) = call(
         finish_kernel, [(SEQ, RES * 64)],
-        got, attended, probs, keys, values, query_blocks, gate_grad, key_value, counts, asking_matrix,
-        present, x0t, inverse, mid, late=(6, 11, 13), free=(0, 7),
+        got, attended, probs, keys, values, query_blocks, base, key_value, counts, asking_matrix,
+        present, x0t, inverse, late=(6, 11), free=(0, 7),
     )
     return out
 

time: 159 us -> 156 us (0.981)
  waiting for transfers between devices: 37.1 us -> 34.6 us
    all_to_all x3, waiting for transfers between devices: 33 us -> 31.1 us  [exchange(): return lax.all_to_all(send, 'seq', 0, 0, tiled=True)]
    unnamed x13 -> x10, local copies, waits for them, and re-layouts: 4.79 us -> 3.97 us
  transfers between devices with their start and end apart: 17 -> 17, of which waited for: 8 -> 9; matrix products, arithmetic and copies ran while one was open for 4% -> 4% of each run, Pallas kernels for 33% -> 35%
where the time goes in v6:
time: 156 us; the launch traced here: 155 us
  Pallas kernels  76.5 us (49%)
  starting transfers between devices  35.9 us (23%)
  waiting for transfers between devices  34.6 us (22%)
  local copies, waits for them, and re-layouts  6.28 us (4%)
    pallas_call x8, Pallas kernels, call(): pl.pallas_call(functools.partial(staged, kernel, (len(operands), len(shap...  35.7 us
    all_to_all x3, waiting for transfers between devices, exchange(): return lax.all_to_all(send, 'seq', 0, 0, tiled=True)  31.1 us
    pallas_call x1, Pallas kernels, right_products(): pl.pallas_call(right_kernel, grid_spec=grid_spec, out_shape=[pltpu.HBM((F...  23.5 us
    all_to_all x3, starting transfers between devices, exchange(): return lax.all_to_all(send, 'seq', 0, 0, tiled=True)  21 us
    pallas_call x1, Pallas kernels, left_products(): pl.pallas_call(left_kernel, grid=(steps,), in_specs=[rows, rows] + [whole...  17.2 us
    ppermute x6, starting transfers between devices, fetch_chip(): lax.ppermute(values, 'x', [((i + distance) % 4, i) for i in range(4)])  7.64 us
    ppermute x3, starting transfers between devices, send_chip(): lax.ppermute(values, 'x', [(i, (i + distance) % 4) for i in range(4)])  6.55 us
    unnamed x10, local copies, waits for them, and re-layouts  3.97 us
  transfers between devices with their start and end apart: 17, of which 9 were waited for; matrix products, arithmetic and copies ran while one was open for 4% of the time, Pallas kernels for 35%

profile of v6, /device:TPU:32, one launch (start us, length us, event | category | flops | bytes accessed | tf_op | source)
XLA Modules:
  0.0 154.6 jit_solution(1418589450337553332)
XLA Ops:
  0.0 0.0 collective-permute-start
  0.0 2.8 %collective-permute-start.1 = (s32[32,128]{1,0:T(8,128)}, s32[32,128]{1,0:T(8,128)S(1)}, u32[]{:S(2)}, u32[]{:S(2)}) collective-permute-start(s32[32,128]{1,0:T(8,128)} %bitcast.21), channel_id=1, source_target_pairs={{2,0},{4,2},{6,4},{0,6},{3,1},{5,3},{7,5},{1,7},{10,8},{12,10},{14... | collective-permute-start | bytes 49160 | tf_op jit(solution)/shard_map/ppermute | solution.py:633
  2.8 0.8 collective-permute-start.2
  3.6 0.9 collective-permute-start.3
  4.4 3.1 %norm_kernel.1 = (f32[2048,128]{1,0:T(8,128)}, f32[32,128]{1,0:T(8,128)}, f32[32,128]{1,0:T(8,128)}, f32[32,24,128]{2,1,0:T(8,128)}) custom-call(f32[128,2048]{1,0:T(8,128)} %refs_1_.1, s32[32,128]{1,0:T(8,128)} %bitcast.24), custom_call_target="tpu_custom_call" | custom-call | flops 100000000 | bytes 2539520 | tf_op jit(solution)/shard_map/norm_kernel/pallas_call | solution.py:451
  7.5 0.0 collective-permute-done.refs_2_
  7.5 0.0 collective-permute-done.1.refs_3_
  7.6 0.7 collective-permute-done.2.refs_4_
  8.2 0.5 collective-permute-done.3.refs_5_
  8.7 2.0 %pair_kernel.1 = f32[32,24,128]{2,1,0:T(8,128)} custom-call(f32[32,24,128]{2,1,0:T(8,128)} %get-tuple-element.46.refs_0_, s32[32,128]{1,0:T(8,128)} %bitcast.25, s32[32,128]{1,0:T(8,128)S(1)} %collective-permute-done.refs_2_, s32[32,128]{1,0:T(8,128)S(1)} %collective-permute-done.1.refs_3_, s32[32,128]{1,0:T(8,128)S(1)} %collective-permute-done.2.refs_4_, ...), custom_call_target="tpu_custom_call" | custom-call | flops 100000000 | bytes 868352 | tf_op jit(solution)/shard_map/pair_kernel/pallas_call | solution.py:451
  10.7 0.1 collective-permute-start.4
  10.8 11.4 %all-to-all-start = ((f32[32,24,128]{2,1,0:T(8,128)}), f32[32,24,128]{2,1,0:T(8,128)S(1)}, u32[]{:S(2)}, u32[]{:S(2)}) async-start(f32[32,24,128]{2,1,0:T(8,128)} %pair_kernel.1), calls=%async_computation | async-start | bytes 786432 | tf_op jit(solution)/shard_map/all_to_all | solution.py:641
  22.2 2.1 %copy.21 = f32[32,32,128]{2,0,1:T(8,128)} copy(f32[32,32,128]{2,1,0:T(8,128)} %bitcast.19) | data formatting | bytes 1048576 | tf_op jit(solution)/shard_map/reshape | solution.py:668
  24.3 0.8 copy.22
  25.2 0.1 pad_add_fusion.place
  25.2 0.7 maximum_bitcast_fusion.refs_4_
  25.9 0.0 copy-start
  25.9 0.7 copy-done
  26.6 4.7 %project_kernel.1 = (f32[256,128]{1,0:T(8,128)}, f32[256,128]{1,0:T(8,128)}, f32[2048,128]{1,0:T(8,128)}, f32[2048,128]{1,0:T(8,128)}, f32[2048,128]{1,0:T(8,128)}) custom-call(f32[2048,128]{1,0:T(8,128)} %get-tuple-element.52.refs_0_.refs_5_.refs_11_, f32[128,2048]{1,0:T(8,128)} %refs_1_.1, f32[128,2048]{1,0:T(8,128)} %refs_2_.1, f32[8,64]{1,0:T(8,128)S(1)} %bitcast.16, ...), custom_call_target="tpu_custom_call" | custom-call | flops 100000000 | bytes 6574080 | tf_op jit(solution)/shard_map/project_kernel/pallas_call | solution.py:451
  31.3 6.4 %all-to-all-done.refs_0_ = f32[32,24,128]{2,1,0:T(8,128)S(1)} async-done(((f32[32,24,128]{2,1,0:T(8,128)}), f32[32,24,128]{2,1,0:T(8,128)S(1)}, u32[]{:S(2)}, u32[]{:S(2)}) %all-to-all-start) | async-done | bytes 393248 | tf_op jit(solution)/shard_map/all_to_all | solution.py:641
  37.7 0.0 collective-permute-done.4
  37.7 4.8 %score_kernel.1 = (f32[256,128]{1,0:T(8,128)}, f32[32,16]{1,0:T(8,128)}, f32[32,128]{1,0:T(8,128)}, f32[256,256]{1,0:T(8,128)}, f32[32,32,128]{2,1,0:T(8,128)}) custom-call(f32[32,24,128]{2,1,0:T(8,128)S(1)} %all-to-all-done.refs_0_, f32[256,128]{1,0:T(8,128)} %get-tuple-element.53.refs_1_.refs_3_, f32[256,128]{1,0:T(8,128)} %get-tuple-element.54.refs_2_.refs_4_, ...), custom_call_target="tpu_custom_call" | custom-call | flops 100000000 | bytes 1624064 | tf_op jit(solution)/shard_map/score_kernel/pallas_call | solution.py:451
  42.6 4.8 %all-to-all-start.1 = ((f32[32,32,128]{2,1,0:T(8,128)}), f32[32,32,128]{2,1,0:T(8,128)S(1)}, u32[]{:S(2)}, u32[]{:S(2)}) async-start(f32[32,32,128]{2,1,0:T(8,128)} %get-tuple-element.56), calls=%async_computation.1 | async-start | bytes 1048576 | tf_op jit(solution)/shard_map/all_to_all | solution.py:641
  47.4 0.8 copy.24
  48.2 0.8 copy.25
  49.0 0.1 fusion
  49.0 0.1 copy.26.refs_7_
  49.1 0.8 copy.23
  50.0 14.9 %all-to-all-done.1.refs_0_ = f32[32,32,128]{2,1,0:T(8,128)S(1)} async-done(((f32[32,32,128]{2,1,0:T(8,128)}), f32[32,32,128]{2,1,0:T(8,128)S(1)}, u32[]{:S(2)}, u32[]{:S(2)}) %all-to-all-start.1) | async-done | bytes 524320 | tf_op jit(solution)/shard_map/all_to_all | solution.py:641
  64.9 5.3 %attend_kernel.1 = (f32[256,128]{1,0:T(8,128)}, f32[32,64]{1,0:T(8,128)}, f32[2048,128]{1,0:T(8,128)}, f32[32,128]{1,0:T(8,128)}, f32[1024,128]{1,0:T(8,128)}, /...) custom-call(f32[32,32,128]{2,1,0:T(8,128)S(1)} %all-to-all-done.1.refs_0_, ...), custom_call_target="tpu_custom_call" | custom-call | flops 100000000 | bytes 5093376 | tf_op jit(solution)/shard_map/attend_kernel/pallas_call | solution.py:451
  70.2 0.1 collective-permute-start.5
  70.3 1.5 collective-permute-start.6
  71.8 1.5 collective-permute-start.7
  73.3 0.2 collective-permute-start.8
  73.5 0.0 collective-permute-done.5.left_far
  73.5 23.5 %right_products.1 = (bf16[32,2048,128]{2,1,0:T(8,128)(2,1)}, bf16[32,2048,128]{2,1,0:T(8,128)(2,1)}, f32[32,32,128]{2,1,0:T(8,128)}, f32[32,32,128]{2,1,0:T(8,12...) custom-call(s32[2]{0:T(128)S(1)} %pad_add_fusion.place, f32[32,4,2,32,128]{4,3,2,1,0:T(8,128)} %bitcast.17, ...), custom_call_target="tpu_custom_call" | custom-call | flops 1000 | bytes 1000 | tf_op jit(solution)/shard_map/right_products/pallas_call | solution.py:549
  97.0 3.3 %collective-permute-start.11 = (f32[32,32,128]{2,1,0:T(8,128)}, f32[32,32,128]{2,1,0:T(8,128)S(1)}, u32[]{:S(2)}, u32[]{:S(2)}) collective-permute-start(f32[32,32,128]{2,1,0:T(8,128)} %get-tuple-element.71), channel_id=1, source_target_pairs={{0,4},{2,6},{4,0},{6,2},{1,5},{3,7},{5,1},{7,3},{8,12},{10,14},{12... | collective-permute-start | bytes 1572872 | tf_op jit(solution)/shard_map/ppermute | solution.py:637
  100.3 0.7 collective-permute-start.12
  101.0 0.0 collective-permute-done.6.right_1
  101.0 2.6 %collective-permute-start.13 = (f32[32,32,128]{2,1,0:T(8,128)}, f32[32,32,128]{2,1,0:T(8,128)S(1)}, u32[]{:S(2)}, u32[]{:S(2)}) collective-permute-start(f32[32,32,128]{2,1,0:T(8,128)} %get-tuple-element.73), channel_id=1, source_target_pairs={{0,6},{2,0},{4,2},{6,4},{1,7},{3,1},{5,3},{7,5},{8,14},{10,8},{12,... | collective-permute-start | bytes 1572872 | tf_op jit(solution)/shard_map/ppermute | solution.py:637
  103.6 0.0 collective-permute-done.7.right_2
  103.6 0.0 collective-permute-done.8.right_3
  103.6 0.0 copy-start.1
  103.6 0.0 copy-start.2
  103.6 17.2 %left_products.1 = (f32[1024,128]{1,0:T(8,128)}, f32[512,128]{1,0:T(8,128)}, f32[512,128]{1,0:T(8,128)}) custom-call(bf16[32,2048,128]{2,1,0:T(8,128)(2,1)} %get-tuple-element.64.high, bf16[32,2048,128]{2,1,0:T(8,128)(2,1)} %get-tuple-element.65.low, f32[32,32,128]{2,1,0:T(8,128)} %get-tuple-element.66.right_0, ...), custom_call_target="tpu_custom_call" | custom-call | flops 1000 | bytes 1000 | tf_op jit(solution)/shard_map/left_products/pallas_call | solution.py:610
  120.8 0.0 collective-permute-start.10
  120.8 0.5 collective-permute-start.9
  121.3 0.1 pad_maximum_fusion.refs_13_
  121.4 1.2 collective-permute-done.10.refs_2_
  122.6 0.4 collective-permute-done.9.refs_1_
  122.9 0.0 collective-permute-done.11.refs_4_
  122.9 0.4 collective-permute-done.12.refs_5_
  123.4 0.3 collective-permute-done.13.refs_6_
  123.7 5.7 %middle_kernel.1 = (f32[2048,128]{1,0:T(8,128)}, f32[32,24,128]{2,1,0:T(8,128)}) custom-call(f32[1024,128]{1,0:T(8,128)} %get-tuple-element.67.refs_0_, f32[512,128]{1,0:T(8,128)S(1)} %collective-permute-done.9.refs_1_, f32[512,128]{1,0:T(8,128)S(1)} %collective-permute-done.10.refs_2_, f32[32,32,128]{2,1,0:T(8,128)} %get-tuple-element.70.refs_3_, ...), custom_call_target="tpu_custom_call" | custom-call | flops 100000000 | bytes 7802880 | tf_op jit(solution)/shard_map/middle_kernel/pallas_call | solution.py:451
  129.3 4.9 %all-to-all-start.2 = ((f32[32,24,128]{2,1,0:T(8,128)}), f32[32,24,128]{2,1,0:T(8,128)S(1)}, u32[]{:S(2)}, u32[]{:S(2)}) async-start(f32[32,24,128]{2,1,0:T(8,128)} %get-tuple-element.78), calls=%async_computation.2 | async-start | bytes 786432 | tf_op jit(solution)/shard_map/all_to_all | solution.py:641
  134.2 0.0 copy-done.1
  134.2 0.0 copy-done.2
  134.3 0.1 copy.27.refs_7_
  134.3 4.9 %gate_back_kernel.1.refs_6_ = f32[2048,128]{1,0:T(8,128)} custom-call(f32[2048,128]{1,0:T(8,128)} %get-tuple-element.82.refs_0_, f32[32,64]{1,0:T(8,128)} %get-tuple-element.79.refs_1_, f32[2048,128]{1,0:T(8,128)} %get-tuple-element.60.refs_4_.refs_12_.refs_2_, f32[64,64]{1,0:T(8,128)} %refs_3_.1, f32[64,64]{1,0:T(8,128)} %refs_4_.3, ...), custom_call_target="tpu_custom_call" | custom-call | flops 100000000 | bytes 4251648 | tf_op jit(solution)/shard_map/gate_back_kernel/pallas_call | solution.py:451
  139.2 9.8 %all-to-all-done.2.refs_0_ = f32[32,24,128]{2,1,0:T(8,128)S(1)} async-done(((f32[32,24,128]{2,1,0:T(8,128)}), f32[32,24,128]{2,1,0:T(8,128)S(1)}, u32[]{:S(2)}, u32[]{:S(2)}) %all-to-all-start.2) | async-done | bytes 393248 | tf_op jit(solution)/shard_map/all_to_all | solution.py:641
  149.0 5.4 %finish_kernel.1 = f32[128,2048]{1,0:T(8,128)} custom-call(f32[32,24,128]{2,1,0:T(8,128)S(1)} %all-to-all-done.2.refs_0_, f32[32,64]{1,0:T(8,128)} %get-tuple-element.79.refs_1_, f32[256,128]{1,0:T(8,128)} %get-tuple-element.80.refs_2_, f32[256,128]{1,0:T(8,128)} %get-tuple-element.53.refs_1_.refs_3_, f32[256,128]{1,0:T(8,128)} %get-tuple-element.54.refs_2_.refs_4_, ...), custom_call_target="tpu_custom_call" | custom-call | flops 100000000 | bytes 4272128 | tf_op jit(solution)/shard_map/finish_kernel/pallas_call | solution.py:451
  (1 shorter events, 0.0 us)
Async XLA Ops:
  0.0 7.5 %collective-permute-start = (s32[32,128]{1,0:T(8,128)}, s32[32,128]{1,0:T(8,128)S(1)}, u32[]{:S(2)}, u32[]{:S(2)}) collective-permute-start(s32[32,128]{1,0:T(8,128)} %bitcast.20), channel_id=1, source_target_pairs={{0,1},{1,0},{2,3},{3,2},{4,5},{5,4},{6,7},{7,6},{8,9},{9,8},{10,11... | collective-permute-start | bytes 49160 | tf_op jit(solution)/shard_map/ppermute | solution.py:629
  0.0 7.5 %collective-permute-start.1 = (s32[32,128]{1,0:T(8,128)}, s32[32,128]{1,0:T(8,128)S(1)}, u32[]{:S(2)}, u32[]{:S(2)}) collective-permute-start(s32[32,128]{1,0:T(8,128)} %bitcast.21), channel_id=1, source_target_pairs={{2,0},{4,2},{6,4},{0,6},{3,1},{5,3},{7,5},{1,7},{10,8},{12,10},{14... | collective-permute-start | bytes 49160 | tf_op jit(solution)/shard_map/ppermute | solution.py:633
  2.8 5.5 %collective-permute-start.2 = (s32[32,128]{1,0:T(8,128)}, s32[32,128]{1,0:T(8,128)S(1)}, u32[]{:S(2)}, u32[]{:S(2)}) collective-permute-start(s32[32,128]{1,0:T(8,128)} %bitcast.22), channel_id=1, source_target_pairs={{4,0},{6,2},{0,4},{2,6},{5,1},{7,3},{1,5},{3,7},{12,8},{14,10},{8,... | collective-permute-start | bytes 49160 | tf_op jit(solution)/shard_map/ppermute | solution.py:633
  3.6 5.2 %collective-permute-start.3 = (s32[32,128]{1,0:T(8,128)}, s32[32,128]{1,0:T(8,128)S(1)}, u32[]{:S(2)}, u32[]{:S(2)}) collective-permute-start(s32[32,128]{1,0:T(8,128)} %bitcast.23), channel_id=1, source_target_pairs={{6,0},{0,2},{2,4},{4,6},{7,1},{1,3},{3,5},{5,7},{14,8},{8,10},{10,... | collective-permute-start | bytes 49160 | tf_op jit(solution)/shard_map/ppermute | solution.py:633
  10.7 27.0 %collective-permute-start.4 = (f32[32,256,128]{2,1,0:T(8,128)}, f32[32,256,128]{2,1,0:T(8,128)}, u32[]{:S(2)}, u32[]{:S(2)}) collective-permute-start(f32[32,256,128]{2,1,0:T(8,128)} %param.14), channel_id=1, source_target_pairs={{0,1},{1,0},{2,3},{3,2},{4,5},{5,4},{6,7},{7,6},{8,9},{9,8},{10,11... | collective-permute-start | bytes 12582920 | tf_op jit(solution)/shard_map/ppermute | solution.py:629
  10.8 26.9 %all-to-all-start = ((f32[32,24,128]{2,1,0:T(8,128)}), f32[32,24,128]{2,1,0:T(8,128)S(1)}, u32[]{:S(2)}, u32[]{:S(2)}) async-start(f32[32,24,128]{2,1,0:T(8,128)} %pair_kernel.1), calls=%async_computation | async-start | bytes 786432 | tf_op jit(solution)/shard_map/all_to_all | solution.py:641
  25.9 0.7 copy-start
  42.6 22.3 %all-to-all-start.1 = ((f32[32,32,128]{2,1,0:T(8,128)}), f32[32,32,128]{2,1,0:T(8,128)S(1)}, u32[]{:S(2)}, u32[]{:S(2)}) async-start(f32[32,32,128]{2,1,0:T(8,128)} %get-tuple-element.56), calls=%async_computation.1 | async-start | bytes 1048576 | tf_op jit(solution)/shard_map/all_to_all | solution.py:641
  70.2 3.3 %collective-permute-start.5 = (f32[1024,128]{1,0:T(8,128)}, f32[1024,128]{1,0:T(8,128)S(1)}, u32[]{:S(2)}, u32[]{:S(2)}) collective-permute-start(f32[1024,128]{1,0:T(8,128)} %get-tuple-element.63.left), channel_id=1, source_target_pairs={{0,1},{1,0},{2,3},{3,2},{4,5},{5,4},{6,7},{7,6},{8,9},{9,8},{10,11... | collective-permute-start | bytes 1572872 | tf_op jit(solution)/shard_map/ppermute | solution.py:629
  70.3 30.7 %collective-permute-start.6 = (f32[32,32,128]{2,1,0:T(8,128)}, f32[32,32,128]{2,1,0:T(8,128)S(1)}, u32[]{:S(2)}, u32[]{:S(2)}) collective-permute-start(f32[32,32,128]{2,1,0:T(8,128)} %get-tuple-element.66.right_0), channel_id=1, source_target_pairs={{2,0},{4,2},{6,4},{0,6},{3,1},{5,3},{7,5},{1,7},{10,8},{12,10},{14... | collective-permute-start | bytes 1572872 | tf_op jit(solution)/shard_map/ppermute | solution.py:633
  71.8 31.8 %collective-permute-start.7 = (f32[32,32,128]{2,1,0:T(8,128)}, f32[32,32,128]{2,1,0:T(8,128)S(1)}, u32[]{:S(2)}, u32[]{:S(2)}) collective-permute-start(f32[32,32,128]{2,1,0:T(8,128)} %get-tuple-element.66.right_0), channel_id=1, source_target_pairs={{4,0},{6,2},{0,4},{2,6},{5,1},{7,3},{1,5},{3,7},{12,8},{14,10},{8,... | collective-permute-start | bytes 1572872 | tf_op jit(solution)/shard_map/ppermute | solution.py:633
  73.3 30.3 %collective-permute-start.8 = (f32[32,32,128]{2,1,0:T(8,128)}, f32[32,32,128]{2,1,0:T(8,128)S(1)}, u32[]{:S(2)}, u32[]{:S(2)}) collective-permute-start(f32[32,32,128]{2,1,0:T(8,128)} %get-tuple-element.66.right_0), channel_id=1, source_target_pairs={{6,0},{0,2},{2,4},{4,6},{7,1},{1,3},{3,5},{5,7},{14,8},{8,10},{10,... | collective-permute-start | bytes 1572872 | tf_op jit(solution)/shard_map/ppermute | solution.py:633
  97.0 25.9 %collective-permute-start.11 = (f32[32,32,128]{2,1,0:T(8,128)}, f32[32,32,128]{2,1,0:T(8,128)S(1)}, u32[]{:S(2)}, u32[]{:S(2)}) collective-permute-start(f32[32,32,128]{2,1,0:T(8,128)} %get-tuple-element.71), channel_id=1, source_target_pairs={{0,4},{2,6},{4,0},{6,2},{1,5},{3,7},{5,1},{7,3},{8,12},{10,14},{12... | collective-permute-start | bytes 1572872 | tf_op jit(solution)/shard_map/ppermute | solution.py:637
  100.3 23.0 %collective-permute-start.12 = (f32[32,32,128]{2,1,0:T(8,128)}, f32[32,32,128]{2,1,0:T(8,128)S(1)}, u32[]{:S(2)}, u32[]{:S(2)}) collective-permute-start(f32[32,32,128]{2,1,0:T(8,128)} %get-tuple-element.72), channel_id=1, source_target_pairs={{0,2},{2,4},{4,6},{6,0},{1,3},{3,5},{5,7},{7,1},{8,10},{10,12},{12... | collective-permute-start | bytes 1572872 | tf_op jit(solution)/shard_map/ppermute | solution.py:637
  101.0 22.7 %collective-permute-start.13 = (f32[32,32,128]{2,1,0:T(8,128)}, f32[32,32,128]{2,1,0:T(8,128)S(1)}, u32[]{:S(2)}, u32[]{:S(2)}) collective-permute-start(f32[32,32,128]{2,1,0:T(8,128)} %get-tuple-element.73), channel_id=1, source_target_pairs={{0,6},{2,0},{4,2},{6,4},{1,7},{3,1},{5,3},{7,5},{8,14},{10,8},{12,... | collective-permute-start | bytes 1572872 | tf_op jit(solution)/shard_map/ppermute | solution.py:637
  103.6 30.6 %copy-start.1 = (f32[64,8]{0,1:T(8,128)S(1)}, f32[64,8]{0,1:T(8,128)}, u32[]{:S(2)}) copy-start(f32[64,8]{0,1:T(8,128)} %param.17) | copy-start | bytes 6148
  103.6 30.7 %copy-start.2 = (f32[64,8]{0,1:T(8,128)S(1)}, f32[64,8]{0,1:T(8,128)}, u32[]{:S(2)}) copy-start(f32[64,8]{0,1:T(8,128)} %param.18) | copy-start | bytes 6148
  120.8 1.7 %collective-permute-start.10 = (f32[512,128]{1,0:T(8,128)}, f32[512,128]{1,0:T(8,128)S(1)}, u32[]{:S(2)}, u32[]{:S(2)}) collective-permute-start(f32[512,128]{1,0:T(8,128)} %get-tuple-element.69), channel_id=1, source_target_pairs={{0,1},{1,0},{2,3},{3,2},{4,5},{5,4},{6,7},{7,6},{8,9},{9,8},{10,11... | collective-permute-start | bytes 786440 | tf_op jit(solution)/shard_map/ppermute | solution.py:629
  120.8 2.1 %collective-permute-start.9 = (f32[512,128]{1,0:T(8,128)}, f32[512,128]{1,0:T(8,128)S(1)}, u32[]{:S(2)}, u32[]{:S(2)}) collective-permute-start(f32[512,128]{1,0:T(8,128)} %get-tuple-element.68), channel_id=1, source_target_pairs={{0,1},{1,0},{2,3},{3,2},{4,5},{5,4},{6,7},{7,6},{8,9},{9,8},{10,11... | collective-permute-start | bytes 786440 | tf_op jit(solution)/shard_map/ppermute | solution.py:629
  129.3 19.7 %all-to-all-start.2 = ((f32[32,24,128]{2,1,0:T(8,128)}), f32[32,24,128]{2,1,0:T(8,128)S(1)}, u32[]{:S(2)}, u32[]{:S(2)}) async-start(f32[32,24,128]{2,1,0:T(8,128)} %get-tuple-element.78), calls=%async_computation.2 | async-start | bytes 786432 | tf_op jit(solution)/shard_map/all_to_all | solution.py:641

commit v7 on v6

--- a/solution.py
+++ b/solution.py
@@ -352,10 +352,11 @@
     send_all(send, slice(16, 16 + moments.shape[0]), moments[...])
 
 
-def gate_back_kernel(mid, attended, gate, mixing_back, filter_weight, x0t, inverse, base):
+def gate_back_kernel(mid, attended, gate, mixing_back, filter_weight, x0t, inverse, query_blocks, base, query_turned):
     parts = lhs_parts(filter_weight[...])
     mixing_parts = lhs_parts(mixing_back[...])
     heads_t = attended[...].T
+    query_turned[...] = query_blocks[...].T
     for first in range(0, RES, SIDE):
         group = range(first, first + SIDE)
         above = jnp.concatenate([mid[64 * i : 64 * i + 64] for i in group], axis=1)
@@ -372,7 +373,7 @@
 
 
 def finish_kernel(
-    got, attended, probs, keys, values, query_blocks, base, key_value, counts, asking, present, x0t, inverse, out, arrive
+    got, attended, probs, values, query_turned, base, key_value, counts, asking, present, x0t, inverse, out, arrive
 ):
     att_grad = unpack(jnp.sum(got[:, 0:16, :], axis=0))
     moments = got[:, 16:, :].reshape(RES * 8, 128)
@@ -389,7 +390,7 @@
 
     blocks = head_blocks(att_grad)
     score_grad = probs[...] * (near_nn(blocks, values[...]) - along)
-    key_grad = near_nn(query_blocks[...].T, score_grad)
+    key_grad = near_nn(query_turned[...], score_grad)
     value_grad = near_nn(blocks.T, probs[...])
     parts = lhs_parts(key_value[...])
     arrive()
@@ -710,13 +711,14 @@
         scratch=[pltpu.VMEM((RES * 32, SEQ), F32)],
     )
     got = exchange(send)
-    (base,) = call(
-        gate_back_kernel, [flat], mid, attended, gate, final_mixing_matrix, sigmoid_filter_matrix, x0t, inverse
+    base, query_turned = call(
+        gate_back_kernel, [flat, (RES * 8, RES * 8)],
+        mid, attended, gate, final_mixing_matrix, sigmoid_filter_matrix, x0t, inverse, query_blocks,
     )
     (out,) = call(
         finish_kernel, [(SEQ, RES * 64)],
-        got, attended, probs, keys, values, query_blocks, base, key_value, counts, asking_matrix,
-        present, x0t, inverse, late=(6, 11), free=(0, 7),
+        got, attended, probs, values, query_turned, base, key_value, counts, asking_matrix,
+        present, x0t, inverse, late=(5, 10), free=(0, 6),
     )
     return out
 

time: 156 us -> 156 us (level)
  no operation moved by 1% of the time
where the time goes in v7:
time: 156 us; the launch traced here: 155 us
  Pallas kernels  76.7 us (49%)
  starting transfers between devices  35.9 us (23%)
  waiting for transfers between devices  34.4 us (22%)
  local copies, waits for them, and re-layouts  6.28 us (4%)
    pallas_call x8, Pallas kernels, call(): pl.pallas_call(functools.partial(staged, kernel, (len(operands), len(shap...  35.9 us
    all_to_all x3, waiting for transfers between devices, exchange(): return lax.all_to_all(send, 'seq', 0, 0, tiled=True)  31 us
    pallas_call x1, Pallas kernels, right_products(): pl.pallas_call(right_kernel, grid_spec=grid_spec, out_shape=[pltpu.HBM((F...  23.6 us
    all_to_all x3, starting transfers between devices, exchange(): return lax.all_to_all(send, 'seq', 0, 0, tiled=True)  21 us
    pallas_call x1, Pallas kernels, left_products(): pl.pallas_call(left_kernel, grid=(steps,), in_specs=[rows, rows] + [whole...  17.2 us
    ppermute x6, starting transfers between devices, fetch_chip(): lax.ppermute(values, 'x', [((i + distance) % 4, i) for i in range(4)])  7.64 us
    ppermute x3, starting transfers between devices, send_chip(): lax.ppermute(values, 'x', [(i, (i + distance) % 4) for i in range(4)])  6.55 us
    unnamed x10, local copies, waits for them, and re-layouts  3.97 us
  transfers between devices with their start and end apart: 17, of which 9 were waited for; matrix products, arithmetic and copies ran while one was open for 4% of the time, Pallas kernels for 35%

profile of v7, /device:TPU:32, one launch (start us, length us, event | category | flops | bytes accessed | tf_op | source)
XLA Modules:
  0.0 154.5 jit_solution(11118811918265763406)
XLA Ops:
  0.0 0.0 collective-permute-start
  0.0 2.8 %collective-permute-start.1 = (s32[32,128]{1,0:T(8,128)}, s32[32,128]{1,0:T(8,128)S(1)}, u32[]{:S(2)}, u32[]{:S(2)}) collective-permute-start(s32[32,128]{1,0:T(8,128)} %bitcast.21), channel_id=1, source_target_pairs={{2,0},{4,2},{6,4},{0,6},{3,1},{5,3},{7,5},{1,7},{10,8},{12,10},{14... | collective-permute-start | bytes 49160 | tf_op jit(solution)/shard_map/ppermute | solution.py:634
  2.8 0.8 collective-permute-start.2
  3.6 0.9 collective-permute-start.3
  4.4 3.1 %norm_kernel.1 = (f32[2048,128]{1,0:T(8,128)}, f32[32,128]{1,0:T(8,128)}, f32[32,128]{1,0:T(8,128)}, f32[32,24,128]{2,1,0:T(8,128)}) custom-call(f32[128,2048]{1,0:T(8,128)} %refs_1_.1, s32[32,128]{1,0:T(8,128)} %bitcast.24), custom_call_target="tpu_custom_call" | custom-call | flops 100000000 | bytes 2539520 | tf_op jit(solution)/shard_map/norm_kernel/pallas_call | solution.py:452
  7.5 0.0 collective-permute-done.refs_2_
  7.5 0.0 collective-permute-done.1.refs_3_
  7.6 0.7 collective-permute-done.2.refs_4_
  8.2 0.5 collective-permute-done.3.refs_5_
  8.7 2.0 %pair_kernel.1 = f32[32,24,128]{2,1,0:T(8,128)} custom-call(f32[32,24,128]{2,1,0:T(8,128)} %get-tuple-element.48.refs_0_, s32[32,128]{1,0:T(8,128)} %bitcast.25, s32[32,128]{1,0:T(8,128)S(1)} %collective-permute-done.refs_2_, s32[32,128]{1,0:T(8,128)S(1)} %collective-permute-done.1.refs_3_, s32[32,128]{1,0:T(8,128)S(1)} %collective-permute-done.2.refs_4_, ...), custom_call_target="tpu_custom_call" | custom-call | flops 100000000 | bytes 868352 | tf_op jit(solution)/shard_map/pair_kernel/pallas_call | solution.py:452
  10.7 0.1 collective-permute-start.4
  10.8 11.4 %all-to-all-start = ((f32[32,24,128]{2,1,0:T(8,128)}), f32[32,24,128]{2,1,0:T(8,128)S(1)}, u32[]{:S(2)}, u32[]{:S(2)}) async-start(f32[32,24,128]{2,1,0:T(8,128)} %pair_kernel.1), calls=%async_computation | async-start | bytes 786432 | tf_op jit(solution)/shard_map/all_to_all | solution.py:642
  22.2 2.1 %copy.21 = f32[32,32,128]{2,0,1:T(8,128)} copy(f32[32,32,128]{2,1,0:T(8,128)} %bitcast.19) | data formatting | bytes 1048576 | tf_op jit(solution)/shard_map/reshape | solution.py:669
  24.3 0.8 copy.22
  25.2 0.1 pad_add_fusion.place
  25.2 0.7 maximum_bitcast_fusion.refs_4_
  25.9 0.0 copy-start
  25.9 0.7 copy-done
  26.6 4.7 %project_kernel.1 = (f32[256,128]{1,0:T(8,128)}, f32[256,128]{1,0:T(8,128)}, f32[2048,128]{1,0:T(8,128)}, f32[2048,128]{1,0:T(8,128)}, f32[2048,128]{1,0:T(8,128)}) custom-call(f32[2048,128]{1,0:T(8,128)} %get-tuple-element.54.refs_0_.refs_5_.refs_10_, f32[128,2048]{1,0:T(8,128)} %refs_1_.1, f32[128,2048]{1,0:T(8,128)} %refs_2_.1, f32[8,64]{1,0:T(8,128)S(1)} %bitcast.16, ...), custom_call_target="tpu_custom_call" | custom-call | flops 100000000 | bytes 6574080 | tf_op jit(solution)/shard_map/project_kernel/pallas_call | solution.py:452
  31.3 6.4 %all-to-all-done.refs_0_ = f32[32,24,128]{2,1,0:T(8,128)S(1)} async-done(((f32[32,24,128]{2,1,0:T(8,128)}), f32[32,24,128]{2,1,0:T(8,128)S(1)}, u32[]{:S(2)}, u32[]{:S(2)}) %all-to-all-start) | async-done | bytes 393248 | tf_op jit(solution)/shard_map/all_to_all | solution.py:642
  37.7 0.0 collective-permute-done.4
  37.7 4.8 %score_kernel.1 = (f32[256,128]{1,0:T(8,128)}, f32[32,16]{1,0:T(8,128)}, f32[32,128]{1,0:T(8,128)}, f32[256,256]{1,0:T(8,128)}, f32[32,32,128]{2,1,0:T(8,128)}) custom-call(f32[32,24,128]{2,1,0:T(8,128)S(1)} %all-to-all-done.refs_0_, f32[256,128]{1,0:T(8,128)} %get-tuple-element.55.refs_1_, f32[256,128]{1,0:T(8,128)} %get-tuple-element.56.refs_2_.refs_3_, ...), custom_call_target="tpu_custom_call" | custom-call | flops 100000000 | bytes 1624064 | tf_op jit(solution)/shard_map/score_kernel/pallas_call | solution.py:452
  42.6 4.8 %all-to-all-start.1 = ((f32[32,32,128]{2,1,0:T(8,128)}), f32[32,32,128]{2,1,0:T(8,128)S(1)}, u32[]{:S(2)}, u32[]{:S(2)}) async-start(f32[32,32,128]{2,1,0:T(8,128)} %get-tuple-element.58), calls=%async_computation.1 | async-start | bytes 1048576 | tf_op jit(solution)/shard_map/all_to_all | solution.py:642
  47.3 0.8 copy.24
  48.1 0.8 copy.25
  48.9 0.1 fusion
  49.0 0.1 copy.26.refs_7_
  49.1 0.8 copy.23
  49.9 14.9 %all-to-all-done.1.refs_0_ = f32[32,32,128]{2,1,0:T(8,128)S(1)} async-done(((f32[32,32,128]{2,1,0:T(8,128)}), f32[32,32,128]{2,1,0:T(8,128)S(1)}, u32[]{:S(2)}, u32[]{:S(2)}) %all-to-all-start.1) | async-done | bytes 524320 | tf_op jit(solution)/shard_map/all_to_all | solution.py:642
  64.9 5.3 %attend_kernel.1 = (f32[256,128]{1,0:T(8,128)}, f32[32,64]{1,0:T(8,128)}, f32[2048,128]{1,0:T(8,128)}, f32[32,128]{1,0:T(8,128)}, f32[1024,128]{1,0:T(8,128)}, /...) custom-call(f32[32,32,128]{2,1,0:T(8,128)S(1)} %all-to-all-done.1.refs_0_, ...), custom_call_target="tpu_custom_call" | custom-call | flops 100000000 | bytes 5093376 | tf_op jit(solution)/shard_map/attend_kernel/pallas_call | solution.py:452
  70.2 0.1 collective-permute-start.5
  70.3 1.5 collective-permute-start.6
  71.8 1.5 collective-permute-start.7
  73.3 0.2 collective-permute-start.8
  73.5 0.0 collective-permute-done.5.left_far
  73.5 23.6 %right_products.1 = (bf16[32,2048,128]{2,1,0:T(8,128)(2,1)}, bf16[32,2048,128]{2,1,0:T(8,128)(2,1)}, f32[32,32,128]{2,1,0:T(8,128)}, f32[32,32,128]{2,1,0:T(8,12...) custom-call(s32[2]{0:T(128)S(1)} %pad_add_fusion.place, f32[32,4,2,32,128]{4,3,2,1,0:T(8,128)} %bitcast.17, ...), custom_call_target="tpu_custom_call" | custom-call | flops 1000 | bytes 1000 | tf_op jit(solution)/shard_map/right_products/pallas_call | solution.py:550
  97.1 3.3 %collective-permute-start.11 = (f32[32,32,128]{2,1,0:T(8,128)}, f32[32,32,128]{2,1,0:T(8,128)S(1)}, u32[]{:S(2)}, u32[]{:S(2)}) collective-permute-start(f32[32,32,128]{2,1,0:T(8,128)} %get-tuple-element.73), channel_id=1, source_target_pairs={{0,4},{2,6},{4,0},{6,2},{1,5},{3,7},{5,1},{7,3},{8,12},{10,14},{12... | collective-permute-start | bytes 1572872 | tf_op jit(solution)/shard_map/ppermute | solution.py:638
  100.4 0.7 collective-permute-start.12
  101.0 0.0 collective-permute-done.6.right_1
  101.0 2.6 %collective-permute-start.13 = (f32[32,32,128]{2,1,0:T(8,128)}, f32[32,32,128]{2,1,0:T(8,128)S(1)}, u32[]{:S(2)}, u32[]{:S(2)}) collective-permute-start(f32[32,32,128]{2,1,0:T(8,128)} %get-tuple-element.75), channel_id=1, source_target_pairs={{0,6},{2,0},{4,2},{6,4},{1,7},{3,1},{5,3},{7,5},{8,14},{10,8},{12,... | collective-permute-start | bytes 1572872 | tf_op jit(solution)/shard_map/ppermute | solution.py:638
  103.6 0.0 collective-permute-done.7.right_2
  103.6 0.0 collective-permute-done.8.right_3
  103.6 0.0 copy-start.1
  103.6 0.0 copy-start.2
  103.6 17.2 %left_products.1 = (f32[1024,128]{1,0:T(8,128)}, f32[512,128]{1,0:T(8,128)}, f32[512,128]{1,0:T(8,128)}) custom-call(bf16[32,2048,128]{2,1,0:T(8,128)(2,1)} %get-tuple-element.66.high, bf16[32,2048,128]{2,1,0:T(8,128)(2,1)} %get-tuple-element.67.low, f32[32,32,128]{2,1,0:T(8,128)} %get-tuple-element.68.right_0, ...), custom_call_target="tpu_custom_call" | custom-call | flops 1000 | bytes 1000 | tf_op jit(solution)/shard_map/left_products/pallas_call | solution.py:611
  120.9 0.0 collective-permute-start.10
  120.9 0.5 collective-permute-start.9
  121.4 0.1 pad_maximum_fusion.refs_13_
  121.5 1.2 collective-permute-done.10.refs_2_
  122.6 0.4 collective-permute-done.9.refs_1_
  123.0 0.0 collective-permute-done.11.refs_4_
  123.0 0.4 collective-permute-done.12.refs_5_
  123.4 0.3 collective-permute-done.13.refs_6_
  123.7 5.7 %middle_kernel.1 = (f32[2048,128]{1,0:T(8,128)}, f32[32,24,128]{2,1,0:T(8,128)}) custom-call(f32[1024,128]{1,0:T(8,128)} %get-tuple-element.69.refs_0_, f32[512,128]{1,0:T(8,128)S(1)} %collective-permute-done.9.refs_1_, f32[512,128]{1,0:T(8,128)S(1)} %collective-permute-done.10.refs_2_, f32[32,32,128]{2,1,0:T(8,128)} %get-tuple-element.72.refs_3_, ...), custom_call_target="tpu_custom_call" | custom-call | flops 100000000 | bytes 7802880 | tf_op jit(solution)/shard_map/middle_kernel/pallas_call | solution.py:452
  129.4 4.9 %all-to-all-start.2 = ((f32[32,24,128]{2,1,0:T(8,128)}), f32[32,24,128]{2,1,0:T(8,128)S(1)}, u32[]{:S(2)}, u32[]{:S(2)}) async-start(f32[32,24,128]{2,1,0:T(8,128)} %get-tuple-element.80), calls=%async_computation.2 | async-start | bytes 786432 | tf_op jit(solution)/shard_map/all_to_all | solution.py:642
  134.3 0.0 copy-done.1
  134.3 0.0 copy-done.2
  134.3 0.1 copy.27.refs_6_
  134.4 5.0 %gate_back_kernel.1 = (f32[2048,128]{1,0:T(8,128)}, f32[256,256]{1,0:T(8,128)}) custom-call(f32[2048,128]{1,0:T(8,128)} %get-tuple-element.83.refs_0_, f32[32,64]{1,0:T(8,128)} %get-tuple-element.81.refs_1_, f32[2048,128]{1,0:T(8,128)} %get-tuple-element.62.refs_4_.refs_12_.refs_2_, f32[64,64]{1,0:T(8,128)} %refs_3_.1, f32[64,64]{1,0:T(8,128)} %refs_4_.3, ...), custom_call_target="tpu_custom_call" | custom-call | flops 100000000 | bytes 4775936 | tf_op jit(solution)/shard_map/gate_back_kernel/pallas_call | solution.py:452
  139.4 9.6 %all-to-all-done.2.refs_0_ = f32[32,24,128]{2,1,0:T(8,128)S(1)} async-done(((f32[32,24,128]{2,1,0:T(8,128)}), f32[32,24,128]{2,1,0:T(8,128)S(1)}, u32[]{:S(2)}, u32[]{:S(2)}) %all-to-all-start.2) | async-done | bytes 393248 | tf_op jit(solution)/shard_map/all_to_all | solution.py:642
  149.0 5.3 %finish_kernel.1 = f32[128,2048]{1,0:T(8,128)} custom-call(f32[32,24,128]{2,1,0:T(8,128)S(1)} %all-to-all-done.2.refs_0_, f32[32,64]{1,0:T(8,128)} %get-tuple-element.81.refs_1_, f32[256,128]{1,0:T(8,128)} %get-tuple-element.82.refs_2_, f32[256,128]{1,0:T(8,128)} %get-tuple-element.56.refs_2_.refs_3_, f32[256,256]{1,0:T(8,128)} %get-tuple-element.86.refs_4_, ...), custom_call_target="tpu_custom_call" | custom-call | flops 100000000 | bytes 4141056 | tf_op jit(solution)/shard_map/finish_kernel/pallas_call | solution.py:452
  (1 shorter events, 0.0 us)
Async XLA Ops:
  0.0 7.5 %collective-permute-start = (s32[32,128]{1,0:T(8,128)}, s32[32,128]{1,0:T(8,128)S(1)}, u32[]{:S(2)}, u32[]{:S(2)}) collective-permute-start(s32[32,128]{1,0:T(8,128)} %bitcast.20), channel_id=1, source_target_pairs={{0,1},{1,0},{2,3},{3,2},{4,5},{5,4},{6,7},{7,6},{8,9},{9,8},{10,11... | collective-permute-start | bytes 49160 | tf_op jit(solution)/shard_map/ppermute | solution.py:630
  0.0 7.5 %collective-permute-start.1 = (s32[32,128]{1,0:T(8,128)}, s32[32,128]{1,0:T(8,128)S(1)}, u32[]{:S(2)}, u32[]{:S(2)}) collective-permute-start(s32[32,128]{1,0:T(8,128)} %bitcast.21), channel_id=1, source_target_pairs={{2,0},{4,2},{6,4},{0,6},{3,1},{5,3},{7,5},{1,7},{10,8},{12,10},{14... | collective-permute-start | bytes 49160 | tf_op jit(solution)/shard_map/ppermute | solution.py:634
  2.8 5.5 %collective-permute-start.2 = (s32[32,128]{1,0:T(8,128)}, s32[32,128]{1,0:T(8,128)S(1)}, u32[]{:S(2)}, u32[]{:S(2)}) collective-permute-start(s32[32,128]{1,0:T(8,128)} %bitcast.22), channel_id=1, source_target_pairs={{4,0},{6,2},{0,4},{2,6},{5,1},{7,3},{1,5},{3,7},{12,8},{14,10},{8,... | collective-permute-start | bytes 49160 | tf_op jit(solution)/shard_map/ppermute | solution.py:634
  3.6 5.2 %collective-permute-start.3 = (s32[32,128]{1,0:T(8,128)}, s32[32,128]{1,0:T(8,128)S(1)}, u32[]{:S(2)}, u32[]{:S(2)}) collective-permute-start(s32[32,128]{1,0:T(8,128)} %bitcast.23), channel_id=1, source_target_pairs={{6,0},{0,2},{2,4},{4,6},{7,1},{1,3},{3,5},{5,7},{14,8},{8,10},{10,... | collective-permute-start | bytes 49160 | tf_op jit(solution)/shard_map/ppermute | solution.py:634
  10.7 27.0 %collective-permute-start.4 = (f32[32,256,128]{2,1,0:T(8,128)}, f32[32,256,128]{2,1,0:T(8,128)}, u32[]{:S(2)}, u32[]{:S(2)}) collective-permute-start(f32[32,256,128]{2,1,0:T(8,128)} %param.14), channel_id=1, source_target_pairs={{0,1},{1,0},{2,3},{3,2},{4,5},{5,4},{6,7},{7,6},{8,9},{9,8},{10,11... | collective-permute-start | bytes 12582920 | tf_op jit(solution)/shard_map/ppermute | solution.py:630
  10.8 26.9 %all-to-all-start = ((f32[32,24,128]{2,1,0:T(8,128)}), f32[32,24,128]{2,1,0:T(8,128)S(1)}, u32[]{:S(2)}, u32[]{:S(2)}) async-start(f32[32,24,128]{2,1,0:T(8,128)} %pair_kernel.1), calls=%async_computation | async-start | bytes 786432 | tf_op jit(solution)/shard_map/all_to_all | solution.py:642
  25.9 0.7 copy-start
  42.6 22.3 %all-to-all-start.1 = ((f32[32,32,128]{2,1,0:T(8,128)}), f32[32,32,128]{2,1,0:T(8,128)S(1)}, u32[]{:S(2)}, u32[]{:S(2)}) async-start(f32[32,32,128]{2,1,0:T(8,128)} %get-tuple-element.58), calls=%async_computation.1 | async-start | bytes 1048576 | tf_op jit(solution)/shard_map/all_to_all | solution.py:642
  70.2 3.3 %collective-permute-start.5 = (f32[1024,128]{1,0:T(8,128)}, f32[1024,128]{1,0:T(8,128)S(1)}, u32[]{:S(2)}, u32[]{:S(2)}) collective-permute-start(f32[1024,128]{1,0:T(8,128)} %get-tuple-element.65.left), channel_id=1, source_target_pairs={{0,1},{1,0},{2,3},{3,2},{4,5},{5,4},{6,7},{7,6},{8,9},{9,8},{10,11... | collective-permute-start | bytes 1572872 | tf_op jit(solution)/shard_map/ppermute | solution.py:630
  70.3 30.7 %collective-permute-start.6 = (f32[32,32,128]{2,1,0:T(8,128)}, f32[32,32,128]{2,1,0:T(8,128)S(1)}, u32[]{:S(2)}, u32[]{:S(2)}) collective-permute-start(f32[32,32,128]{2,1,0:T(8,128)} %get-tuple-element.68.right_0), channel_id=1, source_target_pairs={{2,0},{4,2},{6,4},{0,6},{3,1},{5,3},{7,5},{1,7},{10,8},{12,10},{14... | collective-permute-start | bytes 1572872 | tf_op jit(solution)/shard_map/ppermute | solution.py:634
  71.8 31.8 %collective-permute-start.7 = (f32[32,32,128]{2,1,0:T(8,128)}, f32[32,32,128]{2,1,0:T(8,128)S(1)}, u32[]{:S(2)}, u32[]{:S(2)}) collective-permute-start(f32[32,32,128]{2,1,0:T(8,128)} %get-tuple-element.68.right_0), channel_id=1, source_target_pairs={{4,0},{6,2},{0,4},{2,6},{5,1},{7,3},{1,5},{3,7},{12,8},{14,10},{8,... | collective-permute-start | bytes 1572872 | tf_op jit(solution)/shard_map/ppermute | solution.py:634
  73.3 30.3 %collective-permute-start.8 = (f32[32,32,128]{2,1,0:T(8,128)}, f32[32,32,128]{2,1,0:T(8,128)S(1)}, u32[]{:S(2)}, u32[]{:S(2)}) collective-permute-start(f32[32,32,128]{2,1,0:T(8,128)} %get-tuple-element.68.right_0), channel_id=1, source_target_pairs={{6,0},{0,2},{2,4},{4,6},{7,1},{1,3},{3,5},{5,7},{14,8},{8,10},{10,... | collective-permute-start | bytes 1572872 | tf_op jit(solution)/shard_map/ppermute | solution.py:634
  97.1 25.9 %collective-permute-start.11 = (f32[32,32,128]{2,1,0:T(8,128)}, f32[32,32,128]{2,1,0:T(8,128)S(1)}, u32[]{:S(2)}, u32[]{:S(2)}) collective-permute-start(f32[32,32,128]{2,1,0:T(8,128)} %get-tuple-element.73), channel_id=1, source_target_pairs={{0,4},{2,6},{4,0},{6,2},{1,5},{3,7},{5,1},{7,3},{8,12},{10,14},{12... | collective-permute-start | bytes 1572872 | tf_op jit(solution)/shard_map/ppermute | solution.py:638
  100.4 23.0 %collective-permute-start.12 = (f32[32,32,128]{2,1,0:T(8,128)}, f32[32,32,128]{2,1,0:T(8,128)S(1)}, u32[]{:S(2)}, u32[]{:S(2)}) collective-permute-start(f32[32,32,128]{2,1,0:T(8,128)} %get-tuple-element.74), channel_id=1, source_target_pairs={{0,2},{2,4},{4,6},{6,0},{1,3},{3,5},{5,7},{7,1},{8,10},{10,12},{12... | collective-permute-start | bytes 1572872 | tf_op jit(solution)/shard_map/ppermute | solution.py:638
  101.0 22.7 %collective-permute-start.13 = (f32[32,32,128]{2,1,0:T(8,128)}, f32[32,32,128]{2,1,0:T(8,128)S(1)}, u32[]{:S(2)}, u32[]{:S(2)}) collective-permute-start(f32[32,32,128]{2,1,0:T(8,128)} %get-tuple-element.75), channel_id=1, source_target_pairs={{0,6},{2,0},{4,2},{6,4},{1,7},{3,1},{5,3},{7,5},{8,14},{10,8},{12,... | collective-permute-start | bytes 1572872 | tf_op jit(solution)/shard_map/ppermute | solution.py:638
  103.6 30.6 %copy-start.1 = (f32[64,8]{0,1:T(8,128)S(1)}, f32[64,8]{0,1:T(8,128)}, u32[]{:S(2)}) copy-start(f32[64,8]{0,1:T(8,128)} %param.17) | copy-start | bytes 6148
  103.6 30.6 %copy-start.2 = (f32[64,8]{0,1:T(8,128)S(1)}, f32[64,8]{0,1:T(8,128)}, u32[]{:S(2)}) copy-start(f32[64,8]{0,1:T(8,128)} %param.18) | copy-start | bytes 6148
  120.9 1.7 %collective-permute-start.10 = (f32[512,128]{1,0:T(8,128)}, f32[512,128]{1,0:T(8,128)S(1)}, u32[]{:S(2)}, u32[]{:S(2)}) collective-permute-start(f32[512,128]{1,0:T(8,128)} %get-tuple-element.71), channel_id=1, source_target_pairs={{0,1},{1,0},{2,3},{3,2},{4,5},{5,4},{6,7},{7,6},{8,9},{9,8},{10,11... | collective-permute-start | bytes 786440 | tf_op jit(solution)/shard_map/ppermute | solution.py:630
  120.9 2.1 %collective-permute-start.9 = (f32[512,128]{1,0:T(8,128)}, f32[512,128]{1,0:T(8,128)S(1)}, u32[]{:S(2)}, u32[]{:S(2)}) collective-permute-start(f32[512,128]{1,0:T(8,128)} %get-tuple-element.70), channel_id=1, source_target_pairs={{0,1},{1,0},{2,3},{3,2},{4,5},{5,4},{6,7},{7,6},{8,9},{9,8},{10,11... | collective-permute-start | bytes 786440 | tf_op jit(solution)/shard_map/ppermute | solution.py:630
  129.4 19.6 %all-to-all-start.2 = ((f32[32,24,128]{2,1,0:T(8,128)}), f32[32,24,128]{2,1,0:T(8,128)S(1)}, u32[]{:S(2)}, u32[]{:S(2)}) async-start(f32[32,24,128]{2,1,0:T(8,128)} %get-tuple-element.80), calls=%async_computation.2 | async-start | bytes 786432 | tf_op jit(solution)/shard_map/all_to_all | solution.py:642
